TPU v7x, 256 devices: a whole 4x4x8 slice. The times are simulated.
256 devices in a mesh: rep: 4 (over z_lo), fsdp: 64 (over z_hi, x, y, core).
Axes of the slice: x: 4, y: 4, z: 8 (z_hi: 2, z_lo: 4; z = z_hi * 4 + z_lo), core: 2. Of those that a mesh axis runs over, the one named last changes fastest.
Arguments:
- activations: bfloat16 [1, 32768, 4096], P(None, ('rep', 'fsdp')), may hold values from -24 to 24
- unit_grads: bfloat16 [1, 32768, 11008], P(None, ('rep', 'fsdp')), may hold values from -0.0625 to 0.0625
- momentum: float32 [4, 1, 4096, 11008], P('rep', None, 'fsdp'), may hold values from -6 to 6
Outputs:
- update: float32 [1, 4096, 11008], P(None, 'fsdp')
- new_momentum: float32 [4, 1, 4096, 11008], P('rep', None, 'fsdp')
All inputs are finite; a program needn't handle non-finite values.
Results may differ from a plain program's by a relative error of at most 0.0003.
Values may be sent and summed in bfloat16 or wider, within the bound.
No kernel may reach another device: no remote copies, remote signals or barrier semaphores. Data moves between devices by JAX's collectives and lax.ppermute only.
A program may use at most 192 MiB of HBM per device.

v0:
```python
import jax
import jax.numpy as jnp
from jax import lax
from jax.sharding import PartitionSpec as P

SPAN = 64
BAND = 8
STRIPS = 4


decay_rate = 0.9


def band_table():
    freqs = jnp.arange(BAND, dtype=jnp.float32)[:, None]
    points = jnp.arange(SPAN, dtype=jnp.float32)[None, :]
    scales = jnp.where(freqs == 0.0, jnp.sqrt(1.0 / SPAN), jnp.sqrt(2.0 / SPAN))
    return scales * jnp.cos(jnp.pi * (2.0 * points + 1.0) * freqs / (2.0 * SPAN))


def on_device(activations, unit_grads, momentum):
    basis = band_table()
    layers, tok_rows, features = activations.shape
    width = unit_grads.shape[2]
    devices = lax.axis_size("fsdp")
    blocks_count = devices // STRIPS
    own_rows = features // devices
    strip_rows = own_rows // STRIPS
    block_width = width // blocks_count
    strip_cols = devices * strip_rows
    strips = activations.reshape(layers, tok_rows, devices, STRIPS, strip_rows)
    strips = strips.transpose(0, 1, 3, 2, 4).reshape(layers, tok_rows, STRIPS, strip_cols)
    unit_blocks = unit_grads.reshape(layers, tok_rows, blocks_count, block_width)
    feat_send = jnp.broadcast_to(
        strips[:, :, :, None, :], (layers, tok_rows, STRIPS, blocks_count, strip_cols)
    )
    unit_send = jnp.broadcast_to(
        unit_blocks[:, :, None, :, :], (layers, tok_rows, STRIPS, blocks_count, block_width)
    )
    feat_send = feat_send.reshape(layers, tok_rows, devices, strip_cols)
    unit_send = unit_send.reshape(layers, tok_rows, devices, block_width)
    feat_tile, unit_tile = (
        lax.all_to_all(feat_send, "fsdp", split_axis=2, concat_axis=1, tiled=True),
        lax.all_to_all(unit_send, "fsdp", split_axis=2, concat_axis=1, tiled=True),
    )
    partial_value = jnp.einsum(
        "ltd,ltr->ldr", feat_tile[:, :, 0], unit_tile[:, :, 0], preferred_element_type=jnp.float32
    )
    partial_value = partial_value.reshape(layers, devices, 1, strip_rows, block_width)
    arrived = lax.all_to_all(partial_value, "fsdp", split_axis=1, concat_axis=2, tiled=True)
    grads = arrived.reshape(layers, STRIPS, blocks_count, strip_rows, block_width).transpose(
        0, 1, 3, 2, 4
    )
    grads = grads.reshape(layers, own_rows, width)
    mixed = decay_rate * momentum[0] + grads
    blocks = mixed.reshape(layers, own_rows // SPAN, SPAN, width // SPAN, SPAN)
    band = jnp.einsum("kb,labcd,jd->lakcj", basis, blocks, basis, precision=lax.Precision.HIGHEST)
    local_back = jnp.einsum(
        "kb,lakcj,jd->labcd", basis, band, basis, precision=lax.Precision.HIGHEST
    )
    new_momentum = (blocks - local_back).reshape(1, layers, own_rows, width)
    total = lax.psum(band, "rep")
    decoded = jnp.einsum("kb,lakcj,jd->labcd", basis, total, basis, precision=lax.Precision.HIGHEST)
    update = decoded.reshape(layers, own_rows, width) / lax.axis_size("rep")
    return (update, new_momentum)


def solution(mesh):
    return jax.shard_map(
        on_device,
        mesh=mesh,
        in_specs=(
            P(None, ("rep", "fsdp"), None),
            P(None, ("rep", "fsdp"), None),
            P("rep", None, "fsdp", None),
        ),
        out_specs=(P(None, "fsdp", None), P("rep", None, "fsdp", None)),
        check_vma=False,
    )
```

profile of v0, /device:TPU:32, one launch (start us, length us, event | category | flops | bytes accessed | tf_op | source)
XLA Modules:
  0.0 940.6 jit_solution(2431863090640441314)
XLA Ops:
  0.6 3.9 copy.36
  4.5 5.7 broadcast_in_dim.32
  10.2 0.0 copy-start
  10.2 14.0 %all-to-all-start.1 = ((bf16[1,128,64,688]{1,3,0,2:T(8,128)(2,1)}), bf16[1,128,64,688]{1,3,0,2:T(8,128)(2,1)}, u32[]{:S(2)}, u32[]{:S(2)}) async-start(bf16[1,128,64,688]{1,3,0,2:T(8,128)(2,1)} %bitcast.70), calls=%async_computation.1 | async-start | bytes 22544384 | tf_op jit(solution)/shard_map/all_to_all | solution.py:44
  24.3 0.0 copy-done
  24.3 0.7 copy.32
  24.9 0.2 copy.33
  25.1 247.7 %all-to-all-done.1 = bf16[1,128,64,688]{1,3,0,2:T(8,128)(2,1)} async-done(((bf16[1,128,64,688]{1,3,0,2:T(8,128)(2,1)}), bf16[1,128,64,688]{1,3,0,2:T(8,128)(2,1)}, u32[]{:S(2)}, u32[]{:S(2)}) %all-to-all-start.1) | async-done | bytes 11272224 | tf_op jit(solution)/shard_map/all_to_all | solution.py:44
  272.9 6.2 broadcast_in_dim.29
  279.0 10.3 %all-to-all-start = ((bf16[1,128,64,1024]{1,3,0,2:T(8,128)(2,1)}), bf16[1,128,64,1024]{1,3,0,2:T(8,128)(2,1)}, u32[]{:S(2)}, u32[]{:S(2)}) async-start(bf16[1,128,64,1024]{1,3,0,2:T(8,128)(2,1)} %bitcast.68), calls=%async_computation | async-start | bytes 33554432 | tf_op jit(solution)/shard_map/all_to_all | solution.py:43
  289.3 17.6 %copy.37 = bf16[1,64,128,1,688]{2,1,4,3,0:T(8,128)(2,1)} copy(bf16[1,64,128,1,688]{2,4,1,3,0:T(8,128)(2,1)} %bitcast.12) | data formatting | bytes 22544384 | tf_op jit(solution)/shard_map/all_to_all | solution.py:44
  306.9 17.6 %reshape.150 = bf16[8192,688,1]{0,1,2:T(8,128)(2,1)} reshape(bf16[1,64,128,1,688]{2,1,4,3,0:T(8,128)(2,1)} %copy.37) | data formatting | bytes 22544384 | tf_op jit(solution)/shard_map/reshape.5
  324.6 253.6 %all-to-all-done = bf16[1,128,64,1024]{1,3,0,2:T(8,128)(2,1)} async-done(((bf16[1,128,64,1024]{1,3,0,2:T(8,128)(2,1)}), bf16[1,128,64,1024]{1,3,0,2:T(8,128)(2,1)}, u32[]{:S(2)}, u32[]{:S(2)}) %all-to-all-start) | async-done | bytes 16777248 | tf_op jit(solution)/shard_map/all_to_all | solution.py:43
  578.2 22.4 %copy.34 = bf16[1,128,64,1024]{3,1,2,0:T(8,128)(2,1)} copy(bf16[1,128,64,1024]{1,3,0,2:T(8,128)(2,1)} %all-to-all-done) | data formatting | bytes 33554432 | tf_op jit(solution)/shard_map/all_to_all | solution.py:43
  600.6 21.3 %copy.35 = bf16[1024,8192]{1,0:T(8,128)(2,1)} copy(bf16[1024,8192]{0,1:T(8,128)(2,1)} %bitcast.69) | data formatting | bytes 33554432 | tf_op jit(solution)/shard_map/ltd,ltr->ldr/dot_general | solution.py:46
  621.9 19.5 %convolution_bitcast_fusion = f32[1,64,1,16,688]{4,3,2,0,1:T(8,128)} fusion(bf16[64,16,8192]{2,1,0:T(8,128)(2,1)} %bitcast.73, bf16[8192,688,1]{0,1,2:T(8,128)(2,1)} %reshape.150), kind=kOutput, calls=%fused_computation.3 | convolution fusion | flops 11542724608 | bytes 30867456 | tf_op jit(solution)/shard_map/ltd,ltr->ldr/dot_general | solution.py:46
  641.4 90.1 %all-to-all-start.2 = ((f32[1,64,1,16,688]{4,3,2,0,1:T(8,128)}), f32[1,64,1,16,688]{4,3,2,0,1:T(8,128)}, u32[]{:S(2)}, u32[]{:S(2)}) async-start(f32[1,64,1,16,688]{4,3,2,0,1:T(8,128)} %convolution_bitcast_fusion), calls=%async_computation.2 | async-start | bytes 6291456 | tf_op jit(solution)/shard_map/all_to_all | solution.py:50
  731.6 2.0 broadcast_multiply_fusion
  733.6 3.6 mul.137
  737.2 3.7 mul.147
  740.9 6.2 copy.45
  747.1 26.3 %all-to-all-done.2 = f32[1,64,1,16,688]{4,3,2,0,1:T(8,128)} async-done(((f32[1,64,1,16,688]{4,3,2,0,1:T(8,128)}), f32[1,64,1,16,688]{4,3,2,0,1:T(8,128)}, u32[]{:S(2)}, u32[]{:S(2)}) %all-to-all-start.2) | async-done | bytes 2818080 | tf_op jit(solution)/shard_map/all_to_all | solution.py:50
  773.5 3.7 copy.61
  777.2 5.4 reshape.145
  782.6 5.4 reshape.147
  788.0 7.5 add.38
  795.5 6.6 copy.40
  802.1 4.0 fusion.12
  806.1 0.5 convolution_bitcast_fusion.1
  806.6 0.7 fusion.3
  807.3 90.5 %psum.7 = f32[8,172,8]{1,2,0:T(8,128)S(1)} all-reduce(f32[8,172,8]{1,2,0:T(8,128)S(1)} %convolution_bitcast_fusion.1), channel_id=1, replica_groups=mesh['rep'=4,'fsdp'=64] {'rep'}, use_global_device_ids=true, to_apply=%region_0.1 | all-reduce | flops 11008 | bytes 88064 | tf_op jit(solution)/shard_map/psum | solution.py:62
  897.9 6.2 copy.46
  904.1 7.7 bitcast_subtract_fusion
  911.8 6.0 copy.49
  917.8 5.4 reshape.149
  923.3 0.7 fusion.5
  924.0 5.2 multiply_bitcast_fusion
  929.2 6.0 copy.44
  935.2 5.4 div.34
  (2 shorter events, 0.0 us)
Async XLA Ops:
  10.2 14.0 %copy-start = (bf16[1,128,4096]{2,1,0:T(8,128)(2,1)S(1)}, bf16[1,128,4096]{2,1,0:T(8,128)(2,1)}, u32[]{:S(2)}) copy-start(bf16[1,128,4096]{2,1,0:T(8,128)(2,1)} %param.3) | copy-start | bytes 3145732
  10.2 262.6 %all-to-all-start.1 = ((bf16[1,128,64,688]{1,3,0,2:T(8,128)(2,1)}), bf16[1,128,64,688]{1,3,0,2:T(8,128)(2,1)}, u32[]{:S(2)}, u32[]{:S(2)}) async-start(bf16[1,128,64,688]{1,3,0,2:T(8,128)(2,1)} %bitcast.70), calls=%async_computation.1 | async-start | bytes 22544384 | tf_op jit(solution)/shard_map/all_to_all | solution.py:44
  279.0 299.2 %all-to-all-start = ((bf16[1,128,64,1024]{1,3,0,2:T(8,128)(2,1)}), bf16[1,128,64,1024]{1,3,0,2:T(8,128)(2,1)}, u32[]{:S(2)}, u32[]{:S(2)}) async-start(bf16[1,128,64,1024]{1,3,0,2:T(8,128)(2,1)} %bitcast.68), calls=%async_computation | async-start | bytes 33554432 | tf_op jit(solution)/shard_map/all_to_all | solution.py:43
  641.4 132.0 %all-to-all-start.2 = ((f32[1,64,1,16,688]{4,3,2,0,1:T(8,128)}), f32[1,64,1,16,688]{4,3,2,0,1:T(8,128)}, u32[]{:S(2)}, u32[]{:S(2)}) async-start(f32[1,64,1,16,688]{4,3,2,0,1:T(8,128)} %convolution_bitcast_fusion), calls=%async_computation.2 | async-start | bytes 6291456 | tf_op jit(solution)/shard_map/all_to_all | solution.py:50
where the time goes:
time: 945 us; the launch traced here: 941 us
  waiting for transfers between devices  528 us (56%)
  local copies, waits for them, and re-layouts  159 us (17%)
  starting transfers between devices  114 us (12%)
  blocking collectives  90.5 us (10%)
  matrix products  38.3 us (4%)
  other arithmetic  9.54 us (1%)
    all_to_all x1, waiting for transfers between devices, on_device(): lax.all_to_all(feat_send, 'fsdp', split_axis=2, concat_axis=1, tiled=True)  254 us
    all_to_all x1, waiting for transfers between devices, on_device(): lax.all_to_all(unit_send, 'fsdp', split_axis=2, concat_axis=1, tiled=True)  248 us
    psum x1, blocking collectives, on_device(): total = lax.psum(band, 'rep')  90.5 us
    all_to_all x1, starting transfers between devices, on_device(): lax.all_to_all(partial_value, 'fsdp', split_axis=1, concat_axis=2, tiled=...  90.1 us
    all_to_all x1, waiting for transfers between devices, on_device(): lax.all_to_all(partial_value, 'fsdp', split_axis=1, concat_axis=2, tiled=...  26.3 us
    all_to_all x1, local copies, waits for them, and re-layouts, on_device(): lax.all_to_all(feat_send, 'fsdp', split_axis=2, concat_axis=1, tiled=True)  22.4 us
    dot_general x1, local copies, waits for them, and re-layouts, on_device(): jnp.einsum('ltd,ltr->ldr', feat_tile[:, :, 0], unit_tile[:, :, 0], prefer...  21.3 us
    dot_general x1, matrix products, on_device(): jnp.einsum('ltd,ltr->ldr', feat_tile[:, :, 0], unit_tile[:, :, 0], prefer...  19.5 us
  transfers between devices with their start and end apart: 3, of which 3 were waited for; matrix products, arithmetic and copies ran while one was open for 5% of the time, Pallas kernels for 0%

commit v1 on v0

v1 whole, which is shorter than its diff:
```python
import functools

import jax
import jax.numpy as jnp
import numpy as np
from jax import lax
from jax.experimental import pallas as pl
from jax.experimental.pallas import tpu as pltpu
from jax.sharding import Mesh
from jax.sharding import PartitionSpec as P

SPAN = 64
BAND = 8
LANES = 128
GROUP = 1024
DECAY = 0.9
CHUNK_TILES = (4, 4, 3)
PARAMS = pltpu.CompilerParams(vmem_limit_bytes=56 << 20)
ANY = pl.BlockSpec(memory_space=pl.ANY)
QUICK = pl.CostEstimate(flops=1, bytes_accessed=1, transcendentals=0)
SMEM = pl.BlockSpec(memory_space=pltpu.SMEM)
VMEM = pl.BlockSpec(memory_space=pltpu.VMEM)


def band_table():
    freqs = np.arange(BAND, dtype=np.float64)[:, None]
    points = np.arange(SPAN, dtype=np.float64)[None, :]
    scales = np.where(freqs == 0.0, np.sqrt(1.0 / SPAN), np.sqrt(2.0 / SPAN))
    return (scales * np.cos(np.pi * (2.0 * points + 1.0) * freqs / (2.0 * SPAN))).astype(np.float32)


def shift(n, by):
    return [(i, (i + by) % n) for i in range(n)]


def halved(value):
    high = value.astype(jnp.bfloat16)
    return high, (value - high.astype(jnp.float32)).astype(jnp.bfloat16)


def dot(a, b):
    (ah, al), (bh, bl) = halved(a), halved(b)
    return jnp.dot(
        jnp.concatenate([ah, ah, al], axis=1),
        jnp.concatenate([bh, bl, bh], axis=0),
        preferred_element_type=jnp.float32,
    )


def groups_of(width):
    return [(start, min(GROUP, width - start)) for start in range(0, width, GROUP)]


def starts_of(width, block):
    return [min(j * block, width - block) for j in range(8)]


def finish_kernel(widths, basis_ref, back_ref, wide_ref, tall_ref, mom_ref, *refs):
    n = len(widths)
    pieces, (new_ref, band_ref, rows_ref) = refs[:n], refs[n:]
    width = mom_ref.shape[1]
    for j, start in enumerate(starts_of(width, sum(widths))):
        for k, w in enumerate(widths):
            at = pl.ds(start + sum(widths[:k]), w)
            new_ref[:, at] = DECAY * mom_ref[:, at] + pieces[k][j]
    rows_ref[...] = jnp.zeros_like(rows_ref)
    for i, (start, w) in enumerate(groups_of(width)):
        rows_ref[i * BAND : (i + 1) * BAND, :w] = dot(basis_ref[...], new_ref[:, start : start + w])
    band = dot(rows_ref[...], wide_ref[...])
    band_ref[...] = band
    rows_ref[...] = dot(band, tall_ref[...])
    for i, (start, w) in enumerate(groups_of(width)):
        new_ref[:, start : start + w] -= dot(back_ref[...], rows_ref[i * BAND : (i + 1) * BAND, :w])


def update_kernel(back_ref, tall_ref, b0, b1, b2, b3, out_ref):
    total = ((b0[...] + b1[...]) + (b2[...] + b3[...])) * 0.25
    rows = dot(total, tall_ref[...])
    for i, (start, w) in enumerate(groups_of(out_ref.shape[1])):
        out_ref[:, start : start + w] = dot(back_ref[...], rows[i * BAND : (i + 1) * BAND, :w])


def call(kernel, out, *args, spec=None):
    shapes = [jax.ShapeDtypeStruct(s, t) for s, t in out]
    return pl.pallas_call(
        kernel,
        out_shape=shapes,
        in_specs=spec or [VMEM] * len(args),
        out_specs=[VMEM] * len(out),
        compiler_params=PARAMS,
        cost_estimate=QUICK,
    )(*args)


def strips_kernel(half, at_ref, acts_ref, *outs):
    for e, out in enumerate(outs):
        for i in range(2):
            at = pl.ds(pl.multiple_of(at_ref[2 * e + i], LANES), half)
            out[i * half : (i + 1) * half] = acts_ref[:, at].T


def blocks_kernel(starts, leads, units_ref, *outs):
    for lead, out in zip(leads, outs):
        for j, start in enumerate(starts):
            out[j] = units_ref[:, start + lead : start + lead + out.shape[2]]


def blocks(units, starts, leads, widths):
    outs = [((8, units.shape[0], w), units.dtype) for w in widths]
    return call(functools.partial(blocks_kernel, starts, leads), outs, units)


def product(left, rights):
    total = None
    for i, some in enumerate(((0,), (1,), (2,), (3, 4))):
        count = 8 // len(some)
        for m, n in enumerate(some):
            part = jnp.concatenate([left[count * m + j, i] for j in range(count)], axis=1)
            term = jnp.dot(part, rights[n][...], preferred_element_type=jnp.float32)
            total = term if total is None else total + term
    return total


def keep_kernel(left_ref, *refs):
    refs[5][...] = product(left_ref, refs[:5])


def send_kernel(left_ref, *refs):
    rights, out, top_ref = refs[:5], refs[5], refs[6]
    i, rows = pl.program_id(0), left_ref.shape[2]
    value = product(left_ref, rights)
    top = jnp.max(jnp.max(jnp.abs(value), axis=0, keepdims=True), axis=1, keepdims=True)

    @pl.when(i == 0)
    def _():
        top_ref[...] = jnp.zeros_like(top_ref)

    top_ref[...] = jnp.maximum(top_ref[...], top)
    out[pl.ds(pl.multiple_of(i * rows, rows), rows)] = value

    @pl.when(i == pl.num_programs(0) - 1)
    def _():
        half, w = out.shape[0] - 16, out.shape[1]
        power = jnp.floor(15.0 - jnp.log2(jnp.maximum(top_ref[:1, :1], 2.0**-100)))
        out[:half] = out[:half] * jnp.exp2(power)
        out[half:] = jnp.broadcast_to(power, (16, w))


def tile(kernel, lefts, rights, extra):
    n, dx, half, tok = lefts.shape
    w = rights[0].shape[1]
    rows = 256
    if extra:
        out_spec = pl.BlockSpec((half + extra, w), lambda i: (0, 0))
        scratch = [pltpu.VMEM((8, LANES), jnp.float32)]
    else:
        out_spec = pl.BlockSpec((rows, w), lambda i: (i, 0))
        scratch = []
    in_specs = [pl.BlockSpec((n, dx, rows, tok), lambda i: (0, 0, i, 0))]
    depth = rights[0].shape[0]
    for n, b in enumerate(rights):
        size = depth if n < 3 else depth // 2
        place = 0 if n < 3 else b.shape[0] // size - 1
        in_specs.append(pl.BlockSpec((size, w), lambda i, place=place: (place, 0)))
    return pl.pallas_call(
        kernel,
        grid=(half // rows,),
        out_shape=jax.ShapeDtypeStruct((half + extra, w), jnp.float32),
        in_specs=in_specs,
        out_specs=out_spec,
        scratch_shapes=scratch,
        compiler_params=PARAMS,
        cost_estimate=QUICK,
    )(lefts, *rights)


def on_device(activations, unit_grads, momentum):
    acts, units, mom = activations[0], unit_grads[0], momentum[0, 0]
    tok, features = acts.shape
    width = units.shape[1]
    zh, x = lax.axis_index("zh"), lax.axis_index("x")
    plane_rows = features // 2
    half = plane_rows // 4
    own_rows = half // 8
    block = -(-width // (8 * LANES)) * LANES
    widths = [LANES * t for t in CHUNK_TILES]
    f32, b16 = jnp.float32, acts.dtype

    def along(axis, by, value):
        return lax.ppermute(value, axis, shift(2 if axis in ("core", "zh") else 4, by))

    def sync(*values):
        return lax.optimization_barrier(values)

    def swap(value):
        return lax.all_to_all(value, ("y", "core"), 0, 0, tiled=True)

    def column_block(cut):
        return swap(cut).reshape(8 * tok, cut.shape[2])

    def ring(v):
        return along("x", 1, v), along("x", 3, v)

    def halves(r, l):
        depth = 4 * tok
        return r[:depth], l[depth : 2 * depth]

    def payload(sent, five):
        return tile(send_kernel, sent, five, 16).astype(jnp.float16)

    def joined(keep, got):
        other = got[:half].astype(f32) * jnp.exp2(-got[half : half + 1].astype(f32))
        return (keep + other).reshape(8, own_rows, keep.shape[1])

    strips_at = jnp.stack(
        [plane_rows * p + half * ((x + e) % 4) for e in range(4) for p in (zh, 1 - zh)]
    ).astype(jnp.int32)

    starts = starts_of(width, block)
    leads = [sum(widths[:k]) for k in range(len(widths))]

    (cut0,) = blocks(units, starts, leads[:1], widths[:1])
    v0 = column_block(cut0)
    s0, s1, s2, s3 = call(
        functools.partial(strips_kernel, half), [((2 * half, tok), b16)] * 4, strips_at, acts, spec=[SMEM, VMEM]
    )
    local = [s0, along("x", 1, s1), along("x", 3, s3), along("x", 2, s2)]
    kept = jnp.stack([a[:half] for a in local])
    sent = jnp.stack([a[half:] for a in local])

    v0, sent, units = sync(v0, sent, units)
    r0, l0 = ring(v0)
    cut1, cut2 = blocks(units, starts, leads[1:], widths[1:])
    v1 = column_block(cut1)

    v1, r0, l0, sent, kept, cut2 = sync(v1, r0, l0, sent, kept, cut2)
    far_r, far_l = halves(r0, l0)
    right, left = jnp.concatenate([v1, far_r]), jnp.concatenate([v1, far_l])
    right, left, sent, kept, cut2 = sync(right, left, sent, kept, cut2)
    r1, l1 = along("x", 1, right), along("x", 3, left)
    v2 = column_block(cut2)
    sent = lax.all_gather(sent, ("y", "core"))

    r1, l1, v2, sent, kept = sync(r1, l1, v2, sent, kept)
    half1 = halves(r1, l1)
    half1, r1, l1, v2, sent, kept = sync(half1, r1, l1, v2, sent, kept)
    far1 = along("x", 1, half1[0]), along("x", 3, half1[1])
    send0 = payload(sent, [v0, r0, l0, r1, l1])
    kept = lax.all_gather(kept, ("y", "core"))

    far1, send0, v2, sent = sync(far1, send0, v2, sent)
    r2, l2 = ring(v2)
    got0 = along("zh", 1, send0)
    send1 = payload(sent, [v1, r1, l1, *far1])

    r2, l2, got0, send1, kept = sync(r2, l2, got0, send1, kept)
    half2 = halves(r2, l2)
    half2, got0, send1, kept = sync(half2, got0, send1, kept)
    far2 = along("x", 1, half2[0]), along("x", 3, half2[1])
    got1 = along("zh", 1, send1)
    send2 = payload(sent, [v2, r2, l2, *far2])
    total0 = joined(tile(keep_kernel, kept, [v0, r0, l0, r1, l1], 0), got0)

    got1, send2, total0, kept = sync(got1, send2, total0, kept)
    got2 = along("zh", 1, send2)
    done0 = swap(total0)
    total1 = joined(tile(keep_kernel, kept, [v1, r1, l1, *far1], 0), got1)
    keep2 = tile(keep_kernel, kept, [v2, r2, l2, *far2], 0)

    got2, done0, total1, keep2 = sync(got2, done0, total1, keep2)
    done = [done0, swap(total1), swap(joined(keep2, got2))]

    basis = band_table()
    wide = np.kron(np.eye(GROUP // SPAN, dtype=np.float32), basis.T)
    rows = len(groups_of(width)) * BAND
    with jax.named_scope("finish"):
        new, band = pl.pallas_call(
            functools.partial(finish_kernel, widths),
            out_shape=(
                jax.ShapeDtypeStruct(mom.shape, f32),
                jax.ShapeDtypeStruct((rows, LANES), f32),
            ),
            in_specs=[VMEM] * (5 + len(widths)),
            out_specs=(VMEM, VMEM),
            scratch_shapes=[pltpu.VMEM((rows, GROUP), f32)],
            compiler_params=PARAMS,
        )(basis, basis.T, wide, wide.T, mom, *done)
    with jax.named_scope("band"):
        others = [along("rep", s, band) for s in (1, 2, 3)]
    with jax.named_scope("update"):
        (update,) = call(update_kernel, [(mom.shape, f32)], jnp.asarray(basis.T), jnp.asarray(wide.T), band, *others)
    return update[None], new[None, None]


def solution(mesh):
    fine = Mesh(mesh.devices.reshape(4, 2, 4, 4, 2), ("rep", "zh", "x", "y", "core"))
    every = ("rep", "zh", "x", "y", "core")
    return jax.shard_map(
        on_device,
        mesh=fine,
        in_specs=(
            P(None, every, None),
            P(None, every, None),
            P("rep", None, every[1:], None),
        ),
        out_specs=(P(None, every[1:], None), P("rep", None, every[1:], None)),
        check_vma=False,
    )
```

time: 945 us -> 275 us (0.29)
  waiting for transfers between devices: 528 us -> 69.8 us
  local copies, waits for them, and re-layouts: 159 us -> 7.65 us
  starting transfers between devices: 114 us -> 54.3 us
  Pallas kernels: 0 us -> 55.7 us
  matrix products: 38.3 us -> 0 us
  blocking collectives: 90.5 us -> 58.4 us
  between operations: 0.74 us -> 14.3 us
    all_to_all x3, waiting for transfers between devices: 528 us -> 17.7 us  [swap(): return lax.all_to_all(value, ('y', 'core'), 0, 0, tiled=True)]
    all_to_all x3, starting transfers between devices: 114 us -> 11.6 us  [swap(): return lax.all_to_all(value, ('y', 'core'), 0, 0, tiled=True)]
    psum x1 -> x0, blocking collectives: 90.5 us -> none  [on_device(): total = lax.psum(band, 'rep')]
    all_to_all x0 -> x3, blocking collectives: none -> 58.4 us  [swap(): return lax.all_to_all(value, ('y', 'core'), 0, 0, tiled=True)]
    pallas_call x0 -> x11, Pallas kernels: none -> 55.7 us  [the longest x6 37.7 us: tile(): pl.pallas_call(kernel, grid=(half // rows,), out_shape=jax.ShapeDtypeStru...]
    ppermute x0 -> x19, waiting for transfers between devices: none -> 50.7 us  [along(): lax.ppermute(value, axis, shift(2 if axis in ('core', 'zh') else 4, by))]
    ppermute x0 -> x19, starting transfers between devices: none -> 42.6 us  [along(): lax.ppermute(value, axis, shift(2 if axis in ('core', 'zh') else 4, by))]
    all_to_all x2 -> x0, local copies, waits for them, and re-layouts: 40 us -> none  [the longest x1 22.4 us: on_device(): lax.all_to_all(feat_send, 'fsdp', split_axis=2, concat_axis=1, tiled=True)]
  transfers between devices with their start and end apart: 3 -> 24, of which waited for: 3 -> 13; matrix products, arithmetic and copies ran while one was open for 5% -> 4% of each run, Pallas kernels for 0% -> 16%
where the time goes in v1:
time: 275 us; the launch traced here: 274 us
  waiting for transfers between devices  69.8 us (25%)
  blocking collectives  58.4 us (21%)
  Pallas kernels  55.7 us (20%)
  starting transfers between devices  54.3 us (20%)
  other arithmetic  14.3 us (5%)
  between operations  14.3 us (5%)
  local copies, waits for them, and re-layouts  7.65 us (3%)
    all_to_all x3, blocking collectives, swap(): return lax.all_to_all(value, ('y', 'core'), 0, 0, tiled=True)  58.4 us
    ppermute x19, waiting for transfers between devices, along(): lax.ppermute(value, axis, shift(2 if axis in ('core', 'zh') else 4, by))  50.7 us
    ppermute x19, starting transfers between devices, along(): lax.ppermute(value, axis, shift(2 if axis in ('core', 'zh') else 4, by))  42.6 us
    pallas_call x6, Pallas kernels, tile(): pl.pallas_call(kernel, grid=(half // rows,), out_shape=jax.ShapeDtypeStru...  37.7 us
    all_to_all x3, waiting for transfers between devices, swap(): return lax.all_to_all(value, ('y', 'core'), 0, 0, tiled=True)  17.7 us
    pallas_call x4, Pallas kernels, call(): pl.pallas_call(kernel, out_shape=shapes, in_specs=spec or [VMEM] * len(ar...  11.7 us
    all_to_all x3, starting transfers between devices, swap(): return lax.all_to_all(value, ('y', 'core'), 0, 0, tiled=True)  11.6 us
    pallas_call x1, Pallas kernels, on_device(): pl.pallas_call(functools.partial(finish_kernel, widths), out_shape=(jax.S...  6.3 us
  transfers between devices with their start and end apart: 24, of which 13 were waited for; matrix products, arithmetic and copies ran while one was open for 4% of the time, Pallas kernels for 16%

profile of v1, /device:TPU:32, one launch (start us, length us, event | category | flops | bytes accessed | tf_op | source)
XLA Modules:
  0.0 274.5 jit_solution(4860536759806180329)
XLA Ops:
  7.2 0.7 stack.65.at_ref
  7.9 2.3 shard_map.105
  10.2 3.0 %collective-permute-start.2 = (bf16[1024,128]{1,0:T(8,128)(2,1)}, bf16[1024,128]{1,0:T(8,128)(2,1)S(1)}, u32[]{:S(2)}, u32[]{:S(2)}) collective-permute-start(bf16[1024,128]{1,0:T(8,128)(2,1)} %get-tuple-element.62), channel_id=1, source_target_pairs={{0,16},{8,24},{16,0},{24,8},{1,17},{9,25},{17,1},{25,9},{2,18},{10... | collective-permute-start | bytes 786440 | tf_op jit(solution)/shard_map/ppermute | solution.py:190
  13.2 2.9 %shard_map.104 = bf16[8,128,512]{2,1,0:T(8,128)(2,1)} custom-call(bf16[128,11008]{1,0:T(8,128)(2,1)} %bitcast.48), custom_call_target="tpu_custom_call" | custom-call | flops 1 | bytes 1 | tf_op jit(solution)/shard_map/pallas_call | solution.py:85
  16.1 4.5 %all-to-all-start = ((bf16[8,128,512]{2,1,0:T(8,128)(2,1)}), bf16[8,128,512]{2,1,0:T(8,128)(2,1)S(1)}, u32[]{:S(2)}, u32[]{:S(2)}) async-start(bf16[8,128,512]{2,1,0:T(8,128)(2,1)} %shard_map.104), calls=%async_computation | async-start | bytes 2097152 | tf_op jit(solution)/shard_map/all_to_all | solution.py:196
  20.6 1.2 collective-permute-start.1
  21.8 0.9 collective-permute-start
  22.8 6.6 %collective-permute-done.1 = bf16[1024,128]{1,0:T(8,128)(2,1)S(1)} collective-permute-done((bf16[1024,128]{1,0:T(8,128)(2,1)S(1)}, bf16[1024,128]{1,0:T(8,128)(2,1)S(1)}, u32[]{:S(2)}, u32[]{:S(2)}) %collective-permute-start.1) | collective-permute-done | bytes 262176 | tf_op jit(solution)/shard_map/ppermute | solution.py:190
  29.4 2.1 collective-permute-done
  31.4 0.7 slice_bitcast_fusion.2
  32.1 0.9 pad_maximum_fusion.2
  33.0 3.6 %all-to-all-done = bf16[8,128,512]{2,1,0:T(8,128)(2,1)S(1)} async-done(((bf16[8,128,512]{2,1,0:T(8,128)(2,1)}), bf16[8,128,512]{2,1,0:T(8,128)(2,1)S(1)}, u32[]{:S(2)}, u32[]{:S(2)}) %all-to-all-start) | async-done | bytes 1048608 | tf_op jit(solution)/shard_map/all_to_all | solution.py:196
  36.6 0.6 collective-permute-start.3
  37.2 2.6 collective-permute-start.4
  39.8 3.1 %shard_map.106 = (bf16[8,128,512]{2,1,0:T(8,128)(2,1)}, bf16[8,128,384]{2,1,0:T(8,128)(2,1)}) custom-call(bf16[128,11008]{1,0:T(8,128)(2,1)} %bitcast.49), custom_call_target="tpu_custom_call" | custom-call | flops 1 | bytes 1 | tf_op jit(solution)/shard_map/pallas_call | solution.py:85
  42.9 3.6 %all-to-all-start.1 = ((bf16[8,128,512]{2,1,0:T(8,128)(2,1)}), bf16[8,128,512]{2,1,0:T(8,128)(2,1)S(1)}, u32[]{:S(2)}, u32[]{:S(2)}) async-start(bf16[8,128,512]{2,1,0:T(8,128)(2,1)} %get-tuple-element.64), calls=%async_computation.1 | async-start | bytes 2097152 | tf_op jit(solution)/shard_map/all_to_all | solution.py:196
  46.5 1.8 pad_maximum_fusion.3
  48.3 14.0 %all-to-all-done.1 = bf16[8,128,512]{2,1,0:T(8,128)(2,1)S(1)} async-done(((bf16[8,128,512]{2,1,0:T(8,128)(2,1)}), bf16[8,128,512]{2,1,0:T(8,128)(2,1)S(1)}, u32[]{:S(2)}, u32[]{:S(2)}) %all-to-all-start.1) | async-done | bytes 1048608 | tf_op jit(solution)/shard_map/all_to_all | solution.py:196
  62.4 0.1 collective-permute-done.3.refs_1_
  62.5 1.5 slice.69
  64.0 1.9 pad_maximum_fusion
  66.1 3.2 %collective-permute-start.6 = (bf16[1536,512]{1,0:T(8,128)(2,1)}, bf16[1536,512]{1,0:T(8,128)(2,1)S(1)}, u32[]{:S(2)}, u32[]{:S(2)}) collective-permute-start(bf16[1536,512]{1,0:T(8,128)(2,1)} %get-tuple-element.75), channel_id=1, source_target_pairs={{0,24},{8,0},{16,8},{24,16},{1,25},{9,1},{17,9},{25,17},{2,26},{10... | collective-permute-start | bytes 4718600 | tf_op jit(solution)/shard_map/ppermute | solution.py:190
  69.3 21.6 %all_to_all.30 = bf16[8,128,384]{2,1,0:T(8,128)(2,1)} all-to-all(bf16[8,128,384]{2,1,0:T(8,128)(2,1)} %get-tuple-element.76), channel_id=1, replica_groups=mesh['rep'=4,'zh'=2,'x'=4,'y'=4,'core'=2] {'y','core'}, dimensions={0} | all-to-all | bytes 1572864 | tf_op jit(solution)/shard_map/all_to_all | solution.py:196
  90.9 12.4 %collective-permute-done.5.refs_3_.refs_1_ = bf16[1536,512]{1,0:T(8,128)(2,1)S(1)} collective-permute-done((bf16[1536,512]{1,0:T(8,128)(2,1)}, bf16[1536,512]{1,0:T(8,128)(2,1)S(1)}, u32[]{:S(2)}, u32[]{:S(2)}) %collective-permute-start.5) | collective-permute-done | bytes 1572896 | tf_op jit(solution)/shard_map/ppermute | solution.py:190
  103.3 1.5 all-gather.5.cloned.1.call-done
  104.8 0.8 slice.70
  105.6 0.8 slice.71
  106.6 3.2 %collective-permute-start.8 = (bf16[512,512]{1,0:T(8,128)(2,1)}, bf16[512,512]{1,0:T(8,128)(2,1)S(1)}, u32[]{:S(2)}, u32[]{:S(2)}) collective-permute-start(bf16[512,512]{1,0:T(8,128)(2,1)} %slice.71), channel_id=1, source_target_pairs={{0,24},{8,0},{16,8},{24,16},{1,25},{9,1},{17,9},{25,17},{2,26},{10... | collective-permute-start | bytes 1572872 | tf_op jit(solution)/shard_map/ppermute | solution.py:190
  109.8 6.6 %shard_map.107 = f32[528,512]{1,0:T(8,128)} custom-call(bf16[8,4,512,128]{3,2,1,0:T(8,128)(2,1)} %bitcast.39, bf16[1024,512]{1,0:T(8,128)(2,1)} %bitcast.52, bf16[1024,512]{1,0:T(8,128)(2,1)} %copy-done.5, bf16[1024,512]{1,0:T(8,128)(2,1)} %collective-permute-done.4.refs_2_, bf16[1536,512]{1,0:T(8,128)(2,1)} %copy-done, bf16[1536,512]{1,0:T(8,128)(2,1)} %copy-done.1), custom_call_target="tpu_custom_call" | custom-call | flops 1 | bytes 1 | tf_op jit(solution)/shard_map/pallas_call | solution.py:165
  116.4 1.4 convert_element_type.27
  117.8 4.2 %collective-permute-done.7.refs_3_ = bf16[512,512]{1,0:T(8,128)(2,1)S(1)} collective-permute-done((bf16[512,512]{1,0:T(8,128)(2,1)}, bf16[512,512]{1,0:T(8,128)(2,1)S(1)}, u32[]{:S(2)}, u32[]{:S(2)}) %collective-permute-start.7) | collective-permute-done | bytes 524320 | tf_op jit(solution)/shard_map/ppermute | solution.py:190
  122.1 0.1 collective-permute-start.9
  122.2 3.2 %collective-permute-start.10 = (bf16[1024,384]{1,0:T(8,128)(2,1)S(1)}, bf16[1024,384]{1,0:T(8,128)(2,1)S(1)}, u32[]{:S(2)}, u32[]{:S(2)}) collective-permute-start(bf16[1024,384]{1,0:T(8,128)(2,1)S(1)} %bitcast.57), channel_id=1, source_target_pairs={{0,24},{8,0},{16,8},{24,16},{1,25},{9,1},{17,9},{25,17},{2,26},{10... | collective-permute-start | bytes 2359304 | tf_op jit(solution)/shard_map/ppermute | solution.py:190
  125.4 6.3 %collective-permute-start.11 = (f16[528,512]{1,0:T(8,128)(2,1)S(1)}, f16[528,512]{1,0:T(8,128)(2,1)S(1)}, u32[]{:S(2)}, u32[]{:S(2)}) collective-permute-start(f16[528,512]{1,0:T(8,128)(2,1)S(1)} %convert_element_type.27), channel_id=1, source_target_pairs={{0,32},{32,0},{1,33},{33,1},{2,34},{34,2},{3,35},{35,3},{4,36},{36... | collective-permute-start | bytes 1622024 | tf_op jit(solution)/shard_map/ppermute | solution.py:190
  131.7 6.7 %shard_map.108 = f32[528,512]{1,0:T(8,128)} custom-call(bf16[8,4,512,128]{3,2,1,0:T(8,128)(2,1)} %bitcast.40, bf16[1024,512]{1,0:T(8,128)(2,1)} %bitcast.46, bf16[1536,512]{1,0:T(8,128)(2,1)} %copy-done, bf16[1536,512]{1,0:T(8,128)(2,1)} %copy-done.1, bf16[512,512]{1,0:T(8,128)(2,1)} %copy-done.11, bf16[512,512]{1,0:T(8,128)(2,1)} %copy-done.12), custom_call_target="tpu_custom_call" | custom-call | flops 1 | bytes 1 | tf_op jit(solution)/shard_map/pallas_call | solution.py:165
  138.4 1.3 convert_element_type.28
  139.8 15.1 %collective-permute-done.11 = f16[528,512]{1,0:T(8,128)(2,1)S(1)} collective-permute-done((f16[528,512]{1,0:T(8,128)(2,1)S(1)}, f16[528,512]{1,0:T(8,128)(2,1)S(1)}, u32[]{:S(2)}, u32[]{:S(2)}) %collective-permute-start.11) | collective-permute-done | bytes 540704 | tf_op jit(solution)/shard_map/ppermute | solution.py:190
  154.9 0.8 copy-done.15
  155.8 5.7 %collective-permute-start.12 = (f16[528,512]{1,0:T(8,128)(2,1)S(1)}, f16[528,512]{1,0:T(8,128)(2,1)S(1)}, u32[]{:S(2)}, u32[]{:S(2)}) collective-permute-start(f16[528,512]{1,0:T(8,128)(2,1)S(1)} %convert_element_type.28), channel_id=1, source_target_pairs={{0,32},{32,0},{1,33},{33,1},{2,34},{34,2},{3,35},{35,3},{4,36},{36... | collective-permute-start | bytes 1622024 | tf_op jit(solution)/shard_map/ppermute | solution.py:190
  161.5 3.2 %collective-permute-start.14 = (bf16[512,384]{1,0:T(8,128)(2,1)S(1)}, bf16[512,384]{1,0:T(8,128)(2,1)S(1)}, u32[]{:S(2)}, u32[]{:S(2)}) collective-permute-start(bf16[512,384]{1,0:T(8,128)(2,1)S(1)} %slice.73), channel_id=1, source_target_pairs={{0,24},{8,0},{16,8},{24,16},{1,25},{9,1},{17,9},{25,17},{2,26},{10... | collective-permute-start | bytes 1179656 | tf_op jit(solution)/shard_map/ppermute | solution.py:190
  164.7 0.7 multiply_exponential_fusion.1
  165.4 6.2 %shard_map.110 = f32[512,512]{1,0:T(8,128)} custom-call(bf16[8,4,512,128]{3,2,1,0:T(8,128)(2,1)} %bitcast.42, bf16[1024,512]{1,0:T(8,128)(2,1)} %bitcast.53, bf16[1024,512]{1,0:T(8,128)(2,1)} %copy-done.5, bf16[1024,512]{1,0:T(8,128)(2,1)} %collective-permute-done.4.refs_2_, bf16[1536,512]{1,0:T(8,128)(2,1)} %copy-done, bf16[1536,512]{1,0:T(8,128)(2,1)} %copy-done.1), custom_call_target="tpu_custom_call" | custom-call | flops 1 | bytes 1 | tf_op jit(solution)/shard_map/pallas_call | solution.py:165
  171.6 2.4 multiply_add_fusion.1
  174.0 0.7 copy-done.13
  174.7 0.7 copy-done.14
  175.5 6.2 %shard_map.109 = f32[528,384]{1,0:T(8,128)} custom-call(bf16[8,4,512,128]{3,2,1,0:T(8,128)(2,1)} %bitcast.41, bf16[1024,384]{1,0:T(8,128)(2,1)} %bitcast.54, bf16[1024,384]{1,0:T(8,128)(2,1)} %copy-done.6, bf16[1024,384]{1,0:T(8,128)(2,1)} %copy-done.7, bf16[512,384]{1,0:T(8,128)(2,1)} %copy-done.13, bf16[512,384]{1,0:T(8,128)(2,1)} %copy-done.14), custom_call_target="tpu_custom_call" | custom-call | flops 1 | bytes 1 | tf_op jit(solution)/shard_map/pallas_call | solution.py:165
  181.7 2.0 convert_element_type.29
  183.6 3.6 %all-to-all-start.3 = ((f32[8,64,512]{2,1,0:T(8,128)}), f32[8,64,512]{2,1,0:T(8,128)S(1)}, u32[]{:S(2)}, u32[]{:S(2)}) async-start(f32[8,64,512]{2,1,0:T(8,128)} %bitcast.25), calls=%async_computation.3 | async-start | bytes 2097152 | tf_op jit(solution)/shard_map/all_to_all | solution.py:196
  187.2 2.8 %collective-permute-start.15 = (f16[528,384]{1,0:T(8,128)(2,1)}, f16[528,384]{1,0:T(8,128)(2,1)}, u32[]{:S(2)}, u32[]{:S(2)}) collective-permute-start(f16[528,384]{1,0:T(8,128)(2,1)} %convert_element_type.29), channel_id=1, source_target_pairs={{0,32},{32,0},{1,33},{33,1},{2,34},{34,2},{3,35},{35,3},{4,36},{36... | collective-permute-start | bytes 1216520 | tf_op jit(solution)/shard_map/ppermute | solution.py:190
  190.0 6.1 %shard_map.111 = f32[512,512]{1,0:T(8,128)} custom-call(bf16[8,4,512,128]{3,2,1,0:T(8,128)(2,1)} %bitcast.43, bf16[1024,512]{1,0:T(8,128)(2,1)} %bitcast.47, bf16[1536,512]{1,0:T(8,128)(2,1)} %copy-done, bf16[1536,512]{1,0:T(8,128)(2,1)} %copy-done.1, bf16[512,512]{1,0:T(8,128)(2,1)} %copy-done.11, bf16[512,512]{1,0:T(8,128)(2,1)} %copy-done.12), custom_call_target="tpu_custom_call" | custom-call | flops 1 | bytes 1 | tf_op jit(solution)/shard_map/pallas_call | solution.py:165
  196.1 5.8 %shard_map.112 = f32[512,384]{1,0:T(8,128)} custom-call(bf16[8,4,512,128]{3,2,1,0:T(8,128)(2,1)} %bitcast.44, bf16[1024,384]{1,0:T(8,128)(2,1)} %bitcast.55, bf16[1024,384]{1,0:T(8,128)(2,1)} %copy-done.6, bf16[1024,384]{1,0:T(8,128)(2,1)} %copy-done.7, bf16[512,384]{1,0:T(8,128)(2,1)} %copy-done.13, bf16[512,384]{1,0:T(8,128)(2,1)} %copy-done.14), custom_call_target="tpu_custom_call" | custom-call | flops 1 | bytes 1 | tf_op jit(solution)/shard_map/pallas_call | solution.py:165
  202.0 0.2 multiply_add_fusion
  202.2 5.9 %collective-permute-done.15 = f16[528,384]{1,0:T(8,128)(2,1)} collective-permute-done((f16[528,384]{1,0:T(8,128)(2,1)}, f16[528,384]{1,0:T(8,128)(2,1)}, u32[]{:S(2)}, u32[]{:S(2)}) %collective-permute-start.15) | collective-permute-done | bytes 405536 | tf_op jit(solution)/shard_map/ppermute | solution.py:190
  208.1 0.7 exponential_reduce_fusion
  208.8 1.1 multiply_add_fusion.2
  209.9 17.6 %all_to_all.31.refs_2_ = f32[8,64,384]{2,1,0:T(8,128)} all-to-all(f32[8,64,384]{2,1,0:T(8,128)S(1)} %bitcast.59), channel_id=1, replica_groups=mesh['rep'=4,'zh'=2,'x'=4,'y'=4,'core'=2] {'y','core'}, dimensions={0} | all-to-all | bytes 1572864 | tf_op jit(solution)/shard_map/all_to_all | solution.py:196
  227.5 19.2 %all_to_all.32.refs_1_ = f32[8,64,512]{2,1,0:T(8,128)} all-to-all(f32[8,64,512]{2,1,0:T(8,128)S(1)} %bitcast.58), channel_id=1, replica_groups=mesh['rep'=4,'zh'=2,'x'=4,'y'=4,'core'=2] {'y','core'}, dimensions={0} | all-to-all | bytes 2097152 | tf_op jit(solution)/shard_map/all_to_all | solution.py:196
  246.7 6.3 %finish.1 = (f32[64,11008]{1,0:T(8,128)}, f32[88,128]{1,0:T(8,128)}) custom-call(f32[8,64]{1,0:T(8,128)} %constant.64.clone.basis_ref, f32[64,8]{1,0:T(8,128)} %constant.65.clone.back_ref, f32[1024,128]{1,0:T(8,128)} %constant.66.clone.wide_ref, f32[128,1024]{1,0:T(8,128)} %constant.67.clone.tall_ref, f32[64,11008]{1,0:T(8,128)} %bitcast.61, ...), custom_call_target="tpu_custom_call" | custom-call | tf_op jit(solution)/shard_map/finish/pallas_call | solution.py:277
  253.0 4.4 %collective-permute-start.16 = (f32[88,128]{1,0:T(8,128)}, f32[88,128]{1,0:T(8,128)S(1)}, u32[]{:S(2)}, u32[]{:S(2)}) collective-permute-start(f32[88,128]{1,0:T(8,128)} %get-tuple-element.114.b0), channel_id=1, source_target_pairs={{0,64},{64,128},{128,192},{192,0},{1,65},{65,129},{129,193},{193,1... | collective-permute-start | bytes 135176 | tf_op jit(solution)/shard_map/band/ppermute | solution.py:190
  257.4 2.0 collective-permute-start.17
  259.5 3.1 %collective-permute-done.17.b2 = f32[88,128]{1,0:T(8,128)S(1)} collective-permute-done((f32[88,128]{1,0:T(8,128)}, f32[88,128]{1,0:T(8,128)S(1)}, u32[]{:S(2)}, u32[]{:S(2)}) %collective-permute-start.17) | collective-permute-done | bytes 45088 | tf_op jit(solution)/shard_map/band/ppermute | solution.py:190
  262.6 1.0 collective-permute-done.18.b3
  263.7 0.6 copy-done.20
  264.3 3.4 %update.1 = f32[64,11008]{1,0:T(8,128)} custom-call(f32[64,8]{1,0:T(8,128)} %constant.65.clone.back_ref, f32[128,1024]{1,0:T(8,128)} %constant.67.clone.tall_ref, f32[88,128]{1,0:T(8,128)} %get-tuple-element.114.b0, f32[88,128]{1,0:T(8,128)} %copy-done.18, f32[88,128]{1,0:T(8,128)} %copy-done.19, f32[88,128]{1,0:T(8,128)} %copy-done.20), custom_call_target="tpu_custom_call" | custom-call | flops 1 | bytes 1 | tf_op jit(solution)/shard_map/update/pallas_call | solution.py:85
  (69 shorter events, 0.7 us)
Async XLA Ops:
  10.2 12.5 %collective-permute-start.2 = (bf16[1024,128]{1,0:T(8,128)(2,1)}, bf16[1024,128]{1,0:T(8,128)(2,1)S(1)}, u32[]{:S(2)}, u32[]{:S(2)}) collective-permute-start(bf16[1024,128]{1,0:T(8,128)(2,1)} %get-tuple-element.62), channel_id=1, source_target_pairs={{0,16},{8,24},{16,0},{24,8},{1,17},{9,25},{17,1},{25,9},{2,18},{10... | collective-permute-start | bytes 786440 | tf_op jit(solution)/shard_map/ppermute | solution.py:190
  13.2 7.4 %copy-start.22 = (bf16[1024,128]{1,0:T(8,128)(2,1)S(1)}, bf16[1024,128]{1,0:T(8,128)(2,1)}, u32[]{:S(2)}) copy-start(bf16[1024,128]{1,0:T(8,128)(2,1)} %get-tuple-element.61) | copy-start | bytes 786436
  13.2 8.6 %copy-start.21 = (bf16[1024,128]{1,0:T(8,128)(2,1)S(1)}, bf16[1024,128]{1,0:T(8,128)(2,1)}, u32[]{:S(2)}) copy-start(bf16[1024,128]{1,0:T(8,128)(2,1)} %get-tuple-element.60) | copy-start | bytes 786436
  13.2 9.5 %copy-start.17 = (bf16[1024,128]{1,0:T(8,128)(2,1)S(1)}, bf16[1024,128]{1,0:T(8,128)(2,1)}, u32[]{:S(2)}) copy-start(bf16[1024,128]{1,0:T(8,128)(2,1)} %get-tuple-element.59) | copy-start | bytes 786436
  16.1 20.4 %all-to-all-start = ((bf16[8,128,512]{2,1,0:T(8,128)(2,1)}), bf16[8,128,512]{2,1,0:T(8,128)(2,1)S(1)}, u32[]{:S(2)}, u32[]{:S(2)}) async-start(bf16[8,128,512]{2,1,0:T(8,128)(2,1)} %shard_map.104), calls=%async_computation | async-start | bytes 2097152 | tf_op jit(solution)/shard_map/all_to_all | solution.py:196
  20.6 8.7 %collective-permute-start.1 = (bf16[1024,128]{1,0:T(8,128)(2,1)S(1)}, bf16[1024,128]{1,0:T(8,128)(2,1)S(1)}, u32[]{:S(2)}, u32[]{:S(2)}) collective-permute-start(bf16[1024,128]{1,0:T(8,128)(2,1)S(1)} %copy-done.22), channel_id=1, source_target_pairs={{0,24},{8,0},{16,8},{24,16},{1,25},{9,1},{17,9},{25,17},{2,26},{10... | collective-permute-start | bytes 786440 | tf_op jit(solution)/shard_map/ppermute | solution.py:190
  21.8 9.6 %collective-permute-start = (bf16[1024,128]{1,0:T(8,128)(2,1)S(1)}, bf16[1024,128]{1,0:T(8,128)(2,1)S(1)}, u32[]{:S(2)}, u32[]{:S(2)}) collective-permute-start(bf16[1024,128]{1,0:T(8,128)(2,1)S(1)} %copy-done.21), channel_id=1, source_target_pairs={{0,8},{8,16},{16,24},{24,0},{1,9},{9,17},{17,25},{25,1},{2,10},{10... | collective-permute-start | bytes 786440 | tf_op jit(solution)/shard_map/ppermute | solution.py:190
  36.6 11.7 %copy-start.3 = (bf16[8,128,512]{2,1,0:T(8,128)(2,1)}, bf16[8,128,512]{2,1,0:T(8,128)(2,1)S(1)}, u32[]{:S(2)}) copy-start(bf16[8,128,512]{2,1,0:T(8,128)(2,1)S(1)} %all-to-all-done) | copy-start | bytes 3145732
  36.6 25.9 %collective-permute-start.3 = (bf16[1024,512]{1,0:T(8,128)(2,1)S(1)}, bf16[1024,512]{1,0:T(8,128)(2,1)S(1)}, u32[]{:S(2)}, u32[]{:S(2)}) collective-permute-start(bf16[1024,512]{1,0:T(8,128)(2,1)S(1)} %bitcast.50), channel_id=1, source_target_pairs={{0,8},{8,16},{16,24},{24,0},{1,9},{9,17},{17,25},{25,1},{2,10},{10... | collective-permute-start | bytes 3145736 | tf_op jit(solution)/shard_map/ppermute | solution.py:190
  37.2 25.3 %collective-permute-start.4 = (bf16[1024,512]{1,0:T(8,128)(2,1)S(1)}, bf16[1024,512]{1,0:T(8,128)(2,1)}, u32[]{:S(2)}, u32[]{:S(2)}) collective-permute-start(bf16[1024,512]{1,0:T(8,128)(2,1)S(1)} %bitcast.51), channel_id=1, source_target_pairs={{0,24},{8,0},{16,8},{24,16},{1,25},{9,1},{17,9},{25,17},{2,26},{10... | collective-permute-start | bytes 3145736 | tf_op jit(solution)/shard_map/ppermute | solution.py:190
  42.9 19.5 %all-to-all-start.1 = ((bf16[8,128,512]{2,1,0:T(8,128)(2,1)}), bf16[8,128,512]{2,1,0:T(8,128)(2,1)S(1)}, u32[]{:S(2)}, u32[]{:S(2)}) async-start(bf16[8,128,512]{2,1,0:T(8,128)(2,1)} %get-tuple-element.64), calls=%async_computation.1 | async-start | bytes 2097152 | tf_op jit(solution)/shard_map/all_to_all | solution.py:196
  46.5 58.3 %all-gather.5.cloned.1.call-start = ((), (), s32[]{:S(2)}) async-start(), calls=%async_computation.6 | async-start | bytes 4718592 | tf_op jit(solution)/shard_map/all_gather | solution.py:242
  62.4 3.5 %copy-start.2 = (bf16[8,128,512]{2,1,0:T(8,128)(2,1)}, bf16[8,128,512]{2,1,0:T(8,128)(2,1)S(1)}, u32[]{:S(2)}) copy-start(bf16[8,128,512]{2,1,0:T(8,128)(2,1)S(1)} %all-to-all-done.1) | copy-start | bytes 3145732
  62.5 3.4 %copy-start.5 = (bf16[1024,512]{1,0:T(8,128)(2,1)}, bf16[1024,512]{1,0:T(8,128)(2,1)S(1)}, u32[]{:S(2)}) copy-start(bf16[1024,512]{1,0:T(8,128)(2,1)S(1)} %collective-permute-done.3.refs_1_) | copy-start | bytes 3145732
  65.9 89.8 %all-gather.7.cloned.1.call-start = ((), (), s32[]{:S(2)}) async-start(), calls=%async_computation.7 | async-start | bytes 4718592 | tf_op jit(solution)/shard_map/all_gather | solution.py:249
  66.0 37.3 %collective-permute-start.5 = (bf16[1536,512]{1,0:T(8,128)(2,1)}, bf16[1536,512]{1,0:T(8,128)(2,1)S(1)}, u32[]{:S(2)}, u32[]{:S(2)}) collective-permute-start(bf16[1536,512]{1,0:T(8,128)(2,1)} %get-tuple-element.74), channel_id=1, source_target_pairs={{0,8},{8,16},{16,24},{24,0},{1,9},{9,17},{17,25},{25,1},{2,10},{10... | collective-permute-start | bytes 4718600 | tf_op jit(solution)/shard_map/ppermute | solution.py:190
  66.1 37.2 %collective-permute-start.6 = (bf16[1536,512]{1,0:T(8,128)(2,1)}, bf16[1536,512]{1,0:T(8,128)(2,1)S(1)}, u32[]{:S(2)}, u32[]{:S(2)}) collective-permute-start(bf16[1536,512]{1,0:T(8,128)(2,1)} %get-tuple-element.75), channel_id=1, source_target_pairs={{0,24},{8,0},{16,8},{24,16},{1,25},{9,1},{17,9},{25,17},{2,26},{10... | collective-permute-start | bytes 4718600 | tf_op jit(solution)/shard_map/ppermute | solution.py:190
  103.3 6.5 %copy-start = (bf16[1536,512]{1,0:T(8,128)(2,1)}, bf16[1536,512]{1,0:T(8,128)(2,1)S(1)}, u32[]{:S(2)}) copy-start(bf16[1536,512]{1,0:T(8,128)(2,1)S(1)} %collective-permute-done.5.refs_3_.refs_1_) | copy-start | bytes 4718596
  103.3 6.5 %copy-start.1 = (bf16[1536,512]{1,0:T(8,128)(2,1)}, bf16[1536,512]{1,0:T(8,128)(2,1)S(1)}, u32[]{:S(2)}) copy-start(bf16[1536,512]{1,0:T(8,128)(2,1)S(1)} %collective-permute-done.6.refs_4_.refs_2_) | copy-start | bytes 4718596
  106.5 15.6 %copy-start.4 = (bf16[8,128,384]{2,1,0:T(8,128)(2,1)S(1)}, bf16[8,128,384]{2,1,0:T(8,128)(2,1)}, u32[]{:S(2)}) copy-start(bf16[8,128,384]{2,1,0:T(8,128)(2,1)} %all_to_all.30) | copy-start | bytes 2359300
  106.5 15.6 %collective-permute-start.7 = (bf16[512,512]{1,0:T(8,128)(2,1)}, bf16[512,512]{1,0:T(8,128)(2,1)S(1)}, u32[]{:S(2)}, u32[]{:S(2)}) collective-permute-start(bf16[512,512]{1,0:T(8,128)(2,1)} %slice.70), channel_id=1, source_target_pairs={{0,8},{8,16},{16,24},{24,0},{1,9},{9,17},{17,25},{25,1},{2,10},{10... | collective-permute-start | bytes 1572872 | tf_op jit(solution)/shard_map/ppermute | solution.py:190
  106.6 15.5 %collective-permute-start.8 = (bf16[512,512]{1,0:T(8,128)(2,1)}, bf16[512,512]{1,0:T(8,128)(2,1)S(1)}, u32[]{:S(2)}, u32[]{:S(2)}) collective-permute-start(bf16[512,512]{1,0:T(8,128)(2,1)} %slice.71), channel_id=1, source_target_pairs={{0,24},{8,0},{16,8},{24,16},{1,25},{9,1},{17,9},{25,17},{2,26},{10... | collective-permute-start | bytes 1572872 | tf_op jit(solution)/shard_map/ppermute | solution.py:190
  122.1 9.6 %copy-start.11 = (bf16[512,512]{1,0:T(8,128)(2,1)}, bf16[512,512]{1,0:T(8,128)(2,1)S(1)}, u32[]{:S(2)}) copy-start(bf16[512,512]{1,0:T(8,128)(2,1)S(1)} %collective-permute-done.7.refs_3_) | copy-start | bytes 1572868
  122.1 9.6 %copy-start.12 = (bf16[512,512]{1,0:T(8,128)(2,1)}, bf16[512,512]{1,0:T(8,128)(2,1)S(1)}, u32[]{:S(2)}) copy-start(bf16[512,512]{1,0:T(8,128)(2,1)S(1)} %collective-permute-done.8.refs_4_) | copy-start | bytes 1572868
  122.1 32.8 %collective-permute-start.9 = (bf16[1024,384]{1,0:T(8,128)(2,1)S(1)}, bf16[1024,384]{1,0:T(8,128)(2,1)S(1)}, u32[]{:S(2)}, u32[]{:S(2)}) collective-permute-start(bf16[1024,384]{1,0:T(8,128)(2,1)S(1)} %bitcast.56), channel_id=1, source_target_pairs={{0,8},{8,16},{16,24},{24,0},{1,9},{9,17},{17,25},{25,1},{2,10},{10... | collective-permute-start | bytes 2359304 | tf_op jit(solution)/shard_map/ppermute | solution.py:190
  122.2 33.5 %collective-permute-start.10 = (bf16[1024,384]{1,0:T(8,128)(2,1)S(1)}, bf16[1024,384]{1,0:T(8,128)(2,1)S(1)}, u32[]{:S(2)}, u32[]{:S(2)}) collective-permute-start(bf16[1024,384]{1,0:T(8,128)(2,1)S(1)} %bitcast.57), channel_id=1, source_target_pairs={{0,24},{8,0},{16,8},{24,16},{1,25},{9,1},{17,9},{25,17},{2,26},{10... | collective-permute-start | bytes 2359304 | tf_op jit(solution)/shard_map/ppermute | solution.py:190
  125.4 29.5 %collective-permute-start.11 = (f16[528,512]{1,0:T(8,128)(2,1)S(1)}, f16[528,512]{1,0:T(8,128)(2,1)S(1)}, u32[]{:S(2)}, u32[]{:S(2)}) collective-permute-start(f16[528,512]{1,0:T(8,128)(2,1)S(1)} %convert_element_type.27), channel_id=1, source_target_pairs={{0,32},{32,0},{1,33},{33,1},{2,34},{34,2},{3,35},{35,3},{4,36},{36... | collective-permute-start | bytes 1622024 | tf_op jit(solution)/shard_map/ppermute | solution.py:190
  154.9 0.8 copy-start.15
  155.7 15.9 %copy-start.6 = (bf16[1024,384]{1,0:T(8,128)(2,1)}, bf16[1024,384]{1,0:T(8,128)(2,1)S(1)}, u32[]{:S(2)}) copy-start(bf16[1024,384]{1,0:T(8,128)(2,1)S(1)} %collective-permute-done.9.refs_1_) | copy-start | bytes 2359300
  155.7 15.9 %copy-start.7 = (bf16[1024,384]{1,0:T(8,128)(2,1)}, bf16[1024,384]{1,0:T(8,128)(2,1)S(1)}, u32[]{:S(2)}) copy-start(bf16[1024,384]{1,0:T(8,128)(2,1)S(1)} %collective-permute-done.10.refs_2_) | copy-start | bytes 2359300
  155.8 27.8 %collective-permute-start.12 = (f16[528,512]{1,0:T(8,128)(2,1)S(1)}, f16[528,512]{1,0:T(8,128)(2,1)S(1)}, u32[]{:S(2)}, u32[]{:S(2)}) collective-permute-start(f16[528,512]{1,0:T(8,128)(2,1)S(1)} %convert_element_type.28), channel_id=1, source_target_pairs={{0,32},{32,0},{1,33},{33,1},{2,34},{34,2},{3,35},{35,3},{4,36},{36... | collective-permute-start | bytes 1622024 | tf_op jit(solution)/shard_map/ppermute | solution.py:190
  161.5 12.5 %collective-permute-start.13 = (bf16[512,384]{1,0:T(8,128)(2,1)S(1)}, bf16[512,384]{1,0:T(8,128)(2,1)S(1)}, u32[]{:S(2)}, u32[]{:S(2)}) collective-permute-start(bf16[512,384]{1,0:T(8,128)(2,1)S(1)} %slice.72), channel_id=1, source_target_pairs={{0,8},{8,16},{16,24},{24,0},{1,9},{9,17},{17,25},{25,1},{2,10},{10... | collective-permute-start | bytes 1179656 | tf_op jit(solution)/shard_map/ppermute | solution.py:190
  161.5 12.5 %collective-permute-start.14 = (bf16[512,384]{1,0:T(8,128)(2,1)S(1)}, bf16[512,384]{1,0:T(8,128)(2,1)S(1)}, u32[]{:S(2)}, u32[]{:S(2)}) collective-permute-start(bf16[512,384]{1,0:T(8,128)(2,1)S(1)} %slice.73), channel_id=1, source_target_pairs={{0,24},{8,0},{16,8},{24,16},{1,25},{9,1},{17,9},{25,17},{2,26},{10... | collective-permute-start | bytes 1179656 | tf_op jit(solution)/shard_map/ppermute | solution.py:190
  165.4 6.2 %copy-start.16 = (f16[528,512]{1,0:T(8,128)(2,1)S(1)}, f16[528,512]{1,0:T(8,128)(2,1)}, u32[]{:S(2)}) copy-start(f16[528,512]{1,0:T(8,128)(2,1)} %copy-done.15) | copy-start | bytes 1622020
  174.0 0.8 copy-start.13
  174.7 0.7 copy-start.14
  183.6 24.4 %all-to-all-start.3 = ((f32[8,64,512]{2,1,0:T(8,128)}), f32[8,64,512]{2,1,0:T(8,128)S(1)}, u32[]{:S(2)}, u32[]{:S(2)}) async-start(f32[8,64,512]{2,1,0:T(8,128)} %bitcast.25), calls=%async_computation.3 | async-start | bytes 2097152 | tf_op jit(solution)/shard_map/all_to_all | solution.py:196
  187.2 20.9 %collective-permute-start.15 = (f16[528,384]{1,0:T(8,128)(2,1)}, f16[528,384]{1,0:T(8,128)(2,1)}, u32[]{:S(2)}, u32[]{:S(2)}) collective-permute-start(f16[528,384]{1,0:T(8,128)(2,1)} %convert_element_type.29), channel_id=1, source_target_pairs={{0,32},{32,0},{1,33},{33,1},{2,34},{34,2},{3,35},{35,3},{4,36},{36... | collective-permute-start | bytes 1216520 | tf_op jit(solution)/shard_map/ppermute | solution.py:190
  196.1 5.9 %copy-start.8 = (f32[512,512]{1,0:T(8,128)S(1)}, f32[512,512]{1,0:T(8,128)}, u32[]{:S(2)}) copy-start(f32[512,512]{1,0:T(8,128)} %shard_map.111) | copy-start | bytes 3145732
  201.9 6.8 %copy-start.10 = (f32[512,384]{1,0:T(8,128)S(1)}, f32[512,384]{1,0:T(8,128)}, u32[]{:S(2)}) copy-start(f32[512,384]{1,0:T(8,128)} %shard_map.112) | copy-start | bytes 2359300
  208.1 38.6 %copy-start.9 = (f32[8,64,512]{2,1,0:T(8,128)}, f32[8,64,512]{2,1,0:T(8,128)S(1)}, u32[]{:S(2)}) copy-start(f32[8,64,512]{2,1,0:T(8,128)S(1)} %all-to-all-done.3.refs_0_) | copy-start | bytes 3145732
  253.0 6.5 %collective-permute-start.16 = (f32[88,128]{1,0:T(8,128)}, f32[88,128]{1,0:T(8,128)S(1)}, u32[]{:S(2)}, u32[]{:S(2)}) collective-permute-start(f32[88,128]{1,0:T(8,128)} %get-tuple-element.114.b0), channel_id=1, source_target_pairs={{0,64},{64,128},{128,192},{192,0},{1,65},{65,129},{129,193},{193,1... | collective-permute-start | bytes 135176 | tf_op jit(solution)/shard_map/band/ppermute | solution.py:190
  257.4 5.2 %collective-permute-start.17 = (f32[88,128]{1,0:T(8,128)}, f32[88,128]{1,0:T(8,128)S(1)}, u32[]{:S(2)}, u32[]{:S(2)}) collective-permute-start(f32[88,128]{1,0:T(8,128)} %get-tuple-element.114.b0), channel_id=1, source_target_pairs={{0,128},{64,192},{128,0},{192,64},{1,129},{65,193},{129,1},{193,65... | collective-permute-start | bytes 135176 | tf_op jit(solution)/shard_map/band/ppermute | solution.py:190
  259.4 4.3 %collective-permute-start.18 = (f32[88,128]{1,0:T(8,128)}, f32[88,128]{1,0:T(8,128)S(1)}, u32[]{:S(2)}, u32[]{:S(2)}) collective-permute-start(f32[88,128]{1,0:T(8,128)} %get-tuple-element.114.b0), channel_id=1, source_target_pairs={{0,192},{64,0},{128,64},{192,128},{1,193},{65,1},{129,65},{193,129... | collective-permute-start | bytes 135176 | tf_op jit(solution)/shard_map/band/ppermute | solution.py:190
  259.5 4.2 %copy-start.18 = (f32[88,128]{1,0:T(8,128)}, f32[88,128]{1,0:T(8,128)S(1)}, u32[]{:S(2)}) copy-start(f32[88,128]{1,0:T(8,128)S(1)} %collective-permute-done.16.b1) | copy-start | bytes 135172
  262.6 1.0 copy-start.19
  263.7 0.6 copy-start.20
Sparse Core Ops, SparseCore 0:
  66.1 38.6 all-gather.4
  106.6 33.9 all-gather.6

commit v2 on v1

--- a/solution.py
+++ b/solution.py
@@ -174,6 +174,15 @@
     )(lefts, *rights)
 
 
+def join_kernel(*refs):
+    out, lead = refs[-1], 0
+    for keep_ref, got_ref in zip(refs[:-1:2], refs[1:-1:2]):
+        half, w = keep_ref.shape
+        scale = jnp.exp2(-got_ref[half : half + 1, :1])
+        out[:, lead : lead + w] = keep_ref[...] + got_ref[:half] * scale
+        lead += w
+
+
 def on_device(activations, unit_grads, momentum):
     acts, units, mom = activations[0], unit_grads[0], momentum[0, 0]
     tok, features = acts.shape
@@ -264,23 +273,26 @@
     got1, send2, total0, kept = sync(got1, send2, total0, kept)
     got2 = along("zh", 1, send2)
     done0 = swap(total0)
-    total1 = joined(tile(keep_kernel, kept, [v1, r1, l1, *far1], 0), got1)
+    keep1 = tile(keep_kernel, kept, [v1, r1, l1, *far1], 0)
     keep2 = tile(keep_kernel, kept, [v2, r2, l2, *far2], 0)
-
-    got2, done0, total1, keep2 = sync(got2, done0, total1, keep2)
-    done = [done0, swap(total1), swap(joined(keep2, got2))]
+    other1 = got1.astype(f32)
+
+    got2, done0, keep1, keep2, other1 = sync(got2, done0, keep1, keep2, other1)
+    late = block - widths[0]
+    (total,) = call(join_kernel, [((half, late), f32)], keep1, other1, keep2, got2.astype(f32))
+    done = [done0, swap(total.reshape(8, own_rows, late))]
 
     basis = band_table()
     wide = np.kron(np.eye(GROUP // SPAN, dtype=np.float32), basis.T)
     rows = len(groups_of(width)) * BAND
     with jax.named_scope("finish"):
         new, band = pl.pallas_call(
-            functools.partial(finish_kernel, widths),
+            functools.partial(finish_kernel, [d.shape[2] for d in done]),
             out_shape=(
                 jax.ShapeDtypeStruct(mom.shape, f32),
                 jax.ShapeDtypeStruct((rows, LANES), f32),
             ),
-            in_specs=[VMEM] * (5 + len(widths)),
+            in_specs=[VMEM] * (5 + len(done)),
             out_specs=(VMEM, VMEM),
             scratch_shapes=[pltpu.VMEM((rows, GROUP), f32)],
             compiler_params=PARAMS,

time: 275 us -> 270 us (0.982)
  blocking collectives: 58.4 us -> 50.8 us
  Pallas kernels: 55.7 us -> 59.2 us
    all_to_all x3 -> x2, blocking collectives: 58.4 us -> 50.8 us  [swap(): return lax.all_to_all(value, ('y', 'core'), 0, 0, tiled=True)]
    pallas_call x4 -> x5, Pallas kernels: 11.7 us -> 15.2 us  [call(): pl.pallas_call(kernel, out_shape=shapes, in_specs=spec or [VMEM] * len(ar...]
  transfers between devices with their start and end apart: 24 -> 24, of which waited for: 13 -> 14; matrix products, arithmetic and copies ran while one was open for 4% -> 4% of each run, Pallas kernels for 16% -> 16%
where the time goes in v2:
time: 270 us; the launch traced here: 269 us
  waiting for transfers between devices  68.2 us (25%)
  Pallas kernels  59.2 us (22%)
  starting transfers between devices  55.1 us (20%)
  blocking collectives  50.8 us (19%)
  between operations  14.3 us (5%)
  other arithmetic  13.7 us (5%)
  local copies, waits for them, and re-layouts  7.53 us (3%)
    all_to_all x2, blocking collectives, swap(): return lax.all_to_all(value, ('y', 'core'), 0, 0, tiled=True)  50.8 us
    ppermute x19, waiting for transfers between devices, along(): lax.ppermute(value, axis, shift(2 if axis in ('core', 'zh') else 4, by))  49 us
    ppermute x19, starting transfers between devices, along(): lax.ppermute(value, axis, shift(2 if axis in ('core', 'zh') else 4, by))  43.3 us
    pallas_call x6, Pallas kernels, tile(): pl.pallas_call(kernel, grid=(half // rows,), out_shape=jax.ShapeDtypeStru...  37.6 us
    all_to_all x3, waiting for transfers between devices, swap(): return lax.all_to_all(value, ('y', 'core'), 0, 0, tiled=True)  17.7 us
    pallas_call x5, Pallas kernels, call(): pl.pallas_call(kernel, out_shape=shapes, in_specs=spec or [VMEM] * len(ar...  15.2 us
    all_to_all x3, starting transfers between devices, swap(): return lax.all_to_all(value, ('y', 'core'), 0, 0, tiled=True)  11.7 us
    pallas_call x1, Pallas kernels, on_device(): pl.pallas_call(functools.partial(finish_kernel, [d.shape[2] for d in done...  6.38 us
  transfers between devices with their start and end apart: 24, of which 14 were waited for; matrix products, arithmetic and copies ran while one was open for 4% of the time, Pallas kernels for 16%

profile of v2, /device:TPU:32, one launch (start us, length us, event | category | flops | bytes accessed | tf_op | source)
XLA Modules:
  0.0 268.7 jit_solution(11141434535577595716)
XLA Ops:
  7.2 0.7 stack.65.at_ref
  7.9 2.3 shard_map.105
  10.2 3.0 %collective-permute-start.2 = (bf16[1024,128]{1,0:T(8,128)(2,1)}, bf16[1024,128]{1,0:T(8,128)(2,1)S(1)}, u32[]{:S(2)}, u32[]{:S(2)}) collective-permute-start(bf16[1024,128]{1,0:T(8,128)(2,1)} %get-tuple-element.63), channel_id=1, source_target_pairs={{0,16},{8,24},{16,0},{24,8},{1,17},{9,25},{17,1},{25,9},{2,18},{10... | collective-permute-start | bytes 786440 | tf_op jit(solution)/shard_map/ppermute | solution.py:199
  13.2 2.8 %shard_map.104 = bf16[8,128,512]{2,1,0:T(8,128)(2,1)} custom-call(bf16[128,11008]{1,0:T(8,128)(2,1)} %bitcast.46), custom_call_target="tpu_custom_call" | custom-call | flops 1 | bytes 1 | tf_op jit(solution)/shard_map/pallas_call | solution.py:85
  16.1 4.6 %all-to-all-start = ((bf16[8,128,512]{2,1,0:T(8,128)(2,1)}), bf16[8,128,512]{2,1,0:T(8,128)(2,1)S(1)}, u32[]{:S(2)}, u32[]{:S(2)}) async-start(bf16[8,128,512]{2,1,0:T(8,128)(2,1)} %shard_map.104), calls=%async_computation | async-start | bytes 2097152 | tf_op jit(solution)/shard_map/all_to_all | solution.py:205
  20.7 1.2 collective-permute-start.1
  21.9 0.9 collective-permute-start
  22.8 6.6 %collective-permute-done.1 = bf16[1024,128]{1,0:T(8,128)(2,1)S(1)} collective-permute-done((bf16[1024,128]{1,0:T(8,128)(2,1)S(1)}, bf16[1024,128]{1,0:T(8,128)(2,1)S(1)}, u32[]{:S(2)}, u32[]{:S(2)}) %collective-permute-start.1) | collective-permute-done | bytes 262176 | tf_op jit(solution)/shard_map/ppermute | solution.py:199
  29.4 2.1 collective-permute-done
  31.5 0.7 slice_bitcast_fusion.2
  32.1 0.9 pad_maximum_fusion.2
  33.0 3.6 %all-to-all-done = bf16[8,128,512]{2,1,0:T(8,128)(2,1)S(1)} async-done(((bf16[8,128,512]{2,1,0:T(8,128)(2,1)}), bf16[8,128,512]{2,1,0:T(8,128)(2,1)S(1)}, u32[]{:S(2)}, u32[]{:S(2)}) %all-to-all-start) | async-done | bytes 1048608 | tf_op jit(solution)/shard_map/all_to_all | solution.py:205
  36.6 0.6 collective-permute-start.3
  37.2 2.6 collective-permute-start.4
  39.9 3.1 %shard_map.106 = (bf16[8,128,512]{2,1,0:T(8,128)(2,1)}, bf16[8,128,384]{2,1,0:T(8,128)(2,1)}) custom-call(bf16[128,11008]{1,0:T(8,128)(2,1)} %bitcast.47), custom_call_target="tpu_custom_call" | custom-call | flops 1 | bytes 1 | tf_op jit(solution)/shard_map/pallas_call | solution.py:85
  43.0 3.6 %all-to-all-start.1 = ((bf16[8,128,512]{2,1,0:T(8,128)(2,1)}), bf16[8,128,512]{2,1,0:T(8,128)(2,1)S(1)}, u32[]{:S(2)}, u32[]{:S(2)}) async-start(bf16[8,128,512]{2,1,0:T(8,128)(2,1)} %get-tuple-element.65), calls=%async_computation.1 | async-start | bytes 2097152 | tf_op jit(solution)/shard_map/all_to_all | solution.py:205
  46.6 1.8 pad_maximum_fusion.3
  48.4 14.1 %all-to-all-done.1 = bf16[8,128,512]{2,1,0:T(8,128)(2,1)S(1)} async-done(((bf16[8,128,512]{2,1,0:T(8,128)(2,1)}), bf16[8,128,512]{2,1,0:T(8,128)(2,1)S(1)}, u32[]{:S(2)}, u32[]{:S(2)}) %all-to-all-start.1) | async-done | bytes 1048608 | tf_op jit(solution)/shard_map/all_to_all | solution.py:205
  62.4 0.1 collective-permute-done.3.refs_1_
  62.6 1.5 slice.57
  64.1 1.9 pad_maximum_fusion
  66.1 3.2 %collective-permute-start.6 = (bf16[1536,512]{1,0:T(8,128)(2,1)}, bf16[1536,512]{1,0:T(8,128)(2,1)S(1)}, u32[]{:S(2)}, u32[]{:S(2)}) collective-permute-start(bf16[1536,512]{1,0:T(8,128)(2,1)} %get-tuple-element.76), channel_id=1, source_target_pairs={{0,24},{8,0},{16,8},{24,16},{1,25},{9,1},{17,9},{25,17},{2,26},{10... | collective-permute-start | bytes 4718600 | tf_op jit(solution)/shard_map/ppermute | solution.py:199
  69.3 21.6 %all_to_all.25 = bf16[8,128,384]{2,1,0:T(8,128)(2,1)} all-to-all(bf16[8,128,384]{2,1,0:T(8,128)(2,1)} %get-tuple-element.77), channel_id=1, replica_groups=mesh['rep'=4,'zh'=2,'x'=4,'y'=4,'core'=2] {'y','core'}, dimensions={0} | all-to-all | bytes 1572864 | tf_op jit(solution)/shard_map/all_to_all | solution.py:205
  90.9 12.4 %collective-permute-done.5.refs_3_.refs_1_ = bf16[1536,512]{1,0:T(8,128)(2,1)S(1)} collective-permute-done((bf16[1536,512]{1,0:T(8,128)(2,1)}, bf16[1536,512]{1,0:T(8,128)(2,1)S(1)}, u32[]{:S(2)}, u32[]{:S(2)}) %collective-permute-start.5) | collective-permute-done | bytes 1572896 | tf_op jit(solution)/shard_map/ppermute | solution.py:199
  103.4 1.5 all-gather.5.cloned.1.call-done
  104.8 0.8 slice.58
  105.7 0.8 slice.59
  106.6 3.2 %collective-permute-start.8 = (bf16[512,512]{1,0:T(8,128)(2,1)}, bf16[512,512]{1,0:T(8,128)(2,1)S(1)}, u32[]{:S(2)}, u32[]{:S(2)}) collective-permute-start(bf16[512,512]{1,0:T(8,128)(2,1)} %slice.59), channel_id=1, source_target_pairs={{0,24},{8,0},{16,8},{24,16},{1,25},{9,1},{17,9},{25,17},{2,26},{10... | collective-permute-start | bytes 1572872 | tf_op jit(solution)/shard_map/ppermute | solution.py:199
  109.8 6.6 %shard_map.107 = f32[528,512]{1,0:T(8,128)} custom-call(bf16[8,4,512,128]{3,2,1,0:T(8,128)(2,1)} %bitcast.37, bf16[1024,512]{1,0:T(8,128)(2,1)} %bitcast.50, bf16[1024,512]{1,0:T(8,128)(2,1)} %copy-done.5, bf16[1024,512]{1,0:T(8,128)(2,1)} %collective-permute-done.4.refs_2_, bf16[1536,512]{1,0:T(8,128)(2,1)} %copy-done, bf16[1536,512]{1,0:T(8,128)(2,1)} %copy-done.1), custom_call_target="tpu_custom_call" | custom-call | flops 1 | bytes 1 | tf_op jit(solution)/shard_map/pallas_call | solution.py:165
  116.5 1.4 convert_element_type.21
  117.9 4.2 %collective-permute-done.7.refs_3_ = bf16[512,512]{1,0:T(8,128)(2,1)S(1)} collective-permute-done((bf16[512,512]{1,0:T(8,128)(2,1)}, bf16[512,512]{1,0:T(8,128)(2,1)S(1)}, u32[]{:S(2)}, u32[]{:S(2)}) %collective-permute-start.7) | collective-permute-done | bytes 524320 | tf_op jit(solution)/shard_map/ppermute | solution.py:199
  122.2 3.2 %collective-permute-start.10 = (bf16[1024,384]{1,0:T(8,128)(2,1)S(1)}, bf16[1024,384]{1,0:T(8,128)(2,1)S(1)}, u32[]{:S(2)}, u32[]{:S(2)}) collective-permute-start(bf16[1024,384]{1,0:T(8,128)(2,1)S(1)} %bitcast.56), channel_id=1, source_target_pairs={{0,24},{8,0},{16,8},{24,16},{1,25},{9,1},{17,9},{25,17},{2,26},{10... | collective-permute-start | bytes 2359304 | tf_op jit(solution)/shard_map/ppermute | solution.py:199
  125.4 6.3 %collective-permute-start.11 = (f16[528,512]{1,0:T(8,128)(2,1)S(1)}, f16[528,512]{1,0:T(8,128)(2,1)S(1)}, u32[]{:S(2)}, u32[]{:S(2)}) collective-permute-start(f16[528,512]{1,0:T(8,128)(2,1)S(1)} %convert_element_type.21), channel_id=1, source_target_pairs={{0,32},{32,0},{1,33},{33,1},{2,34},{34,2},{3,35},{35,3},{4,36},{36... | collective-permute-start | bytes 1622024 | tf_op jit(solution)/shard_map/ppermute | solution.py:199
  131.7 6.7 %shard_map.108 = f32[528,512]{1,0:T(8,128)} custom-call(bf16[8,4,512,128]{3,2,1,0:T(8,128)(2,1)} %bitcast.38, bf16[1024,512]{1,0:T(8,128)(2,1)} %bitcast.44, bf16[1536,512]{1,0:T(8,128)(2,1)} %copy-done, bf16[1536,512]{1,0:T(8,128)(2,1)} %copy-done.1, bf16[512,512]{1,0:T(8,128)(2,1)} %copy-done.9, bf16[512,512]{1,0:T(8,128)(2,1)} %copy-done.10), custom_call_target="tpu_custom_call" | custom-call | flops 1 | bytes 1 | tf_op jit(solution)/shard_map/pallas_call | solution.py:165
  138.5 1.3 convert_element_type.22
  139.8 15.1 %collective-permute-done.11 = f16[528,512]{1,0:T(8,128)(2,1)S(1)} collective-permute-done((f16[528,512]{1,0:T(8,128)(2,1)S(1)}, f16[528,512]{1,0:T(8,128)(2,1)S(1)}, u32[]{:S(2)}, u32[]{:S(2)}) %collective-permute-start.11) | collective-permute-done | bytes 540704 | tf_op jit(solution)/shard_map/ppermute | solution.py:199
  155.0 0.7 copy-done.13
  155.8 5.7 %collective-permute-start.12 = (f16[528,512]{1,0:T(8,128)(2,1)S(1)}, f16[528,512]{1,0:T(8,128)(2,1)S(1)}, u32[]{:S(2)}, u32[]{:S(2)}) collective-permute-start(f16[528,512]{1,0:T(8,128)(2,1)S(1)} %convert_element_type.22), channel_id=1, source_target_pairs={{0,32},{32,0},{1,33},{33,1},{2,34},{34,2},{3,35},{35,3},{4,36},{36... | collective-permute-start | bytes 1622024 | tf_op jit(solution)/shard_map/ppermute | solution.py:199
  161.4 3.2 %collective-permute-start.14 = (bf16[512,384]{1,0:T(8,128)(2,1)S(1)}, bf16[512,384]{1,0:T(8,128)(2,1)S(1)}, u32[]{:S(2)}, u32[]{:S(2)}) collective-permute-start(bf16[512,384]{1,0:T(8,128)(2,1)S(1)} %slice.61), channel_id=1, source_target_pairs={{0,24},{8,0},{16,8},{24,16},{1,25},{9,1},{17,9},{25,17},{2,26},{10... | collective-permute-start | bytes 1179656 | tf_op jit(solution)/shard_map/ppermute | solution.py:199
  164.7 0.7 multiply_exponential_fusion
  165.4 6.2 %shard_map.110 = f32[512,512]{1,0:T(8,128)} custom-call(bf16[8,4,512,128]{3,2,1,0:T(8,128)(2,1)} %bitcast.40, bf16[1024,512]{1,0:T(8,128)(2,1)} %bitcast.51, bf16[1024,512]{1,0:T(8,128)(2,1)} %copy-done.5, bf16[1024,512]{1,0:T(8,128)(2,1)} %collective-permute-done.4.refs_2_, bf16[1536,512]{1,0:T(8,128)(2,1)} %copy-done, bf16[1536,512]{1,0:T(8,128)(2,1)} %copy-done.1), custom_call_target="tpu_custom_call" | custom-call | flops 1 | bytes 1 | tf_op jit(solution)/shard_map/pallas_call | solution.py:165
  171.6 2.4 multiply_add_fusion
  173.9 0.7 copy-done.11
  174.7 0.8 copy-done.12
  175.4 6.2 %shard_map.109 = f32[528,384]{1,0:T(8,128)} custom-call(bf16[8,4,512,128]{3,2,1,0:T(8,128)(2,1)} %bitcast.39, bf16[1024,384]{1,0:T(8,128)(2,1)} %bitcast.53, bf16[1024,384]{1,0:T(8,128)(2,1)} %copy-done.6, bf16[1024,384]{1,0:T(8,128)(2,1)} %copy-done.7, bf16[512,384]{1,0:T(8,128)(2,1)} %copy-done.11, bf16[512,384]{1,0:T(8,128)(2,1)} %copy-done.12), custom_call_target="tpu_custom_call" | custom-call | flops 1 | bytes 1 | tf_op jit(solution)/shard_map/pallas_call | solution.py:165
  181.7 1.2 convert_element_type.23
  182.8 0.1 collective-permute-done.12
  183.0 3.6 %all-to-all-start.3 = ((f32[8,64,512]{2,1,0:T(8,128)}), f32[8,64,512]{2,1,0:T(8,128)S(1)}, u32[]{:S(2)}, u32[]{:S(2)}) async-start(f32[8,64,512]{2,1,0:T(8,128)} %bitcast.25), calls=%async_computation.3 | async-start | bytes 2097152 | tf_op jit(solution)/shard_map/all_to_all | solution.py:205
  186.6 3.4 %collective-permute-start.15 = (f16[528,384]{1,0:T(8,128)(2,1)S(1)}, f16[528,384]{1,0:T(8,128)(2,1)S(1)}, u32[]{:S(2)}, u32[]{:S(2)}) collective-permute-start(f16[528,384]{1,0:T(8,128)(2,1)S(1)} %convert_element_type.23), channel_id=1, source_target_pairs={{0,32},{32,0},{1,33},{33,1},{2,34},{34,2},{3,35},{35,3},{4,36},{36... | collective-permute-start | bytes 1216520 | tf_op jit(solution)/shard_map/ppermute | solution.py:199
  189.9 6.1 %shard_map.111.refs_0_ = f32[512,512]{1,0:T(8,128)} custom-call(bf16[8,4,512,128]{3,2,1,0:T(8,128)(2,1)} %bitcast.41, bf16[1024,512]{1,0:T(8,128)(2,1)} %bitcast.45, bf16[1536,512]{1,0:T(8,128)(2,1)} %copy-done, bf16[1536,512]{1,0:T(8,128)(2,1)} %copy-done.1, bf16[512,512]{1,0:T(8,128)(2,1)} %copy-done.9, bf16[512,512]{1,0:T(8,128)(2,1)} %copy-done.10), custom_call_target="tpu_custom_call" | custom-call | flops 1 | bytes 1 | tf_op jit(solution)/shard_map/pallas_call | solution.py:165
  196.0 5.7 %shard_map.112.refs_2_ = f32[512,384]{1,0:T(8,128)} custom-call(bf16[8,4,512,128]{3,2,1,0:T(8,128)(2,1)} %bitcast.42, bf16[1024,384]{1,0:T(8,128)(2,1)} %bitcast.54, bf16[1024,384]{1,0:T(8,128)(2,1)} %copy-done.6, bf16[1024,384]{1,0:T(8,128)(2,1)} %copy-done.7, bf16[512,384]{1,0:T(8,128)(2,1)} %copy-done.11, bf16[512,384]{1,0:T(8,128)(2,1)} %copy-done.12), custom_call_target="tpu_custom_call" | custom-call | flops 1 | bytes 1 | tf_op jit(solution)/shard_map/pallas_call | solution.py:165
  201.8 1.1 convert_element_type.26.refs_1_
  202.9 4.1 %collective-permute-done.15 = f16[528,384]{1,0:T(8,128)(2,1)S(1)} collective-permute-done((f16[528,384]{1,0:T(8,128)(2,1)S(1)}, f16[528,384]{1,0:T(8,128)(2,1)S(1)}, u32[]{:S(2)}, u32[]{:S(2)}) %collective-permute-start.15) | collective-permute-done | bytes 405536 | tf_op jit(solution)/shard_map/ppermute | solution.py:199
  207.0 1.0 convert_element_type.27.refs_3_
  208.0 3.6 %shard_map.113 = f32[512,896]{1,0:T(8,128)} custom-call(f32[512,512]{1,0:T(8,128)} %shard_map.111.refs_0_, f32[528,512]{1,0:T(8,128)} %convert_element_type.26.refs_1_, f32[512,384]{1,0:T(8,128)} %shard_map.112.refs_2_, f32[528,384]{1,0:T(8,128)} %convert_element_type.27.refs_3_), custom_call_target="tpu_custom_call" | custom-call | flops 1 | bytes 1 | tf_op jit(solution)/shard_map/pallas_call | solution.py:85
  211.6 29.2 %all_to_all.26.refs_1_ = f32[8,64,896]{2,1,0:T(8,128)} all-to-all(f32[8,64,896]{2,1,0:T(8,128)} %bitcast.52), channel_id=1, replica_groups=mesh['rep'=4,'zh'=2,'x'=4,'y'=4,'core'=2] {'y','core'}, dimensions={0} | all-to-all | bytes 3670016 | tf_op jit(solution)/shard_map/all_to_all | solution.py:205
  240.8 6.4 %finish.1 = (f32[64,11008]{1,0:T(8,128)}, f32[88,128]{1,0:T(8,128)}) custom-call(f32[8,64]{1,0:T(8,128)} %constant.63.clone.basis_ref, f32[64,8]{1,0:T(8,128)} %constant.64.clone.back_ref, f32[1024,128]{1,0:T(8,128)} %constant.65.clone.wide_ref, f32[128,1024]{1,0:T(8,128)} %constant.66.clone.tall_ref, f32[64,11008]{1,0:T(8,128)} %bitcast.58, ...), custom_call_target="tpu_custom_call" | custom-call | tf_op jit(solution)/shard_map/finish/pallas_call | solution.py:289
  247.2 4.6 %collective-permute-start.16 = (f32[88,128]{1,0:T(8,128)}, f32[88,128]{1,0:T(8,128)S(1)}, u32[]{:S(2)}, u32[]{:S(2)}) collective-permute-start(f32[88,128]{1,0:T(8,128)} %get-tuple-element.116.b0), channel_id=1, source_target_pairs={{0,64},{64,128},{128,192},{192,0},{1,65},{65,129},{129,193},{193,1... | collective-permute-start | bytes 135176 | tf_op jit(solution)/shard_map/band/ppermute | solution.py:199
  251.8 1.8 collective-permute-start.17
  253.6 0.7 collective-permute-done.16.b1
  254.3 2.6 collective-permute-done.17.b2
  257.0 0.9 collective-permute-done.18.b3
  257.9 0.6 copy-done.18
  258.5 3.4 %update.1 = f32[64,11008]{1,0:T(8,128)} custom-call(f32[64,8]{1,0:T(8,128)} %constant.64.clone.back_ref, f32[128,1024]{1,0:T(8,128)} %constant.66.clone.tall_ref, f32[88,128]{1,0:T(8,128)} %get-tuple-element.116.b0, f32[88,128]{1,0:T(8,128)} %copy-done.16, f32[88,128]{1,0:T(8,128)} %copy-done.17, f32[88,128]{1,0:T(8,128)} %copy-done.18), custom_call_target="tpu_custom_call" | custom-call | flops 1 | bytes 1 | tf_op jit(solution)/shard_map/update/pallas_call | solution.py:85
  (63 shorter events, 0.7 us)
Async XLA Ops:
  10.2 12.6 %collective-permute-start.2 = (bf16[1024,128]{1,0:T(8,128)(2,1)}, bf16[1024,128]{1,0:T(8,128)(2,1)S(1)}, u32[]{:S(2)}, u32[]{:S(2)}) collective-permute-start(bf16[1024,128]{1,0:T(8,128)(2,1)} %get-tuple-element.63), channel_id=1, source_target_pairs={{0,16},{8,24},{16,0},{24,8},{1,17},{9,25},{17,1},{25,9},{2,18},{10... | collective-permute-start | bytes 786440 | tf_op jit(solution)/shard_map/ppermute | solution.py:199
  16.1 4.6 %copy-start.20 = (bf16[1024,128]{1,0:T(8,128)(2,1)S(1)}, bf16[1024,128]{1,0:T(8,128)(2,1)}, u32[]{:S(2)}) copy-start(bf16[1024,128]{1,0:T(8,128)(2,1)} %get-tuple-element.62) | copy-start | bytes 786436
  16.1 5.8 %copy-start.19 = (bf16[1024,128]{1,0:T(8,128)(2,1)S(1)}, bf16[1024,128]{1,0:T(8,128)(2,1)}, u32[]{:S(2)}) copy-start(bf16[1024,128]{1,0:T(8,128)(2,1)} %get-tuple-element.61) | copy-start | bytes 786436
  16.1 6.7 %copy-start.15 = (bf16[1024,128]{1,0:T(8,128)(2,1)S(1)}, bf16[1024,128]{1,0:T(8,128)(2,1)}, u32[]{:S(2)}) copy-start(bf16[1024,128]{1,0:T(8,128)(2,1)} %get-tuple-element.60) | copy-start | bytes 786436
  16.1 20.6 %all-to-all-start = ((bf16[8,128,512]{2,1,0:T(8,128)(2,1)}), bf16[8,128,512]{2,1,0:T(8,128)(2,1)S(1)}, u32[]{:S(2)}, u32[]{:S(2)}) async-start(bf16[8,128,512]{2,1,0:T(8,128)(2,1)} %shard_map.104), calls=%async_computation | async-start | bytes 2097152 | tf_op jit(solution)/shard_map/all_to_all | solution.py:205
  20.7 8.7 %collective-permute-start.1 = (bf16[1024,128]{1,0:T(8,128)(2,1)S(1)}, bf16[1024,128]{1,0:T(8,128)(2,1)S(1)}, u32[]{:S(2)}, u32[]{:S(2)}) collective-permute-start(bf16[1024,128]{1,0:T(8,128)(2,1)S(1)} %copy-done.20), channel_id=1, source_target_pairs={{0,24},{8,0},{16,8},{24,16},{1,25},{9,1},{17,9},{25,17},{2,26},{10... | collective-permute-start | bytes 786440 | tf_op jit(solution)/shard_map/ppermute | solution.py:199
  21.9 9.6 %collective-permute-start = (bf16[1024,128]{1,0:T(8,128)(2,1)S(1)}, bf16[1024,128]{1,0:T(8,128)(2,1)S(1)}, u32[]{:S(2)}, u32[]{:S(2)}) collective-permute-start(bf16[1024,128]{1,0:T(8,128)(2,1)S(1)} %copy-done.19), channel_id=1, source_target_pairs={{0,8},{8,16},{16,24},{24,0},{1,9},{9,17},{17,25},{25,1},{2,10},{10... | collective-permute-start | bytes 786440 | tf_op jit(solution)/shard_map/ppermute | solution.py:199
  36.6 6.3 %copy-start.3 = (bf16[8,128,512]{2,1,0:T(8,128)(2,1)}, bf16[8,128,512]{2,1,0:T(8,128)(2,1)S(1)}, u32[]{:S(2)}) copy-start(bf16[8,128,512]{2,1,0:T(8,128)(2,1)S(1)} %all-to-all-done) | copy-start | bytes 3145732
  36.6 25.9 %collective-permute-start.3 = (bf16[1024,512]{1,0:T(8,128)(2,1)S(1)}, bf16[1024,512]{1,0:T(8,128)(2,1)S(1)}, u32[]{:S(2)}, u32[]{:S(2)}) collective-permute-start(bf16[1024,512]{1,0:T(8,128)(2,1)S(1)} %bitcast.48), channel_id=1, source_target_pairs={{0,8},{8,16},{16,24},{24,0},{1,9},{9,17},{17,25},{25,1},{2,10},{10... | collective-permute-start | bytes 3145736 | tf_op jit(solution)/shard_map/ppermute | solution.py:199
  37.2 25.3 %collective-permute-start.4 = (bf16[1024,512]{1,0:T(8,128)(2,1)S(1)}, bf16[1024,512]{1,0:T(8,128)(2,1)}, u32[]{:S(2)}, u32[]{:S(2)}) collective-permute-start(bf16[1024,512]{1,0:T(8,128)(2,1)S(1)} %bitcast.49), channel_id=1, source_target_pairs={{0,24},{8,0},{16,8},{24,16},{1,25},{9,1},{17,9},{25,17},{2,26},{10... | collective-permute-start | bytes 3145736 | tf_op jit(solution)/shard_map/ppermute | solution.py:199
  43.0 19.5 %all-to-all-start.1 = ((bf16[8,128,512]{2,1,0:T(8,128)(2,1)}), bf16[8,128,512]{2,1,0:T(8,128)(2,1)S(1)}, u32[]{:S(2)}, u32[]{:S(2)}) async-start(bf16[8,128,512]{2,1,0:T(8,128)(2,1)} %get-tuple-element.65), calls=%async_computation.1 | async-start | bytes 2097152 | tf_op jit(solution)/shard_map/all_to_all | solution.py:205
  46.5 58.3 %all-gather.5.cloned.1.call-start = ((), (), s32[]{:S(2)}) async-start(), calls=%async_computation.5 | async-start | bytes 4718592 | tf_op jit(solution)/shard_map/all_gather | solution.py:251
  62.4 3.5 %copy-start.2 = (bf16[8,128,512]{2,1,0:T(8,128)(2,1)}, bf16[8,128,512]{2,1,0:T(8,128)(2,1)S(1)}, u32[]{:S(2)}) copy-start(bf16[8,128,512]{2,1,0:T(8,128)(2,1)S(1)} %all-to-all-done.1) | copy-start | bytes 3145732
  62.5 3.4 %copy-start.5 = (bf16[1024,512]{1,0:T(8,128)(2,1)}, bf16[1024,512]{1,0:T(8,128)(2,1)S(1)}, u32[]{:S(2)}) copy-start(bf16[1024,512]{1,0:T(8,128)(2,1)S(1)} %collective-permute-done.3.refs_1_) | copy-start | bytes 3145732
  66.0 89.0 %all-gather.7.cloned.1.call-start = ((), (), s32[]{:S(2)}) async-start(), calls=%async_computation.6 | async-start | bytes 4718592 | tf_op jit(solution)/shard_map/all_gather | solution.py:258
  66.0 37.3 %collective-permute-start.5 = (bf16[1536,512]{1,0:T(8,128)(2,1)}, bf16[1536,512]{1,0:T(8,128)(2,1)S(1)}, u32[]{:S(2)}, u32[]{:S(2)}) collective-permute-start(bf16[1536,512]{1,0:T(8,128)(2,1)} %get-tuple-element.75), channel_id=1, source_target_pairs={{0,8},{8,16},{16,24},{24,0},{1,9},{9,17},{17,25},{25,1},{2,10},{10... | collective-permute-start | bytes 4718600 | tf_op jit(solution)/shard_map/ppermute | solution.py:199
  66.1 37.2 %collective-permute-start.6 = (bf16[1536,512]{1,0:T(8,128)(2,1)}, bf16[1536,512]{1,0:T(8,128)(2,1)S(1)}, u32[]{:S(2)}, u32[]{:S(2)}) collective-permute-start(bf16[1536,512]{1,0:T(8,128)(2,1)} %get-tuple-element.76), channel_id=1, source_target_pairs={{0,24},{8,0},{16,8},{24,16},{1,25},{9,1},{17,9},{25,17},{2,26},{10... | collective-permute-start | bytes 4718600 | tf_op jit(solution)/shard_map/ppermute | solution.py:199
  103.4 6.5 %copy-start = (bf16[1536,512]{1,0:T(8,128)(2,1)}, bf16[1536,512]{1,0:T(8,128)(2,1)S(1)}, u32[]{:S(2)}) copy-start(bf16[1536,512]{1,0:T(8,128)(2,1)S(1)} %collective-permute-done.5.refs_3_.refs_1_) | copy-start | bytes 4718596
  103.4 6.5 %copy-start.1 = (bf16[1536,512]{1,0:T(8,128)(2,1)}, bf16[1536,512]{1,0:T(8,128)(2,1)S(1)}, u32[]{:S(2)}) copy-start(bf16[1536,512]{1,0:T(8,128)(2,1)S(1)} %collective-permute-done.6.refs_4_.refs_2_) | copy-start | bytes 4718596
  106.5 15.6 %copy-start.4 = (bf16[8,128,384]{2,1,0:T(8,128)(2,1)S(1)}, bf16[8,128,384]{2,1,0:T(8,128)(2,1)}, u32[]{:S(2)}) copy-start(bf16[8,128,384]{2,1,0:T(8,128)(2,1)} %all_to_all.25) | copy-start | bytes 2359300
  106.5 15.6 %collective-permute-start.7 = (bf16[512,512]{1,0:T(8,128)(2,1)}, bf16[512,512]{1,0:T(8,128)(2,1)S(1)}, u32[]{:S(2)}, u32[]{:S(2)}) collective-permute-start(bf16[512,512]{1,0:T(8,128)(2,1)} %slice.58), channel_id=1, source_target_pairs={{0,8},{8,16},{16,24},{24,0},{1,9},{9,17},{17,25},{25,1},{2,10},{10... | collective-permute-start | bytes 1572872 | tf_op jit(solution)/shard_map/ppermute | solution.py:199
  106.6 15.5 %collective-permute-start.8 = (bf16[512,512]{1,0:T(8,128)(2,1)}, bf16[512,512]{1,0:T(8,128)(2,1)S(1)}, u32[]{:S(2)}, u32[]{:S(2)}) collective-permute-start(bf16[512,512]{1,0:T(8,128)(2,1)} %slice.59), channel_id=1, source_target_pairs={{0,24},{8,0},{16,8},{24,16},{1,25},{9,1},{17,9},{25,17},{2,26},{10... | collective-permute-start | bytes 1572872 | tf_op jit(solution)/shard_map/ppermute | solution.py:199
  122.1 9.6 %copy-start.9 = (bf16[512,512]{1,0:T(8,128)(2,1)}, bf16[512,512]{1,0:T(8,128)(2,1)S(1)}, u32[]{:S(2)}) copy-start(bf16[512,512]{1,0:T(8,128)(2,1)S(1)} %collective-permute-done.7.refs_3_) | copy-start | bytes 1572868
  122.1 9.6 %copy-start.10 = (bf16[512,512]{1,0:T(8,128)(2,1)}, bf16[512,512]{1,0:T(8,128)(2,1)S(1)}, u32[]{:S(2)}) copy-start(bf16[512,512]{1,0:T(8,128)(2,1)S(1)} %collective-permute-done.8.refs_4_) | copy-start | bytes 1572868
  122.1 32.8 %collective-permute-start.9 = (bf16[1024,384]{1,0:T(8,128)(2,1)S(1)}, bf16[1024,384]{1,0:T(8,128)(2,1)S(1)}, u32[]{:S(2)}, u32[]{:S(2)}) collective-permute-start(bf16[1024,384]{1,0:T(8,128)(2,1)S(1)} %bitcast.55), channel_id=1, source_target_pairs={{0,8},{8,16},{16,24},{24,0},{1,9},{9,17},{17,25},{25,1},{2,10},{10... | collective-permute-start | bytes 2359304 | tf_op jit(solution)/shard_map/ppermute | solution.py:199
  122.2 32.7 %collective-permute-start.10 = (bf16[1024,384]{1,0:T(8,128)(2,1)S(1)}, bf16[1024,384]{1,0:T(8,128)(2,1)S(1)}, u32[]{:S(2)}, u32[]{:S(2)}) collective-permute-start(bf16[1024,384]{1,0:T(8,128)(2,1)S(1)} %bitcast.56), channel_id=1, source_target_pairs={{0,24},{8,0},{16,8},{24,16},{1,25},{9,1},{17,9},{25,17},{2,26},{10... | collective-permute-start | bytes 2359304 | tf_op jit(solution)/shard_map/ppermute | solution.py:199
  125.4 29.5 %collective-permute-start.11 = (f16[528,512]{1,0:T(8,128)(2,1)S(1)}, f16[528,512]{1,0:T(8,128)(2,1)S(1)}, u32[]{:S(2)}, u32[]{:S(2)}) collective-permute-start(f16[528,512]{1,0:T(8,128)(2,1)S(1)} %convert_element_type.21), channel_id=1, source_target_pairs={{0,32},{32,0},{1,33},{33,1},{2,34},{34,2},{3,35},{35,3},{4,36},{36... | collective-permute-start | bytes 1622024 | tf_op jit(solution)/shard_map/ppermute | solution.py:199
  154.9 0.8 copy-start.13
  154.9 16.6 %copy-start.6 = (bf16[1024,384]{1,0:T(8,128)(2,1)}, bf16[1024,384]{1,0:T(8,128)(2,1)S(1)}, u32[]{:S(2)}) copy-start(bf16[1024,384]{1,0:T(8,128)(2,1)S(1)} %collective-permute-done.9.refs_1_) | copy-start | bytes 2359300
  154.9 16.6 %copy-start.7 = (bf16[1024,384]{1,0:T(8,128)(2,1)}, bf16[1024,384]{1,0:T(8,128)(2,1)S(1)}, u32[]{:S(2)}) copy-start(bf16[1024,384]{1,0:T(8,128)(2,1)S(1)} %collective-permute-done.10.refs_2_) | copy-start | bytes 2359300
  155.8 27.2 %collective-permute-start.12 = (f16[528,512]{1,0:T(8,128)(2,1)S(1)}, f16[528,512]{1,0:T(8,128)(2,1)S(1)}, u32[]{:S(2)}, u32[]{:S(2)}) collective-permute-start(f16[528,512]{1,0:T(8,128)(2,1)S(1)} %convert_element_type.22), channel_id=1, source_target_pairs={{0,32},{32,0},{1,33},{33,1},{2,34},{34,2},{3,35},{35,3},{4,36},{36... | collective-permute-start | bytes 1622024 | tf_op jit(solution)/shard_map/ppermute | solution.py:199
  161.4 12.5 %collective-permute-start.13 = (bf16[512,384]{1,0:T(8,128)(2,1)S(1)}, bf16[512,384]{1,0:T(8,128)(2,1)S(1)}, u32[]{:S(2)}, u32[]{:S(2)}) collective-permute-start(bf16[512,384]{1,0:T(8,128)(2,1)S(1)} %slice.60), channel_id=1, source_target_pairs={{0,8},{8,16},{16,24},{24,0},{1,9},{9,17},{17,25},{25,1},{2,10},{10... | collective-permute-start | bytes 1179656 | tf_op jit(solution)/shard_map/ppermute | solution.py:199
  161.4 12.5 %collective-permute-start.14 = (bf16[512,384]{1,0:T(8,128)(2,1)S(1)}, bf16[512,384]{1,0:T(8,128)(2,1)S(1)}, u32[]{:S(2)}, u32[]{:S(2)}) collective-permute-start(bf16[512,384]{1,0:T(8,128)(2,1)S(1)} %slice.61), channel_id=1, source_target_pairs={{0,24},{8,0},{16,8},{24,16},{1,25},{9,1},{17,9},{25,17},{2,26},{10... | collective-permute-start | bytes 1179656 | tf_op jit(solution)/shard_map/ppermute | solution.py:199
  165.4 6.2 %copy-start.14 = (f16[528,512]{1,0:T(8,128)(2,1)S(1)}, f16[528,512]{1,0:T(8,128)(2,1)}, u32[]{:S(2)}) copy-start(f16[528,512]{1,0:T(8,128)(2,1)} %copy-done.13) | copy-start | bytes 1622020
  173.9 0.7 copy-start.11
  174.7 0.8 copy-start.12
  183.0 24.0 %all-to-all-start.3 = ((f32[8,64,512]{2,1,0:T(8,128)}), f32[8,64,512]{2,1,0:T(8,128)S(1)}, u32[]{:S(2)}, u32[]{:S(2)}) async-start(f32[8,64,512]{2,1,0:T(8,128)} %bitcast.25), calls=%async_computation.3 | async-start | bytes 2097152 | tf_op jit(solution)/shard_map/all_to_all | solution.py:205
  186.6 20.4 %collective-permute-start.15 = (f16[528,384]{1,0:T(8,128)(2,1)S(1)}, f16[528,384]{1,0:T(8,128)(2,1)S(1)}, u32[]{:S(2)}, u32[]{:S(2)}) collective-permute-start(f16[528,384]{1,0:T(8,128)(2,1)S(1)} %convert_element_type.23), channel_id=1, source_target_pairs={{0,32},{32,0},{1,33},{33,1},{2,34},{34,2},{3,35},{35,3},{4,36},{36... | collective-permute-start | bytes 1216520 | tf_op jit(solution)/shard_map/ppermute | solution.py:199
  207.0 4.6 %copy-start.8 = (f32[8,64,512]{2,1,0:T(8,128)}, f32[8,64,512]{2,1,0:T(8,128)S(1)}, u32[]{:S(2)}) copy-start(f32[8,64,512]{2,1,0:T(8,128)S(1)} %all-to-all-done.3.refs_0_) | copy-start | bytes 3145732
  247.2 7.1 %collective-permute-start.16 = (f32[88,128]{1,0:T(8,128)}, f32[88,128]{1,0:T(8,128)S(1)}, u32[]{:S(2)}, u32[]{:S(2)}) collective-permute-start(f32[88,128]{1,0:T(8,128)} %get-tuple-element.116.b0), channel_id=1, source_target_pairs={{0,64},{64,128},{128,192},{192,0},{1,65},{65,129},{129,193},{193,1... | collective-permute-start | bytes 135176 | tf_op jit(solution)/shard_map/band/ppermute | solution.py:199
  251.8 5.2 %collective-permute-start.17 = (f32[88,128]{1,0:T(8,128)}, f32[88,128]{1,0:T(8,128)S(1)}, u32[]{:S(2)}, u32[]{:S(2)}) collective-permute-start(f32[88,128]{1,0:T(8,128)} %get-tuple-element.116.b0), channel_id=1, source_target_pairs={{0,128},{64,192},{128,0},{192,64},{1,129},{65,193},{129,1},{193,65... | collective-permute-start | bytes 135176 | tf_op jit(solution)/shard_map/band/ppermute | solution.py:199
  253.6 4.3 %collective-permute-start.18 = (f32[88,128]{1,0:T(8,128)}, f32[88,128]{1,0:T(8,128)S(1)}, u32[]{:S(2)}, u32[]{:S(2)}) collective-permute-start(f32[88,128]{1,0:T(8,128)} %get-tuple-element.116.b0), channel_id=1, source_target_pairs={{0,192},{64,0},{128,64},{192,128},{1,193},{65,1},{129,65},{193,129... | collective-permute-start | bytes 135176 | tf_op jit(solution)/shard_map/band/ppermute | solution.py:199
  254.3 3.5 %copy-start.16 = (f32[88,128]{1,0:T(8,128)}, f32[88,128]{1,0:T(8,128)S(1)}, u32[]{:S(2)}) copy-start(f32[88,128]{1,0:T(8,128)S(1)} %collective-permute-done.16.b1) | copy-start | bytes 135172
  257.0 0.9 copy-start.17
  257.9 0.6 copy-start.18
Sparse Core Ops, SparseCore 0:
  66.1 38.6 all-gather.4
  106.7 33.9 all-gather.6

commit v3 on v2

--- a/solution.py
+++ b/solution.py
@@ -254,11 +254,11 @@
     half1 = halves(r1, l1)
     half1, r1, l1, v2, sent, kept = sync(half1, r1, l1, v2, sent, kept)
     far1 = along("x", 1, half1[0]), along("x", 3, half1[1])
+    r2, l2 = ring(v2)
     send0 = payload(sent, [v0, r0, l0, r1, l1])
     kept = lax.all_gather(kept, ("y", "core"))
 
-    far1, send0, v2, sent = sync(far1, send0, v2, sent)
-    r2, l2 = ring(v2)
+    send0, sent = sync(send0, sent)
     got0 = along("zh", 1, send0)
     send1 = payload(sent, [v1, r1, l1, *far1])
 

time: 270 us -> 268 us (level)
  waiting for transfers between devices: 68.2 us -> 62.2 us
  local copies, waits for them, and re-layouts: 7.53 us -> 11 us
    ppermute x19, waiting for transfers between devices: 49 us -> 43 us  [along(): lax.ppermute(value, axis, shift(2 if axis in ('core', 'zh') else 4, by))]
  transfers between devices with their start and end apart: 24 -> 24, of which waited for: 14 -> 12; matrix products, arithmetic and copies ran while one was open for 4% -> 4% of each run, Pallas kernels for 16% -> 16%
where the time goes in v3:
time: 268 us; the launch traced here: 267 us
  waiting for transfers between devices  62.2 us (23%)
  Pallas kernels  59 us (22%)
  starting transfers between devices  56.5 us (21%)
  blocking collectives  50.8 us (19%)
  between operations  14.3 us (5%)
  other arithmetic  12.9 us (5%)
  local copies, waits for them, and re-layouts  11 us (4%)
    all_to_all x2, blocking collectives, swap(): return lax.all_to_all(value, ('y', 'core'), 0, 0, tiled=True)  50.8 us
    ppermute x19, starting transfers between devices, along(): lax.ppermute(value, axis, shift(2 if axis in ('core', 'zh') else 4, by))  44.7 us
    ppermute x19, waiting for transfers between devices, along(): lax.ppermute(value, axis, shift(2 if axis in ('core', 'zh') else 4, by))  43 us
    pallas_call x6, Pallas kernels, tile(): pl.pallas_call(kernel, grid=(half // rows,), out_shape=jax.ShapeDtypeStru...  37.4 us
    all_to_all x3, waiting for transfers between devices, swap(): return lax.all_to_all(value, ('y', 'core'), 0, 0, tiled=True)  17.7 us
    pallas_call x5, Pallas kernels, call(): pl.pallas_call(kernel, out_shape=shapes, in_specs=spec or [VMEM] * len(ar...  15.3 us
    all_to_all x3, starting transfers between devices, swap(): return lax.all_to_all(value, ('y', 'core'), 0, 0, tiled=True)  11.7 us
    pallas_call x1, Pallas kernels, on_device(): pl.pallas_call(functools.partial(finish_kernel, [d.shape[2] for d in done...  6.38 us
  transfers between devices with their start and end apart: 24, of which 12 were waited for; matrix products, arithmetic and copies ran while one was open for 4% of the time, Pallas kernels for 16%

profile of v3, /device:TPU:32, one launch (start us, length us, event | category | flops | bytes accessed | tf_op | source)
XLA Modules:
  0.0 266.8 jit_solution(10243357550629350099)
XLA Ops:
  7.2 0.7 stack.65.at_ref
  7.9 2.3 shard_map.105
  10.2 3.0 %collective-permute-start.2 = (bf16[1024,128]{1,0:T(8,128)(2,1)}, bf16[1024,128]{1,0:T(8,128)(2,1)S(1)}, u32[]{:S(2)}, u32[]{:S(2)}) collective-permute-start(bf16[1024,128]{1,0:T(8,128)(2,1)} %get-tuple-element.60), channel_id=1, source_target_pairs={{0,16},{8,24},{16,0},{24,8},{1,17},{9,25},{17,1},{25,9},{2,18},{10... | collective-permute-start | bytes 786440 | tf_op jit(solution)/shard_map/ppermute | solution.py:199
  13.2 2.8 %shard_map.104 = bf16[8,128,512]{2,1,0:T(8,128)(2,1)} custom-call(bf16[128,11008]{1,0:T(8,128)(2,1)} %bitcast.46), custom_call_target="tpu_custom_call" | custom-call | flops 1 | bytes 1 | tf_op jit(solution)/shard_map/pallas_call | solution.py:85
  16.1 4.6 %all-to-all-start = ((bf16[8,128,512]{2,1,0:T(8,128)(2,1)}), bf16[8,128,512]{2,1,0:T(8,128)(2,1)S(1)}, u32[]{:S(2)}, u32[]{:S(2)}) async-start(bf16[8,128,512]{2,1,0:T(8,128)(2,1)} %shard_map.104), calls=%async_computation | async-start | bytes 2097152 | tf_op jit(solution)/shard_map/all_to_all | solution.py:205
  20.7 1.2 collective-permute-start.1
  21.9 0.9 collective-permute-start
  22.8 6.6 %collective-permute-done.1 = bf16[1024,128]{1,0:T(8,128)(2,1)S(1)} collective-permute-done((bf16[1024,128]{1,0:T(8,128)(2,1)S(1)}, bf16[1024,128]{1,0:T(8,128)(2,1)S(1)}, u32[]{:S(2)}, u32[]{:S(2)}) %collective-permute-start.1) | collective-permute-done | bytes 262176 | tf_op jit(solution)/shard_map/ppermute | solution.py:199
  29.4 2.1 collective-permute-done
  31.5 0.7 slice_bitcast_fusion.2
  32.1 0.9 pad_maximum_fusion.2
  33.0 3.6 %all-to-all-done = bf16[8,128,512]{2,1,0:T(8,128)(2,1)S(1)} async-done(((bf16[8,128,512]{2,1,0:T(8,128)(2,1)}), bf16[8,128,512]{2,1,0:T(8,128)(2,1)S(1)}, u32[]{:S(2)}, u32[]{:S(2)}) %all-to-all-start) | async-done | bytes 1048608 | tf_op jit(solution)/shard_map/all_to_all | solution.py:205
  36.6 0.6 collective-permute-start.3
  37.2 2.6 collective-permute-start.4
  39.9 3.1 %shard_map.106 = (bf16[8,128,512]{2,1,0:T(8,128)(2,1)}, bf16[8,128,384]{2,1,0:T(8,128)(2,1)}) custom-call(bf16[128,11008]{1,0:T(8,128)(2,1)} %bitcast.47), custom_call_target="tpu_custom_call" | custom-call | flops 1 | bytes 1 | tf_op jit(solution)/shard_map/pallas_call | solution.py:85
  43.0 3.6 %all-to-all-start.1 = ((bf16[8,128,512]{2,1,0:T(8,128)(2,1)}), bf16[8,128,512]{2,1,0:T(8,128)(2,1)S(1)}, u32[]{:S(2)}, u32[]{:S(2)}) async-start(bf16[8,128,512]{2,1,0:T(8,128)(2,1)} %get-tuple-element.62), calls=%async_computation.1 | async-start | bytes 2097152 | tf_op jit(solution)/shard_map/all_to_all | solution.py:205
  46.6 1.8 pad_maximum_fusion.3
  48.4 14.1 %all-to-all-done.1 = bf16[8,128,512]{2,1,0:T(8,128)(2,1)S(1)} async-done(((bf16[8,128,512]{2,1,0:T(8,128)(2,1)}), bf16[8,128,512]{2,1,0:T(8,128)(2,1)S(1)}, u32[]{:S(2)}, u32[]{:S(2)}) %all-to-all-start.1) | async-done | bytes 1048608 | tf_op jit(solution)/shard_map/all_to_all | solution.py:205
  62.6 1.5 slice.57
  64.1 1.9 pad_maximum_fusion
  66.1 3.2 %collective-permute-start.6 = (bf16[1536,512]{1,0:T(8,128)(2,1)}, bf16[1536,512]{1,0:T(8,128)(2,1)S(1)}, u32[]{:S(2)}, u32[]{:S(2)}) collective-permute-start(bf16[1536,512]{1,0:T(8,128)(2,1)} %get-tuple-element.73), channel_id=1, source_target_pairs={{0,24},{8,0},{16,8},{24,16},{1,25},{9,1},{17,9},{25,17},{2,26},{10... | collective-permute-start | bytes 4718600 | tf_op jit(solution)/shard_map/ppermute | solution.py:199
  69.4 21.6 %all_to_all.25 = bf16[8,128,384]{2,1,0:T(8,128)(2,1)} all-to-all(bf16[8,128,384]{2,1,0:T(8,128)(2,1)} %get-tuple-element.74), channel_id=1, replica_groups=mesh['rep'=4,'zh'=2,'x'=4,'y'=4,'core'=2] {'y','core'}, dimensions={0} | all-to-all | bytes 1572864 | tf_op jit(solution)/shard_map/all_to_all | solution.py:205
  90.9 12.4 %collective-permute-done.5.refs_3_.refs_1_ = bf16[1536,512]{1,0:T(8,128)(2,1)S(1)} collective-permute-done((bf16[1536,512]{1,0:T(8,128)(2,1)}, bf16[1536,512]{1,0:T(8,128)(2,1)S(1)}, u32[]{:S(2)}, u32[]{:S(2)}) %collective-permute-start.5) | collective-permute-done | bytes 1572896 | tf_op jit(solution)/shard_map/ppermute | solution.py:199
  103.4 1.5 all-gather.5.cloned.1.call-done
  104.8 0.8 slice.58
  105.6 0.9 slice.59
  106.7 3.2 %collective-permute-start.8 = (bf16[1024,384]{1,0:T(8,128)(2,1)}, bf16[1024,384]{1,0:T(8,128)(2,1)}, u32[]{:S(2)}, u32[]{:S(2)}) collective-permute-start(bf16[1024,384]{1,0:T(8,128)(2,1)} %bitcast.54), channel_id=1, source_target_pairs={{0,24},{8,0},{16,8},{24,16},{1,25},{9,1},{17,9},{25,17},{2,26},{10... | collective-permute-start | bytes 2359304 | tf_op jit(solution)/shard_map/ppermute | solution.py:199
  109.9 6.6 %shard_map.107 = f32[528,512]{1,0:T(8,128)} custom-call(bf16[8,4,512,128]{3,2,1,0:T(8,128)(2,1)} %bitcast.37, bf16[1024,512]{1,0:T(8,128)(2,1)} %bitcast.50, bf16[1024,512]{1,0:T(8,128)(2,1)} %copy-done.4, bf16[1024,512]{1,0:T(8,128)(2,1)} %collective-permute-done.4.refs_2_, bf16[1536,512]{1,0:T(8,128)(2,1)} %copy-done, bf16[1536,512]{1,0:T(8,128)(2,1)} %copy-done.1), custom_call_target="tpu_custom_call" | custom-call | flops 1 | bytes 1 | tf_op jit(solution)/shard_map/pallas_call | solution.py:165
  116.5 1.4 convert_element_type.21
  117.9 6.4 %collective-permute-start.9 = (f16[528,512]{1,0:T(8,128)(2,1)S(1)}, f16[528,512]{1,0:T(8,128)(2,1)S(1)}, u32[]{:S(2)}, u32[]{:S(2)}) collective-permute-start(f16[528,512]{1,0:T(8,128)(2,1)S(1)} %convert_element_type.21), channel_id=1, source_target_pairs={{0,32},{32,0},{1,33},{33,1},{2,34},{34,2},{3,35},{35,3},{4,36},{36... | collective-permute-start | bytes 1622024 | tf_op jit(solution)/shard_map/ppermute | solution.py:199
  124.3 3.2 %collective-permute-start.11 = (bf16[512,512]{1,0:T(8,128)(2,1)S(1)}, bf16[512,512]{1,0:T(8,128)(2,1)S(1)}, u32[]{:S(2)}, u32[]{:S(2)}) collective-permute-start(bf16[512,512]{1,0:T(8,128)(2,1)S(1)} %copy-done.10), channel_id=1, source_target_pairs={{0,24},{8,0},{16,8},{24,16},{1,25},{9,1},{17,9},{25,17},{2,26},{10... | collective-permute-start | bytes 1572872 | tf_op jit(solution)/shard_map/ppermute | solution.py:199
  127.5 11.5 %collective-permute-done.10.refs_3_ = bf16[512,512]{1,0:T(8,128)(2,1)S(1)} collective-permute-done((bf16[512,512]{1,0:T(8,128)(2,1)S(1)}, bf16[512,512]{1,0:T(8,128)(2,1)S(1)}, u32[]{:S(2)}, u32[]{:S(2)}) %collective-permute-start.10) | collective-permute-done | bytes 524320 | tf_op jit(solution)/shard_map/ppermute | solution.py:199
  139.0 0.8 copy-done.6
  139.8 0.8 copy-done.7
  140.6 6.6 %shard_map.108 = f32[528,512]{1,0:T(8,128)} custom-call(bf16[8,4,512,128]{3,2,1,0:T(8,128)(2,1)} %bitcast.38, bf16[1024,512]{1,0:T(8,128)(2,1)} %bitcast.44, bf16[1536,512]{1,0:T(8,128)(2,1)} %copy-done, bf16[1536,512]{1,0:T(8,128)(2,1)} %copy-done.1, bf16[512,512]{1,0:T(8,128)(2,1)} %copy-done.6, bf16[512,512]{1,0:T(8,128)(2,1)} %copy-done.7), custom_call_target="tpu_custom_call" | custom-call | flops 1 | bytes 1 | tf_op jit(solution)/shard_map/pallas_call | solution.py:165
  147.2 1.3 convert_element_type.22
  148.6 1.0 slice.60
  149.7 1.0 slice.61
  150.7 6.4 %collective-permute-start.12 = (f16[528,512]{1,0:T(8,128)(2,1)S(1)}, f16[528,512]{1,0:T(8,128)(2,1)S(1)}, u32[]{:S(2)}, u32[]{:S(2)}) collective-permute-start(f16[528,512]{1,0:T(8,128)(2,1)S(1)} %convert_element_type.22), channel_id=1, source_target_pairs={{0,32},{32,0},{1,33},{33,1},{2,34},{34,2},{3,35},{35,3},{4,36},{36... | collective-permute-start | bytes 1622024 | tf_op jit(solution)/shard_map/ppermute | solution.py:199
  157.1 3.2 %collective-permute-start.14 = (bf16[512,384]{1,0:T(8,128)(2,1)S(1)}, bf16[512,384]{1,0:T(8,128)(2,1)S(1)}, u32[]{:S(2)}, u32[]{:S(2)}) collective-permute-start(bf16[512,384]{1,0:T(8,128)(2,1)S(1)} %slice.61), channel_id=1, source_target_pairs={{0,24},{8,0},{16,8},{24,16},{1,25},{9,1},{17,9},{25,17},{2,26},{10... | collective-permute-start | bytes 1179656 | tf_op jit(solution)/shard_map/ppermute | solution.py:199
  160.3 6.1 %shard_map.110 = f32[512,512]{1,0:T(8,128)} custom-call(bf16[8,4,512,128]{3,2,1,0:T(8,128)(2,1)} %bitcast.40, bf16[1024,512]{1,0:T(8,128)(2,1)} %bitcast.51, bf16[1024,512]{1,0:T(8,128)(2,1)} %copy-done.4, bf16[1024,512]{1,0:T(8,128)(2,1)} %collective-permute-done.4.refs_2_, bf16[1536,512]{1,0:T(8,128)(2,1)} %copy-done, bf16[1536,512]{1,0:T(8,128)(2,1)} %copy-done.1), custom_call_target="tpu_custom_call" | custom-call | flops 1 | bytes 1 | tf_op jit(solution)/shard_map/pallas_call | solution.py:165
  166.4 2.4 multiply_add_fusion
  168.8 0.7 copy-done.8
  169.6 0.7 copy-done.9
  170.3 6.2 %shard_map.109 = f32[528,384]{1,0:T(8,128)} custom-call(bf16[8,4,512,128]{3,2,1,0:T(8,128)(2,1)} %bitcast.39, bf16[1024,384]{1,0:T(8,128)(2,1)} %bitcast.55, bf16[1024,384]{1,0:T(8,128)(2,1)} %collective-permute-done.7.refs_1_, bf16[1024,384]{1,0:T(8,128)(2,1)} %collective-permute-done.8.refs_2_, bf16[512,384]{1,0:T(8,128)(2,1)} %copy-done.8, ...), custom_call_target="tpu_custom_call" | custom-call | flops 1 | bytes 1 | tf_op jit(solution)/shard_map/pallas_call | solution.py:165
  176.5 1.2 convert_element_type.23
  177.7 3.0 %collective-permute-done.12 = f16[528,512]{1,0:T(8,128)(2,1)S(1)} collective-permute-done((f16[528,512]{1,0:T(8,128)(2,1)S(1)}, f16[528,512]{1,0:T(8,128)(2,1)S(1)}, u32[]{:S(2)}, u32[]{:S(2)}) %collective-permute-start.12) | collective-permute-done | bytes 540704 | tf_op jit(solution)/shard_map/ppermute | solution.py:199
  180.7 3.6 %all-to-all-start.3 = ((f32[8,64,512]{2,1,0:T(8,128)}), f32[8,64,512]{2,1,0:T(8,128)S(1)}, u32[]{:S(2)}, u32[]{:S(2)}) async-start(f32[8,64,512]{2,1,0:T(8,128)} %bitcast.25), calls=%async_computation.3 | async-start | bytes 2097152 | tf_op jit(solution)/shard_map/all_to_all | solution.py:205
  184.2 5.6 %collective-permute-start.15 = (f16[528,384]{1,0:T(8,128)(2,1)S(1)}, f16[528,384]{1,0:T(8,128)(2,1)S(1)}, u32[]{:S(2)}, u32[]{:S(2)}) collective-permute-start(f16[528,384]{1,0:T(8,128)(2,1)S(1)} %convert_element_type.23), channel_id=1, source_target_pairs={{0,32},{32,0},{1,33},{33,1},{2,34},{34,2},{3,35},{35,3},{4,36},{36... | collective-permute-start | bytes 1216520 | tf_op jit(solution)/shard_map/ppermute | solution.py:199
  189.8 6.1 %shard_map.111.refs_0_ = f32[512,512]{1,0:T(8,128)} custom-call(bf16[8,4,512,128]{3,2,1,0:T(8,128)(2,1)} %bitcast.41, bf16[1024,512]{1,0:T(8,128)(2,1)} %bitcast.45, bf16[1536,512]{1,0:T(8,128)(2,1)} %copy-done, bf16[1536,512]{1,0:T(8,128)(2,1)} %copy-done.1, bf16[512,512]{1,0:T(8,128)(2,1)} %copy-done.6, bf16[512,512]{1,0:T(8,128)(2,1)} %copy-done.7), custom_call_target="tpu_custom_call" | custom-call | flops 1 | bytes 1 | tf_op jit(solution)/shard_map/pallas_call | solution.py:165
  195.9 5.8 %shard_map.112.refs_2_ = f32[512,384]{1,0:T(8,128)} custom-call(bf16[8,4,512,128]{3,2,1,0:T(8,128)(2,1)} %bitcast.42, bf16[1024,384]{1,0:T(8,128)(2,1)} %bitcast.56, bf16[1024,384]{1,0:T(8,128)(2,1)} %collective-permute-done.7.refs_1_, bf16[1024,384]{1,0:T(8,128)(2,1)} %collective-permute-done.8.refs_2_, bf16[512,384]{1,0:T(8,128)(2,1)} %copy-done.8, ...), custom_call_target="tpu_custom_call" | custom-call | flops 1 | bytes 1 | tf_op jit(solution)/shard_map/pallas_call | solution.py:165
  201.7 1.1 convert_element_type.26.refs_1_
  202.8 3.7 %collective-permute-done.15 = f16[528,384]{1,0:T(8,128)(2,1)S(1)} collective-permute-done((f16[528,384]{1,0:T(8,128)(2,1)S(1)}, f16[528,384]{1,0:T(8,128)(2,1)S(1)}, u32[]{:S(2)}, u32[]{:S(2)}) %collective-permute-start.15) | collective-permute-done | bytes 405536 | tf_op jit(solution)/shard_map/ppermute | solution.py:199
  206.5 1.0 convert_element_type.27.refs_3_
  207.5 3.6 %shard_map.113 = f32[512,896]{1,0:T(8,128)} custom-call(f32[512,512]{1,0:T(8,128)} %shard_map.111.refs_0_, f32[528,512]{1,0:T(8,128)} %convert_element_type.26.refs_1_, f32[512,384]{1,0:T(8,128)} %shard_map.112.refs_2_, f32[528,384]{1,0:T(8,128)} %convert_element_type.27.refs_3_), custom_call_target="tpu_custom_call" | custom-call | flops 1 | bytes 1 | tf_op jit(solution)/shard_map/pallas_call | solution.py:85
  211.1 29.2 %all_to_all.26.refs_1_ = f32[8,64,896]{2,1,0:T(8,128)} all-to-all(f32[8,64,896]{2,1,0:T(8,128)} %bitcast.52), channel_id=1, replica_groups=mesh['rep'=4,'zh'=2,'x'=4,'y'=4,'core'=2] {'y','core'}, dimensions={0} | all-to-all | bytes 3670016 | tf_op jit(solution)/shard_map/all_to_all | solution.py:205
  240.3 6.4 %finish.1 = (f32[64,11008]{1,0:T(8,128)}, f32[88,128]{1,0:T(8,128)}) custom-call(f32[8,64]{1,0:T(8,128)} %constant.63.clone.basis_ref, f32[64,8]{1,0:T(8,128)} %constant.64.clone.back_ref, f32[1024,128]{1,0:T(8,128)} %constant.65.clone.wide_ref, f32[128,1024]{1,0:T(8,128)} %constant.66.clone.tall_ref, f32[64,11008]{1,0:T(8,128)} %bitcast.58, ...), custom_call_target="tpu_custom_call" | custom-call | tf_op jit(solution)/shard_map/finish/pallas_call | solution.py:289
  246.7 3.5 %collective-permute-start.16 = (f32[88,128]{1,0:T(8,128)}, f32[88,128]{1,0:T(8,128)S(1)}, u32[]{:S(2)}, u32[]{:S(2)}) collective-permute-start(f32[88,128]{1,0:T(8,128)} %get-tuple-element.110.b0), channel_id=1, source_target_pairs={{0,64},{64,128},{128,192},{192,0},{1,65},{65,129},{129,193},{193,1... | collective-permute-start | bytes 135176 | tf_op jit(solution)/shard_map/band/ppermute | solution.py:199
  250.2 1.5 collective-permute-start.18
  251.6 0.6 collective-permute-done.16.b1
  252.2 3.1 %collective-permute-done.17.b2 = f32[88,128]{1,0:T(8,128)S(1)} collective-permute-done((f32[88,128]{1,0:T(8,128)}, f32[88,128]{1,0:T(8,128)S(1)}, u32[]{:S(2)}, u32[]{:S(2)}) %collective-permute-start.17) | collective-permute-done | bytes 45088 | tf_op jit(solution)/shard_map/band/ppermute | solution.py:199
  255.3 0.6 copy-done.14
  255.9 0.6 copy-done.15
  256.5 3.4 %update.1 = f32[64,11008]{1,0:T(8,128)} custom-call(f32[64,8]{1,0:T(8,128)} %constant.64.clone.back_ref, f32[128,1024]{1,0:T(8,128)} %constant.66.clone.tall_ref, f32[88,128]{1,0:T(8,128)} %get-tuple-element.110.b0, f32[88,128]{1,0:T(8,128)} %copy-done.13, f32[88,128]{1,0:T(8,128)} %copy-done.14, f32[88,128]{1,0:T(8,128)} %copy-done.15), custom_call_target="tpu_custom_call" | custom-call | flops 1 | bytes 1 | tf_op jit(solution)/shard_map/update/pallas_call | solution.py:85
  (57 shorter events, 0.6 us)
Async XLA Ops:
  10.2 12.6 %collective-permute-start.2 = (bf16[1024,128]{1,0:T(8,128)(2,1)}, bf16[1024,128]{1,0:T(8,128)(2,1)S(1)}, u32[]{:S(2)}, u32[]{:S(2)}) collective-permute-start(bf16[1024,128]{1,0:T(8,128)(2,1)} %get-tuple-element.60), channel_id=1, source_target_pairs={{0,16},{8,24},{16,0},{24,8},{1,17},{9,25},{17,1},{25,9},{2,18},{10... | collective-permute-start | bytes 786440 | tf_op jit(solution)/shard_map/ppermute | solution.py:199
  16.1 4.6 %copy-start.17 = (bf16[1024,128]{1,0:T(8,128)(2,1)S(1)}, bf16[1024,128]{1,0:T(8,128)(2,1)}, u32[]{:S(2)}) copy-start(bf16[1024,128]{1,0:T(8,128)(2,1)} %get-tuple-element.59) | copy-start | bytes 786436
  16.1 5.8 %copy-start.16 = (bf16[1024,128]{1,0:T(8,128)(2,1)S(1)}, bf16[1024,128]{1,0:T(8,128)(2,1)}, u32[]{:S(2)}) copy-start(bf16[1024,128]{1,0:T(8,128)(2,1)} %get-tuple-element.58) | copy-start | bytes 786436
  16.1 6.7 %copy-start.12 = (bf16[1024,128]{1,0:T(8,128)(2,1)S(1)}, bf16[1024,128]{1,0:T(8,128)(2,1)}, u32[]{:S(2)}) copy-start(bf16[1024,128]{1,0:T(8,128)(2,1)} %get-tuple-element.57) | copy-start | bytes 786436
  16.1 20.6 %all-to-all-start = ((bf16[8,128,512]{2,1,0:T(8,128)(2,1)}), bf16[8,128,512]{2,1,0:T(8,128)(2,1)S(1)}, u32[]{:S(2)}, u32[]{:S(2)}) async-start(bf16[8,128,512]{2,1,0:T(8,128)(2,1)} %shard_map.104), calls=%async_computation | async-start | bytes 2097152 | tf_op jit(solution)/shard_map/all_to_all | solution.py:205
  20.7 8.7 %collective-permute-start.1 = (bf16[1024,128]{1,0:T(8,128)(2,1)S(1)}, bf16[1024,128]{1,0:T(8,128)(2,1)S(1)}, u32[]{:S(2)}, u32[]{:S(2)}) collective-permute-start(bf16[1024,128]{1,0:T(8,128)(2,1)S(1)} %copy-done.17), channel_id=1, source_target_pairs={{0,24},{8,0},{16,8},{24,16},{1,25},{9,1},{17,9},{25,17},{2,26},{10... | collective-permute-start | bytes 786440 | tf_op jit(solution)/shard_map/ppermute | solution.py:199
  21.9 9.6 %collective-permute-start = (bf16[1024,128]{1,0:T(8,128)(2,1)S(1)}, bf16[1024,128]{1,0:T(8,128)(2,1)S(1)}, u32[]{:S(2)}, u32[]{:S(2)}) collective-permute-start(bf16[1024,128]{1,0:T(8,128)(2,1)S(1)} %copy-done.16), channel_id=1, source_target_pairs={{0,8},{8,16},{16,24},{24,0},{1,9},{9,17},{17,25},{25,1},{2,10},{10... | collective-permute-start | bytes 786440 | tf_op jit(solution)/shard_map/ppermute | solution.py:199
  36.6 6.3 %copy-start.3 = (bf16[8,128,512]{2,1,0:T(8,128)(2,1)}, bf16[8,128,512]{2,1,0:T(8,128)(2,1)S(1)}, u32[]{:S(2)}) copy-start(bf16[8,128,512]{2,1,0:T(8,128)(2,1)S(1)} %all-to-all-done) | copy-start | bytes 3145732
  36.6 25.9 %collective-permute-start.3 = (bf16[1024,512]{1,0:T(8,128)(2,1)S(1)}, bf16[1024,512]{1,0:T(8,128)(2,1)S(1)}, u32[]{:S(2)}, u32[]{:S(2)}) collective-permute-start(bf16[1024,512]{1,0:T(8,128)(2,1)S(1)} %bitcast.48), channel_id=1, source_target_pairs={{0,8},{8,16},{16,24},{24,0},{1,9},{9,17},{17,25},{25,1},{2,10},{10... | collective-permute-start | bytes 3145736 | tf_op jit(solution)/shard_map/ppermute | solution.py:199
  37.2 25.3 %collective-permute-start.4 = (bf16[1024,512]{1,0:T(8,128)(2,1)S(1)}, bf16[1024,512]{1,0:T(8,128)(2,1)}, u32[]{:S(2)}, u32[]{:S(2)}) collective-permute-start(bf16[1024,512]{1,0:T(8,128)(2,1)S(1)} %bitcast.49), channel_id=1, source_target_pairs={{0,24},{8,0},{16,8},{24,16},{1,25},{9,1},{17,9},{25,17},{2,26},{10... | collective-permute-start | bytes 3145736 | tf_op jit(solution)/shard_map/ppermute | solution.py:199
  43.0 19.5 %all-to-all-start.1 = ((bf16[8,128,512]{2,1,0:T(8,128)(2,1)}), bf16[8,128,512]{2,1,0:T(8,128)(2,1)S(1)}, u32[]{:S(2)}, u32[]{:S(2)}) async-start(bf16[8,128,512]{2,1,0:T(8,128)(2,1)} %get-tuple-element.62), calls=%async_computation.1 | async-start | bytes 2097152 | tf_op jit(solution)/shard_map/all_to_all | solution.py:205
  46.5 58.3 %all-gather.5.cloned.1.call-start = ((), (), s32[]{:S(2)}) async-start(), calls=%async_computation.5 | async-start | bytes 4718592 | tf_op jit(solution)/shard_map/all_gather | solution.py:251
  62.4 3.5 %copy-start.2 = (bf16[8,128,512]{2,1,0:T(8,128)(2,1)}, bf16[8,128,512]{2,1,0:T(8,128)(2,1)S(1)}, u32[]{:S(2)}) copy-start(bf16[8,128,512]{2,1,0:T(8,128)(2,1)S(1)} %all-to-all-done.1) | copy-start | bytes 3145732
  62.5 3.4 %copy-start.4 = (bf16[1024,512]{1,0:T(8,128)(2,1)}, bf16[1024,512]{1,0:T(8,128)(2,1)S(1)}, u32[]{:S(2)}) copy-start(bf16[1024,512]{1,0:T(8,128)(2,1)S(1)} %collective-permute-done.3.refs_1_) | copy-start | bytes 3145732
  66.0 82.6 %all-gather.7.cloned.1.call-start = ((), (), s32[]{:S(2)}) async-start(), calls=%async_computation.6 | async-start | bytes 4718592 | tf_op jit(solution)/shard_map/all_gather | solution.py:259
  66.0 37.3 %collective-permute-start.5 = (bf16[1536,512]{1,0:T(8,128)(2,1)}, bf16[1536,512]{1,0:T(8,128)(2,1)S(1)}, u32[]{:S(2)}, u32[]{:S(2)}) collective-permute-start(bf16[1536,512]{1,0:T(8,128)(2,1)} %get-tuple-element.72), channel_id=1, source_target_pairs={{0,8},{8,16},{16,24},{24,0},{1,9},{9,17},{17,25},{25,1},{2,10},{10... | collective-permute-start | bytes 4718600 | tf_op jit(solution)/shard_map/ppermute | solution.py:199
  66.1 37.2 %collective-permute-start.6 = (bf16[1536,512]{1,0:T(8,128)(2,1)}, bf16[1536,512]{1,0:T(8,128)(2,1)S(1)}, u32[]{:S(2)}, u32[]{:S(2)}) collective-permute-start(bf16[1536,512]{1,0:T(8,128)(2,1)} %get-tuple-element.73), channel_id=1, source_target_pairs={{0,24},{8,0},{16,8},{24,16},{1,25},{9,1},{17,9},{25,17},{2,26},{10... | collective-permute-start | bytes 4718600 | tf_op jit(solution)/shard_map/ppermute | solution.py:199
  103.3 6.5 %copy-start = (bf16[1536,512]{1,0:T(8,128)(2,1)}, bf16[1536,512]{1,0:T(8,128)(2,1)S(1)}, u32[]{:S(2)}) copy-start(bf16[1536,512]{1,0:T(8,128)(2,1)S(1)} %collective-permute-done.5.refs_3_.refs_1_) | copy-start | bytes 4718596
  103.3 6.5 %copy-start.1 = (bf16[1536,512]{1,0:T(8,128)(2,1)}, bf16[1536,512]{1,0:T(8,128)(2,1)S(1)}, u32[]{:S(2)}) copy-start(bf16[1536,512]{1,0:T(8,128)(2,1)S(1)} %collective-permute-done.6.refs_4_.refs_2_) | copy-start | bytes 4718596
  106.5 17.7 %copy-start.11 = (bf16[512,512]{1,0:T(8,128)(2,1)S(1)}, bf16[512,512]{1,0:T(8,128)(2,1)}, u32[]{:S(2)}) copy-start(bf16[512,512]{1,0:T(8,128)(2,1)} %slice.58) | copy-start | bytes 1572868
  106.6 17.7 %copy-start.10 = (bf16[512,512]{1,0:T(8,128)(2,1)S(1)}, bf16[512,512]{1,0:T(8,128)(2,1)}, u32[]{:S(2)}) copy-start(bf16[512,512]{1,0:T(8,128)(2,1)} %slice.59) | copy-start | bytes 1572868
  106.6 42.0 %collective-permute-start.7 = (bf16[1024,384]{1,0:T(8,128)(2,1)}, bf16[1024,384]{1,0:T(8,128)(2,1)}, u32[]{:S(2)}, u32[]{:S(2)}) collective-permute-start(bf16[1024,384]{1,0:T(8,128)(2,1)} %bitcast.53), channel_id=1, source_target_pairs={{0,8},{8,16},{16,24},{24,0},{1,9},{9,17},{17,25},{25,1},{2,10},{10... | collective-permute-start | bytes 2359304 | tf_op jit(solution)/shard_map/ppermute | solution.py:199
  106.7 41.9 %collective-permute-start.8 = (bf16[1024,384]{1,0:T(8,128)(2,1)}, bf16[1024,384]{1,0:T(8,128)(2,1)}, u32[]{:S(2)}, u32[]{:S(2)}) collective-permute-start(bf16[1024,384]{1,0:T(8,128)(2,1)} %bitcast.54), channel_id=1, source_target_pairs={{0,24},{8,0},{16,8},{24,16},{1,25},{9,1},{17,9},{25,17},{2,26},{10... | collective-permute-start | bytes 2359304 | tf_op jit(solution)/shard_map/ppermute | solution.py:199
  117.9 30.7 %collective-permute-start.9 = (f16[528,512]{1,0:T(8,128)(2,1)S(1)}, f16[528,512]{1,0:T(8,128)(2,1)S(1)}, u32[]{:S(2)}, u32[]{:S(2)}) collective-permute-start(f16[528,512]{1,0:T(8,128)(2,1)S(1)} %convert_element_type.21), channel_id=1, source_target_pairs={{0,32},{32,0},{1,33},{33,1},{2,34},{34,2},{3,35},{35,3},{4,36},{36... | collective-permute-start | bytes 1622024 | tf_op jit(solution)/shard_map/ppermute | solution.py:199
  124.3 14.7 %collective-permute-start.10 = (bf16[512,512]{1,0:T(8,128)(2,1)S(1)}, bf16[512,512]{1,0:T(8,128)(2,1)S(1)}, u32[]{:S(2)}, u32[]{:S(2)}) collective-permute-start(bf16[512,512]{1,0:T(8,128)(2,1)S(1)} %copy-done.11), channel_id=1, source_target_pairs={{0,8},{8,16},{16,24},{24,0},{1,9},{9,17},{17,25},{25,1},{2,10},{10... | collective-permute-start | bytes 1572872 | tf_op jit(solution)/shard_map/ppermute | solution.py:199
  124.3 14.7 %collective-permute-start.11 = (bf16[512,512]{1,0:T(8,128)(2,1)S(1)}, bf16[512,512]{1,0:T(8,128)(2,1)S(1)}, u32[]{:S(2)}, u32[]{:S(2)}) collective-permute-start(bf16[512,512]{1,0:T(8,128)(2,1)S(1)} %copy-done.10), channel_id=1, source_target_pairs={{0,24},{8,0},{16,8},{24,16},{1,25},{9,1},{17,9},{25,17},{2,26},{10... | collective-permute-start | bytes 1572872 | tf_op jit(solution)/shard_map/ppermute | solution.py:199
  139.0 0.8 copy-start.6
  139.8 0.8 copy-start.7
  150.7 30.0 %collective-permute-start.12 = (f16[528,512]{1,0:T(8,128)(2,1)S(1)}, f16[528,512]{1,0:T(8,128)(2,1)S(1)}, u32[]{:S(2)}, u32[]{:S(2)}) collective-permute-start(f16[528,512]{1,0:T(8,128)(2,1)S(1)} %convert_element_type.22), channel_id=1, source_target_pairs={{0,32},{32,0},{1,33},{33,1},{2,34},{34,2},{3,35},{35,3},{4,36},{36... | collective-permute-start | bytes 1622024 | tf_op jit(solution)/shard_map/ppermute | solution.py:199
  157.1 11.7 %collective-permute-start.13 = (bf16[512,384]{1,0:T(8,128)(2,1)S(1)}, bf16[512,384]{1,0:T(8,128)(2,1)S(1)}, u32[]{:S(2)}, u32[]{:S(2)}) collective-permute-start(bf16[512,384]{1,0:T(8,128)(2,1)S(1)} %slice.60), channel_id=1, source_target_pairs={{0,8},{8,16},{16,24},{24,0},{1,9},{9,17},{17,25},{25,1},{2,10},{10... | collective-permute-start | bytes 1179656 | tf_op jit(solution)/shard_map/ppermute | solution.py:199
  157.1 11.7 %collective-permute-start.14 = (bf16[512,384]{1,0:T(8,128)(2,1)S(1)}, bf16[512,384]{1,0:T(8,128)(2,1)S(1)}, u32[]{:S(2)}, u32[]{:S(2)}) collective-permute-start(bf16[512,384]{1,0:T(8,128)(2,1)S(1)} %slice.61), channel_id=1, source_target_pairs={{0,24},{8,0},{16,8},{24,16},{1,25},{9,1},{17,9},{25,17},{2,26},{10... | collective-permute-start | bytes 1179656 | tf_op jit(solution)/shard_map/ppermute | solution.py:199
  168.8 0.7 copy-start.8
  169.5 0.7 copy-start.9
  180.7 25.8 %all-to-all-start.3 = ((f32[8,64,512]{2,1,0:T(8,128)}), f32[8,64,512]{2,1,0:T(8,128)S(1)}, u32[]{:S(2)}, u32[]{:S(2)}) async-start(f32[8,64,512]{2,1,0:T(8,128)} %bitcast.25), calls=%async_computation.3 | async-start | bytes 2097152 | tf_op jit(solution)/shard_map/all_to_all | solution.py:205
  184.2 22.2 %collective-permute-start.15 = (f16[528,384]{1,0:T(8,128)(2,1)S(1)}, f16[528,384]{1,0:T(8,128)(2,1)S(1)}, u32[]{:S(2)}, u32[]{:S(2)}) collective-permute-start(f16[528,384]{1,0:T(8,128)(2,1)S(1)} %convert_element_type.23), channel_id=1, source_target_pairs={{0,32},{32,0},{1,33},{33,1},{2,34},{34,2},{3,35},{35,3},{4,36},{36... | collective-permute-start | bytes 1216520 | tf_op jit(solution)/shard_map/ppermute | solution.py:199
  206.5 4.6 %copy-start.5 = (f32[8,64,512]{2,1,0:T(8,128)}, f32[8,64,512]{2,1,0:T(8,128)S(1)}, u32[]{:S(2)}) copy-start(f32[8,64,512]{2,1,0:T(8,128)S(1)} %all-to-all-done.3.refs_0_) | copy-start | bytes 3145732
  246.7 5.5 %collective-permute-start.16 = (f32[88,128]{1,0:T(8,128)}, f32[88,128]{1,0:T(8,128)S(1)}, u32[]{:S(2)}, u32[]{:S(2)}) collective-permute-start(f32[88,128]{1,0:T(8,128)} %get-tuple-element.110.b0), channel_id=1, source_target_pairs={{0,64},{64,128},{128,192},{192,0},{1,65},{65,129},{129,193},{193,1... | collective-permute-start | bytes 135176 | tf_op jit(solution)/shard_map/band/ppermute | solution.py:199
  250.2 5.2 %collective-permute-start.17 = (f32[88,128]{1,0:T(8,128)}, f32[88,128]{1,0:T(8,128)S(1)}, u32[]{:S(2)}, u32[]{:S(2)}) collective-permute-start(f32[88,128]{1,0:T(8,128)} %get-tuple-element.110.b0), channel_id=1, source_target_pairs={{0,128},{64,192},{128,0},{192,64},{1,129},{65,193},{129,1},{193,65... | collective-permute-start | bytes 135176 | tf_op jit(solution)/shard_map/band/ppermute | solution.py:199
  250.2 5.2 %collective-permute-start.18 = (f32[88,128]{1,0:T(8,128)}, f32[88,128]{1,0:T(8,128)S(1)}, u32[]{:S(2)}, u32[]{:S(2)}) collective-permute-start(f32[88,128]{1,0:T(8,128)} %get-tuple-element.110.b0), channel_id=1, source_target_pairs={{0,192},{64,0},{128,64},{192,128},{1,193},{65,1},{129,65},{193,129... | collective-permute-start | bytes 135176 | tf_op jit(solution)/shard_map/band/ppermute | solution.py:199
  252.2 3.1 %copy-start.13 = (f32[88,128]{1,0:T(8,128)}, f32[88,128]{1,0:T(8,128)S(1)}, u32[]{:S(2)}) copy-start(f32[88,128]{1,0:T(8,128)S(1)} %collective-permute-done.16.b1) | copy-start | bytes 135172
  255.3 0.6 copy-start.14
  255.9 0.6 copy-start.15
Sparse Core Ops, SparseCore 0:
  66.1 38.6 all-gather.4
  106.7 33.9 all-gather.6

commit v4 on v3

--- a/solution.py
+++ b/solution.py
@@ -262,12 +262,13 @@
     got0 = along("zh", 1, send0)
     send1 = payload(sent, [v1, r1, l1, *far1])
 
-    r2, l2, got0, send1, kept = sync(r2, l2, got0, send1, kept)
+    r2, l2, send1, kept = sync(r2, l2, send1, kept)
     half2 = halves(r2, l2)
-    half2, got0, send1, kept = sync(half2, got0, send1, kept)
+    half2, send1, kept = sync(half2, send1, kept)
     far2 = along("x", 1, half2[0]), along("x", 3, half2[1])
     got1 = along("zh", 1, send1)
     send2 = payload(sent, [v2, r2, l2, *far2])
+    kept, got0 = sync(kept, got0)
     total0 = joined(tile(keep_kernel, kept, [v0, r0, l0, r1, l1], 0), got0)
 
     got1, send2, total0, kept = sync(got1, send2, total0, kept)

time: 268 us -> 268 us (level)
  transfers between devices with their start and end apart: 24 -> 24, of which waited for: 12 -> 12; matrix products, arithmetic and copies ran while one was open for 4% -> 5% of each run, Pallas kernels for 16% -> 16%
where the time goes in v4:
time: 268 us; the launch traced here: 267 us
  waiting for transfers between devices  62.1 us (23%)
  Pallas kernels  59 us (22%)
  starting transfers between devices  56.7 us (21%)
  blocking collectives  50.8 us (19%)
  between operations  14.2 us (5%)
  other arithmetic  12.9 us (5%)
  local copies, waits for them, and re-layouts  11 us (4%)
    all_to_all x2, blocking collectives, swap(): return lax.all_to_all(value, ('y', 'core'), 0, 0, tiled=True)  50.8 us
    ppermute x19, starting transfers between devices, along(): lax.ppermute(value, axis, shift(2 if axis in ('core', 'zh') else 4, by))  44.9 us
    ppermute x19, waiting for transfers between devices, along(): lax.ppermute(value, axis, shift(2 if axis in ('core', 'zh') else 4, by))  42.8 us
    pallas_call x6, Pallas kernels, tile(): pl.pallas_call(kernel, grid=(half // rows,), out_shape=jax.ShapeDtypeStru...  37.4 us
    all_to_all x3, waiting for transfers between devices, swap(): return lax.all_to_all(value, ('y', 'core'), 0, 0, tiled=True)  17.7 us
    pallas_call x5, Pallas kernels, call(): pl.pallas_call(kernel, out_shape=shapes, in_specs=spec or [VMEM] * len(ar...  15.2 us
    all_to_all x3, starting transfers between devices, swap(): return lax.all_to_all(value, ('y', 'core'), 0, 0, tiled=True)  11.7 us
    pallas_call x1, Pallas kernels, on_device(): pl.pallas_call(functools.partial(finish_kernel, [d.shape[2] for d in done...  6.38 us
  transfers between devices with their start and end apart: 24, of which 12 were waited for; matrix products, arithmetic and copies ran while one was open for 5% of the time, Pallas kernels for 16%

profile of v4, /device:TPU:32, one launch (start us, length us, event | category | flops | bytes accessed | tf_op | source)
XLA Modules:
  0.0 266.7 jit_solution(9684047105080345618)
XLA Ops:
  7.2 0.7 stack.65.at_ref
  7.9 2.3 shard_map.105
  10.2 3.0 %collective-permute-start.2 = (bf16[1024,128]{1,0:T(8,128)(2,1)}, bf16[1024,128]{1,0:T(8,128)(2,1)S(1)}, u32[]{:S(2)}, u32[]{:S(2)}) collective-permute-start(bf16[1024,128]{1,0:T(8,128)(2,1)} %get-tuple-element.60), channel_id=1, source_target_pairs={{0,16},{8,24},{16,0},{24,8},{1,17},{9,25},{17,1},{25,9},{2,18},{10... | collective-permute-start | bytes 786440 | tf_op jit(solution)/shard_map/ppermute | solution.py:199
  13.2 2.8 %shard_map.104 = bf16[8,128,512]{2,1,0:T(8,128)(2,1)} custom-call(bf16[128,11008]{1,0:T(8,128)(2,1)} %bitcast.46), custom_call_target="tpu_custom_call" | custom-call | flops 1 | bytes 1 | tf_op jit(solution)/shard_map/pallas_call | solution.py:85
  16.1 4.6 %all-to-all-start = ((bf16[8,128,512]{2,1,0:T(8,128)(2,1)}), bf16[8,128,512]{2,1,0:T(8,128)(2,1)S(1)}, u32[]{:S(2)}, u32[]{:S(2)}) async-start(bf16[8,128,512]{2,1,0:T(8,128)(2,1)} %shard_map.104), calls=%async_computation | async-start | bytes 2097152 | tf_op jit(solution)/shard_map/all_to_all | solution.py:205
  20.7 1.2 collective-permute-start.1
  21.9 0.9 collective-permute-start
  22.8 6.6 %collective-permute-done.1 = bf16[1024,128]{1,0:T(8,128)(2,1)S(1)} collective-permute-done((bf16[1024,128]{1,0:T(8,128)(2,1)S(1)}, bf16[1024,128]{1,0:T(8,128)(2,1)S(1)}, u32[]{:S(2)}, u32[]{:S(2)}) %collective-permute-start.1) | collective-permute-done | bytes 262176 | tf_op jit(solution)/shard_map/ppermute | solution.py:199
  29.4 2.1 collective-permute-done
  31.5 0.7 slice_bitcast_fusion.2
  32.1 0.9 pad_maximum_fusion.2
  33.0 3.6 %all-to-all-done = bf16[8,128,512]{2,1,0:T(8,128)(2,1)S(1)} async-done(((bf16[8,128,512]{2,1,0:T(8,128)(2,1)}), bf16[8,128,512]{2,1,0:T(8,128)(2,1)S(1)}, u32[]{:S(2)}, u32[]{:S(2)}) %all-to-all-start) | async-done | bytes 1048608 | tf_op jit(solution)/shard_map/all_to_all | solution.py:205
  36.6 0.6 collective-permute-start.3
  37.2 2.6 collective-permute-start.4
  39.9 3.1 %shard_map.106 = (bf16[8,128,512]{2,1,0:T(8,128)(2,1)}, bf16[8,128,384]{2,1,0:T(8,128)(2,1)}) custom-call(bf16[128,11008]{1,0:T(8,128)(2,1)} %bitcast.47), custom_call_target="tpu_custom_call" | custom-call | flops 1 | bytes 1 | tf_op jit(solution)/shard_map/pallas_call | solution.py:85
  43.0 3.6 %all-to-all-start.1 = ((bf16[8,128,512]{2,1,0:T(8,128)(2,1)}), bf16[8,128,512]{2,1,0:T(8,128)(2,1)S(1)}, u32[]{:S(2)}, u32[]{:S(2)}) async-start(bf16[8,128,512]{2,1,0:T(8,128)(2,1)} %get-tuple-element.62), calls=%async_computation.1 | async-start | bytes 2097152 | tf_op jit(solution)/shard_map/all_to_all | solution.py:205
  46.6 1.8 pad_maximum_fusion.3
  48.4 14.0 %all-to-all-done.1 = bf16[8,128,512]{2,1,0:T(8,128)(2,1)S(1)} async-done(((bf16[8,128,512]{2,1,0:T(8,128)(2,1)}), bf16[8,128,512]{2,1,0:T(8,128)(2,1)S(1)}, u32[]{:S(2)}, u32[]{:S(2)}) %all-to-all-start.1) | async-done | bytes 1048608 | tf_op jit(solution)/shard_map/all_to_all | solution.py:205
  62.5 1.5 slice.57
  64.1 1.9 pad_maximum_fusion
  66.1 3.2 %collective-permute-start.6 = (bf16[1536,512]{1,0:T(8,128)(2,1)}, bf16[1536,512]{1,0:T(8,128)(2,1)S(1)}, u32[]{:S(2)}, u32[]{:S(2)}) collective-permute-start(bf16[1536,512]{1,0:T(8,128)(2,1)} %get-tuple-element.73), channel_id=1, source_target_pairs={{0,24},{8,0},{16,8},{24,16},{1,25},{9,1},{17,9},{25,17},{2,26},{10... | collective-permute-start | bytes 4718600 | tf_op jit(solution)/shard_map/ppermute | solution.py:199
  69.3 21.6 %all_to_all.25 = bf16[8,128,384]{2,1,0:T(8,128)(2,1)} all-to-all(bf16[8,128,384]{2,1,0:T(8,128)(2,1)} %get-tuple-element.74), channel_id=1, replica_groups=mesh['rep'=4,'zh'=2,'x'=4,'y'=4,'core'=2] {'y','core'}, dimensions={0} | all-to-all | bytes 1572864 | tf_op jit(solution)/shard_map/all_to_all | solution.py:205
  90.9 12.4 %collective-permute-done.5.refs_3_.refs_1_ = bf16[1536,512]{1,0:T(8,128)(2,1)S(1)} collective-permute-done((bf16[1536,512]{1,0:T(8,128)(2,1)}, bf16[1536,512]{1,0:T(8,128)(2,1)S(1)}, u32[]{:S(2)}, u32[]{:S(2)}) %collective-permute-start.5) | collective-permute-done | bytes 1572896 | tf_op jit(solution)/shard_map/ppermute | solution.py:199
  103.3 1.5 all-gather.5.cloned.1.call-done
  104.8 0.8 slice.58
  105.6 0.8 slice.59
  106.6 3.2 %collective-permute-start.8 = (bf16[1024,384]{1,0:T(8,128)(2,1)}, bf16[1024,384]{1,0:T(8,128)(2,1)}, u32[]{:S(2)}, u32[]{:S(2)}) collective-permute-start(bf16[1024,384]{1,0:T(8,128)(2,1)} %bitcast.54), channel_id=1, source_target_pairs={{0,24},{8,0},{16,8},{24,16},{1,25},{9,1},{17,9},{25,17},{2,26},{10... | collective-permute-start | bytes 2359304 | tf_op jit(solution)/shard_map/ppermute | solution.py:199
  109.8 3.2 %collective-permute-start.10 = (bf16[512,512]{1,0:T(8,128)(2,1)}, bf16[512,512]{1,0:T(8,128)(2,1)S(1)}, u32[]{:S(2)}, u32[]{:S(2)}) collective-permute-start(bf16[512,512]{1,0:T(8,128)(2,1)} %slice.59), channel_id=1, source_target_pairs={{0,24},{8,0},{16,8},{24,16},{1,25},{9,1},{17,9},{25,17},{2,26},{10... | collective-permute-start | bytes 1572872 | tf_op jit(solution)/shard_map/ppermute | solution.py:199
  113.1 6.6 %shard_map.107 = f32[528,512]{1,0:T(8,128)} custom-call(bf16[8,4,512,128]{3,2,1,0:T(8,128)(2,1)} %bitcast.37, bf16[1024,512]{1,0:T(8,128)(2,1)} %bitcast.50, bf16[1024,512]{1,0:T(8,128)(2,1)} %copy-done.4, bf16[1024,512]{1,0:T(8,128)(2,1)} %collective-permute-done.4.refs_2_, bf16[1536,512]{1,0:T(8,128)(2,1)} %copy-done, bf16[1536,512]{1,0:T(8,128)(2,1)} %copy-done.1), custom_call_target="tpu_custom_call" | custom-call | flops 1 | bytes 1 | tf_op jit(solution)/shard_map/pallas_call | solution.py:165
  119.7 1.3 convert_element_type.21
  121.0 6.6 %collective-permute-start.14 = (f16[528,512]{1,0:T(8,128)(2,1)S(1)}, f16[528,512]{1,0:T(8,128)(2,1)S(1)}, u32[]{:S(2)}, u32[]{:S(2)}) collective-permute-start(f16[528,512]{1,0:T(8,128)(2,1)S(1)} %convert_element_type.21), channel_id=1, source_target_pairs={{0,32},{32,0},{1,33},{33,1},{2,34},{34,2},{3,35},{35,3},{4,36},{36... | collective-permute-start | bytes 1622024 | tf_op jit(solution)/shard_map/ppermute | solution.py:199
  127.6 11.3 %collective-permute-done.9.refs_3_ = bf16[512,512]{1,0:T(8,128)(2,1)S(1)} collective-permute-done((bf16[512,512]{1,0:T(8,128)(2,1)}, bf16[512,512]{1,0:T(8,128)(2,1)S(1)}, u32[]{:S(2)}, u32[]{:S(2)}) %collective-permute-start.9) | collective-permute-done | bytes 524320 | tf_op jit(solution)/shard_map/ppermute | solution.py:199
  139.0 0.8 copy-done.6
  139.7 0.8 copy-done.7
  140.5 6.6 %shard_map.108 = f32[528,512]{1,0:T(8,128)} custom-call(bf16[8,4,512,128]{3,2,1,0:T(8,128)(2,1)} %bitcast.38, bf16[1024,512]{1,0:T(8,128)(2,1)} %bitcast.44, bf16[1536,512]{1,0:T(8,128)(2,1)} %copy-done, bf16[1536,512]{1,0:T(8,128)(2,1)} %copy-done.1, bf16[512,512]{1,0:T(8,128)(2,1)} %copy-done.6, bf16[512,512]{1,0:T(8,128)(2,1)} %copy-done.7), custom_call_target="tpu_custom_call" | custom-call | flops 1 | bytes 1 | tf_op jit(solution)/shard_map/pallas_call | solution.py:165
  147.1 1.3 convert_element_type.22
  148.5 1.0 slice.60
  149.6 1.0 slice.61
  150.6 6.4 %collective-permute-start.11 = (f16[528,512]{1,0:T(8,128)(2,1)S(1)}, f16[528,512]{1,0:T(8,128)(2,1)S(1)}, u32[]{:S(2)}, u32[]{:S(2)}) collective-permute-start(f16[528,512]{1,0:T(8,128)(2,1)S(1)} %convert_element_type.22), channel_id=1, source_target_pairs={{0,32},{32,0},{1,33},{33,1},{2,34},{34,2},{3,35},{35,3},{4,36},{36... | collective-permute-start | bytes 1622024 | tf_op jit(solution)/shard_map/ppermute | solution.py:199
  157.0 3.2 %collective-permute-start.13 = (bf16[512,384]{1,0:T(8,128)(2,1)S(1)}, bf16[512,384]{1,0:T(8,128)(2,1)S(1)}, u32[]{:S(2)}, u32[]{:S(2)}) collective-permute-start(bf16[512,384]{1,0:T(8,128)(2,1)S(1)} %slice.61), channel_id=1, source_target_pairs={{0,24},{8,0},{16,8},{24,16},{1,25},{9,1},{17,9},{25,17},{2,26},{10... | collective-permute-start | bytes 1179656 | tf_op jit(solution)/shard_map/ppermute | solution.py:199
  160.2 6.1 %shard_map.110 = f32[512,512]{1,0:T(8,128)} custom-call(bf16[8,4,512,128]{3,2,1,0:T(8,128)(2,1)} %bitcast.40, bf16[1024,512]{1,0:T(8,128)(2,1)} %bitcast.51, bf16[1024,512]{1,0:T(8,128)(2,1)} %copy-done.4, bf16[1024,512]{1,0:T(8,128)(2,1)} %collective-permute-done.4.refs_2_, bf16[1536,512]{1,0:T(8,128)(2,1)} %copy-done, bf16[1536,512]{1,0:T(8,128)(2,1)} %copy-done.1), custom_call_target="tpu_custom_call" | custom-call | flops 1 | bytes 1 | tf_op jit(solution)/shard_map/pallas_call | solution.py:165
  166.4 2.4 multiply_add_fusion
  168.7 0.7 copy-done.8
  169.5 0.8 copy-done.9
  170.2 6.2 %shard_map.109 = f32[528,384]{1,0:T(8,128)} custom-call(bf16[8,4,512,128]{3,2,1,0:T(8,128)(2,1)} %bitcast.39, bf16[1024,384]{1,0:T(8,128)(2,1)} %bitcast.55, bf16[1024,384]{1,0:T(8,128)(2,1)} %collective-permute-done.7.refs_1_, bf16[1024,384]{1,0:T(8,128)(2,1)} %collective-permute-done.8.refs_2_, bf16[512,384]{1,0:T(8,128)(2,1)} %copy-done.8, ...), custom_call_target="tpu_custom_call" | custom-call | flops 1 | bytes 1 | tf_op jit(solution)/shard_map/pallas_call | solution.py:165
  176.4 1.2 convert_element_type.23
  177.6 3.0 %collective-permute-done.11 = f16[528,512]{1,0:T(8,128)(2,1)S(1)} collective-permute-done((f16[528,512]{1,0:T(8,128)(2,1)S(1)}, f16[528,512]{1,0:T(8,128)(2,1)S(1)}, u32[]{:S(2)}, u32[]{:S(2)}) %collective-permute-start.11) | collective-permute-done | bytes 540704 | tf_op jit(solution)/shard_map/ppermute | solution.py:199
  180.6 3.6 %all-to-all-start.3 = ((f32[8,64,512]{2,1,0:T(8,128)}), f32[8,64,512]{2,1,0:T(8,128)S(1)}, u32[]{:S(2)}, u32[]{:S(2)}) async-start(f32[8,64,512]{2,1,0:T(8,128)} %bitcast.25), calls=%async_computation.3 | async-start | bytes 2097152 | tf_op jit(solution)/shard_map/all_to_all | solution.py:205
  184.2 5.6 %collective-permute-start.15 = (f16[528,384]{1,0:T(8,128)(2,1)S(1)}, f16[528,384]{1,0:T(8,128)(2,1)S(1)}, u32[]{:S(2)}, u32[]{:S(2)}) collective-permute-start(f16[528,384]{1,0:T(8,128)(2,1)S(1)} %convert_element_type.23), channel_id=1, source_target_pairs={{0,32},{32,0},{1,33},{33,1},{2,34},{34,2},{3,35},{35,3},{4,36},{36... | collective-permute-start | bytes 1216520 | tf_op jit(solution)/shard_map/ppermute | solution.py:199
  189.8 6.1 %shard_map.111.refs_0_ = f32[512,512]{1,0:T(8,128)} custom-call(bf16[8,4,512,128]{3,2,1,0:T(8,128)(2,1)} %bitcast.41, bf16[1024,512]{1,0:T(8,128)(2,1)} %bitcast.45, bf16[1536,512]{1,0:T(8,128)(2,1)} %copy-done, bf16[1536,512]{1,0:T(8,128)(2,1)} %copy-done.1, bf16[512,512]{1,0:T(8,128)(2,1)} %copy-done.6, bf16[512,512]{1,0:T(8,128)(2,1)} %copy-done.7), custom_call_target="tpu_custom_call" | custom-call | flops 1 | bytes 1 | tf_op jit(solution)/shard_map/pallas_call | solution.py:165
  195.8 5.8 %shard_map.112.refs_2_ = f32[512,384]{1,0:T(8,128)} custom-call(bf16[8,4,512,128]{3,2,1,0:T(8,128)(2,1)} %bitcast.42, bf16[1024,384]{1,0:T(8,128)(2,1)} %bitcast.56, bf16[1024,384]{1,0:T(8,128)(2,1)} %collective-permute-done.7.refs_1_, bf16[1024,384]{1,0:T(8,128)(2,1)} %collective-permute-done.8.refs_2_, bf16[512,384]{1,0:T(8,128)(2,1)} %copy-done.8, ...), custom_call_target="tpu_custom_call" | custom-call | flops 1 | bytes 1 | tf_op jit(solution)/shard_map/pallas_call | solution.py:165
  201.6 1.1 convert_element_type.26.refs_1_
  202.7 3.7 %collective-permute-done.15 = f16[528,384]{1,0:T(8,128)(2,1)S(1)} collective-permute-done((f16[528,384]{1,0:T(8,128)(2,1)S(1)}, f16[528,384]{1,0:T(8,128)(2,1)S(1)}, u32[]{:S(2)}, u32[]{:S(2)}) %collective-permute-start.15) | collective-permute-done | bytes 405536 | tf_op jit(solution)/shard_map/ppermute | solution.py:199
  206.4 1.0 convert_element_type.27.refs_3_
  207.4 3.6 %shard_map.113 = f32[512,896]{1,0:T(8,128)} custom-call(f32[512,512]{1,0:T(8,128)} %shard_map.111.refs_0_, f32[528,512]{1,0:T(8,128)} %convert_element_type.26.refs_1_, f32[512,384]{1,0:T(8,128)} %shard_map.112.refs_2_, f32[528,384]{1,0:T(8,128)} %convert_element_type.27.refs_3_), custom_call_target="tpu_custom_call" | custom-call | flops 1 | bytes 1 | tf_op jit(solution)/shard_map/pallas_call | solution.py:85
  211.0 29.2 %all_to_all.26.refs_1_ = f32[8,64,896]{2,1,0:T(8,128)} all-to-all(f32[8,64,896]{2,1,0:T(8,128)} %bitcast.52), channel_id=1, replica_groups=mesh['rep'=4,'zh'=2,'x'=4,'y'=4,'core'=2] {'y','core'}, dimensions={0} | all-to-all | bytes 3670016 | tf_op jit(solution)/shard_map/all_to_all | solution.py:205
  240.2 6.4 %finish.1 = (f32[64,11008]{1,0:T(8,128)}, f32[88,128]{1,0:T(8,128)}) custom-call(f32[8,64]{1,0:T(8,128)} %constant.63.clone.basis_ref, f32[64,8]{1,0:T(8,128)} %constant.64.clone.back_ref, f32[1024,128]{1,0:T(8,128)} %constant.65.clone.wide_ref, f32[128,1024]{1,0:T(8,128)} %constant.66.clone.tall_ref, f32[64,11008]{1,0:T(8,128)} %bitcast.58, ...), custom_call_target="tpu_custom_call" | custom-call | tf_op jit(solution)/shard_map/finish/pallas_call | solution.py:290
  246.6 3.5 %collective-permute-start.16 = (f32[88,128]{1,0:T(8,128)}, f32[88,128]{1,0:T(8,128)S(1)}, u32[]{:S(2)}, u32[]{:S(2)}) collective-permute-start(f32[88,128]{1,0:T(8,128)} %get-tuple-element.110.b0), channel_id=1, source_target_pairs={{0,64},{64,128},{128,192},{192,0},{1,65},{65,129},{129,193},{193,1... | collective-permute-start | bytes 135176 | tf_op jit(solution)/shard_map/band/ppermute | solution.py:199
  250.1 1.5 collective-permute-start.18
  251.6 0.6 collective-permute-done.16.b1
  252.1 3.1 %collective-permute-done.17.b2 = f32[88,128]{1,0:T(8,128)S(1)} collective-permute-done((f32[88,128]{1,0:T(8,128)}, f32[88,128]{1,0:T(8,128)S(1)}, u32[]{:S(2)}, u32[]{:S(2)}) %collective-permute-start.17) | collective-permute-done | bytes 45088 | tf_op jit(solution)/shard_map/band/ppermute | solution.py:199
  255.3 0.6 copy-done.12
  255.9 0.6 copy-done.13
  256.5 3.4 %update.1 = f32[64,11008]{1,0:T(8,128)} custom-call(f32[64,8]{1,0:T(8,128)} %constant.64.clone.back_ref, f32[128,1024]{1,0:T(8,128)} %constant.66.clone.tall_ref, f32[88,128]{1,0:T(8,128)} %get-tuple-element.110.b0, f32[88,128]{1,0:T(8,128)} %copy-done.11, f32[88,128]{1,0:T(8,128)} %copy-done.12, f32[88,128]{1,0:T(8,128)} %copy-done.13), custom_call_target="tpu_custom_call" | custom-call | flops 1 | bytes 1 | tf_op jit(solution)/shard_map/update/pallas_call | solution.py:85
  (53 shorter events, 0.6 us)
Async XLA Ops:
  10.2 12.6 %collective-permute-start.2 = (bf16[1024,128]{1,0:T(8,128)(2,1)}, bf16[1024,128]{1,0:T(8,128)(2,1)S(1)}, u32[]{:S(2)}, u32[]{:S(2)}) collective-permute-start(bf16[1024,128]{1,0:T(8,128)(2,1)} %get-tuple-element.60), channel_id=1, source_target_pairs={{0,16},{8,24},{16,0},{24,8},{1,17},{9,25},{17,1},{25,9},{2,18},{10... | collective-permute-start | bytes 786440 | tf_op jit(solution)/shard_map/ppermute | solution.py:199
  16.1 4.6 %copy-start.15 = (bf16[1024,128]{1,0:T(8,128)(2,1)S(1)}, bf16[1024,128]{1,0:T(8,128)(2,1)}, u32[]{:S(2)}) copy-start(bf16[1024,128]{1,0:T(8,128)(2,1)} %get-tuple-element.59) | copy-start | bytes 786436
  16.1 5.8 %copy-start.14 = (bf16[1024,128]{1,0:T(8,128)(2,1)S(1)}, bf16[1024,128]{1,0:T(8,128)(2,1)}, u32[]{:S(2)}) copy-start(bf16[1024,128]{1,0:T(8,128)(2,1)} %get-tuple-element.58) | copy-start | bytes 786436
  16.1 6.7 %copy-start.10 = (bf16[1024,128]{1,0:T(8,128)(2,1)S(1)}, bf16[1024,128]{1,0:T(8,128)(2,1)}, u32[]{:S(2)}) copy-start(bf16[1024,128]{1,0:T(8,128)(2,1)} %get-tuple-element.57) | copy-start | bytes 786436
  16.1 20.6 %all-to-all-start = ((bf16[8,128,512]{2,1,0:T(8,128)(2,1)}), bf16[8,128,512]{2,1,0:T(8,128)(2,1)S(1)}, u32[]{:S(2)}, u32[]{:S(2)}) async-start(bf16[8,128,512]{2,1,0:T(8,128)(2,1)} %shard_map.104), calls=%async_computation | async-start | bytes 2097152 | tf_op jit(solution)/shard_map/all_to_all | solution.py:205
  20.7 8.7 %collective-permute-start.1 = (bf16[1024,128]{1,0:T(8,128)(2,1)S(1)}, bf16[1024,128]{1,0:T(8,128)(2,1)S(1)}, u32[]{:S(2)}, u32[]{:S(2)}) collective-permute-start(bf16[1024,128]{1,0:T(8,128)(2,1)S(1)} %copy-done.15), channel_id=1, source_target_pairs={{0,24},{8,0},{16,8},{24,16},{1,25},{9,1},{17,9},{25,17},{2,26},{10... | collective-permute-start | bytes 786440 | tf_op jit(solution)/shard_map/ppermute | solution.py:199
  21.9 9.6 %collective-permute-start = (bf16[1024,128]{1,0:T(8,128)(2,1)S(1)}, bf16[1024,128]{1,0:T(8,128)(2,1)S(1)}, u32[]{:S(2)}, u32[]{:S(2)}) collective-permute-start(bf16[1024,128]{1,0:T(8,128)(2,1)S(1)} %copy-done.14), channel_id=1, source_target_pairs={{0,8},{8,16},{16,24},{24,0},{1,9},{9,17},{17,25},{25,1},{2,10},{10... | collective-permute-start | bytes 786440 | tf_op jit(solution)/shard_map/ppermute | solution.py:199
  36.6 6.3 %copy-start.3 = (bf16[8,128,512]{2,1,0:T(8,128)(2,1)}, bf16[8,128,512]{2,1,0:T(8,128)(2,1)S(1)}, u32[]{:S(2)}) copy-start(bf16[8,128,512]{2,1,0:T(8,128)(2,1)S(1)} %all-to-all-done) | copy-start | bytes 3145732
  36.6 25.9 %collective-permute-start.3 = (bf16[1024,512]{1,0:T(8,128)(2,1)S(1)}, bf16[1024,512]{1,0:T(8,128)(2,1)S(1)}, u32[]{:S(2)}, u32[]{:S(2)}) collective-permute-start(bf16[1024,512]{1,0:T(8,128)(2,1)S(1)} %bitcast.48), channel_id=1, source_target_pairs={{0,8},{8,16},{16,24},{24,0},{1,9},{9,17},{17,25},{25,1},{2,10},{10... | collective-permute-start | bytes 3145736 | tf_op jit(solution)/shard_map/ppermute | solution.py:199
  37.2 25.3 %collective-permute-start.4 = (bf16[1024,512]{1,0:T(8,128)(2,1)S(1)}, bf16[1024,512]{1,0:T(8,128)(2,1)}, u32[]{:S(2)}, u32[]{:S(2)}) collective-permute-start(bf16[1024,512]{1,0:T(8,128)(2,1)S(1)} %bitcast.49), channel_id=1, source_target_pairs={{0,24},{8,0},{16,8},{24,16},{1,25},{9,1},{17,9},{25,17},{2,26},{10... | collective-permute-start | bytes 3145736 | tf_op jit(solution)/shard_map/ppermute | solution.py:199
  43.0 19.5 %all-to-all-start.1 = ((bf16[8,128,512]{2,1,0:T(8,128)(2,1)}), bf16[8,128,512]{2,1,0:T(8,128)(2,1)S(1)}, u32[]{:S(2)}, u32[]{:S(2)}) async-start(bf16[8,128,512]{2,1,0:T(8,128)(2,1)} %get-tuple-element.62), calls=%async_computation.1 | async-start | bytes 2097152 | tf_op jit(solution)/shard_map/all_to_all | solution.py:205
  46.5 58.3 %all-gather.5.cloned.1.call-start = ((), (), s32[]{:S(2)}) async-start(), calls=%async_computation.5 | async-start | bytes 4718592 | tf_op jit(solution)/shard_map/all_gather | solution.py:251
  62.4 3.5 %copy-start.2 = (bf16[8,128,512]{2,1,0:T(8,128)(2,1)}, bf16[8,128,512]{2,1,0:T(8,128)(2,1)S(1)}, u32[]{:S(2)}) copy-start(bf16[8,128,512]{2,1,0:T(8,128)(2,1)S(1)} %all-to-all-done.1) | copy-start | bytes 3145732
  62.5 3.4 %copy-start.4 = (bf16[1024,512]{1,0:T(8,128)(2,1)}, bf16[1024,512]{1,0:T(8,128)(2,1)S(1)}, u32[]{:S(2)}) copy-start(bf16[1024,512]{1,0:T(8,128)(2,1)S(1)} %collective-permute-done.3.refs_1_) | copy-start | bytes 3145732
  66.0 82.6 %all-gather.7.cloned.1.call-start = ((), (), s32[]{:S(2)}) async-start(), calls=%async_computation.6 | async-start | bytes 4718592 | tf_op jit(solution)/shard_map/all_gather | solution.py:259
  66.0 37.3 %collective-permute-start.5 = (bf16[1536,512]{1,0:T(8,128)(2,1)}, bf16[1536,512]{1,0:T(8,128)(2,1)S(1)}, u32[]{:S(2)}, u32[]{:S(2)}) collective-permute-start(bf16[1536,512]{1,0:T(8,128)(2,1)} %get-tuple-element.72), channel_id=1, source_target_pairs={{0,8},{8,16},{16,24},{24,0},{1,9},{9,17},{17,25},{25,1},{2,10},{10... | collective-permute-start | bytes 4718600 | tf_op jit(solution)/shard_map/ppermute | solution.py:199
  66.1 37.2 %collective-permute-start.6 = (bf16[1536,512]{1,0:T(8,128)(2,1)}, bf16[1536,512]{1,0:T(8,128)(2,1)S(1)}, u32[]{:S(2)}, u32[]{:S(2)}) collective-permute-start(bf16[1536,512]{1,0:T(8,128)(2,1)} %get-tuple-element.73), channel_id=1, source_target_pairs={{0,24},{8,0},{16,8},{24,16},{1,25},{9,1},{17,9},{25,17},{2,26},{10... | collective-permute-start | bytes 4718600 | tf_op jit(solution)/shard_map/ppermute | solution.py:199
  103.3 9.7 %copy-start = (bf16[1536,512]{1,0:T(8,128)(2,1)}, bf16[1536,512]{1,0:T(8,128)(2,1)S(1)}, u32[]{:S(2)}) copy-start(bf16[1536,512]{1,0:T(8,128)(2,1)S(1)} %collective-permute-done.5.refs_3_.refs_1_) | copy-start | bytes 4718596
  103.3 9.7 %copy-start.1 = (bf16[1536,512]{1,0:T(8,128)(2,1)}, bf16[1536,512]{1,0:T(8,128)(2,1)S(1)}, u32[]{:S(2)}) copy-start(bf16[1536,512]{1,0:T(8,128)(2,1)S(1)} %collective-permute-done.6.refs_4_.refs_2_) | copy-start | bytes 4718596
  106.5 42.0 %collective-permute-start.7 = (bf16[1024,384]{1,0:T(8,128)(2,1)}, bf16[1024,384]{1,0:T(8,128)(2,1)}, u32[]{:S(2)}, u32[]{:S(2)}) collective-permute-start(bf16[1024,384]{1,0:T(8,128)(2,1)} %bitcast.53), channel_id=1, source_target_pairs={{0,8},{8,16},{16,24},{24,0},{1,9},{9,17},{17,25},{25,1},{2,10},{10... | collective-permute-start | bytes 2359304 | tf_op jit(solution)/shard_map/ppermute | solution.py:199
  106.6 41.9 %collective-permute-start.8 = (bf16[1024,384]{1,0:T(8,128)(2,1)}, bf16[1024,384]{1,0:T(8,128)(2,1)}, u32[]{:S(2)}, u32[]{:S(2)}) collective-permute-start(bf16[1024,384]{1,0:T(8,128)(2,1)} %bitcast.54), channel_id=1, source_target_pairs={{0,24},{8,0},{16,8},{24,16},{1,25},{9,1},{17,9},{25,17},{2,26},{10... | collective-permute-start | bytes 2359304 | tf_op jit(solution)/shard_map/ppermute | solution.py:199
  109.8 29.1 %collective-permute-start.9 = (bf16[512,512]{1,0:T(8,128)(2,1)}, bf16[512,512]{1,0:T(8,128)(2,1)S(1)}, u32[]{:S(2)}, u32[]{:S(2)}) collective-permute-start(bf16[512,512]{1,0:T(8,128)(2,1)} %slice.58), channel_id=1, source_target_pairs={{0,8},{8,16},{16,24},{24,0},{1,9},{9,17},{17,25},{25,1},{2,10},{10... | collective-permute-start | bytes 1572872 | tf_op jit(solution)/shard_map/ppermute | solution.py:199
  109.8 29.1 %collective-permute-start.10 = (bf16[512,512]{1,0:T(8,128)(2,1)}, bf16[512,512]{1,0:T(8,128)(2,1)S(1)}, u32[]{:S(2)}, u32[]{:S(2)}) collective-permute-start(bf16[512,512]{1,0:T(8,128)(2,1)} %slice.59), channel_id=1, source_target_pairs={{0,24},{8,0},{16,8},{24,16},{1,25},{9,1},{17,9},{25,17},{2,26},{10... | collective-permute-start | bytes 1572872 | tf_op jit(solution)/shard_map/ppermute | solution.py:199
  121.0 39.2 %collective-permute-start.14 = (f16[528,512]{1,0:T(8,128)(2,1)S(1)}, f16[528,512]{1,0:T(8,128)(2,1)S(1)}, u32[]{:S(2)}, u32[]{:S(2)}) collective-permute-start(f16[528,512]{1,0:T(8,128)(2,1)S(1)} %convert_element_type.21), channel_id=1, source_target_pairs={{0,32},{32,0},{1,33},{33,1},{2,34},{34,2},{3,35},{35,3},{4,36},{36... | collective-permute-start | bytes 1622024 | tf_op jit(solution)/shard_map/ppermute | solution.py:199
  138.9 0.8 copy-start.6
  139.7 0.8 copy-start.7
  150.6 30.0 %collective-permute-start.11 = (f16[528,512]{1,0:T(8,128)(2,1)S(1)}, f16[528,512]{1,0:T(8,128)(2,1)S(1)}, u32[]{:S(2)}, u32[]{:S(2)}) collective-permute-start(f16[528,512]{1,0:T(8,128)(2,1)S(1)} %convert_element_type.22), channel_id=1, source_target_pairs={{0,32},{32,0},{1,33},{33,1},{2,34},{34,2},{3,35},{35,3},{4,36},{36... | collective-permute-start | bytes 1622024 | tf_op jit(solution)/shard_map/ppermute | solution.py:199
  157.0 11.7 %collective-permute-start.12 = (bf16[512,384]{1,0:T(8,128)(2,1)S(1)}, bf16[512,384]{1,0:T(8,128)(2,1)S(1)}, u32[]{:S(2)}, u32[]{:S(2)}) collective-permute-start(bf16[512,384]{1,0:T(8,128)(2,1)S(1)} %slice.60), channel_id=1, source_target_pairs={{0,8},{8,16},{16,24},{24,0},{1,9},{9,17},{17,25},{25,1},{2,10},{10... | collective-permute-start | bytes 1179656 | tf_op jit(solution)/shard_map/ppermute | solution.py:199
  157.0 11.7 %collective-permute-start.13 = (bf16[512,384]{1,0:T(8,128)(2,1)S(1)}, bf16[512,384]{1,0:T(8,128)(2,1)S(1)}, u32[]{:S(2)}, u32[]{:S(2)}) collective-permute-start(bf16[512,384]{1,0:T(8,128)(2,1)S(1)} %slice.61), channel_id=1, source_target_pairs={{0,24},{8,0},{16,8},{24,16},{1,25},{9,1},{17,9},{25,17},{2,26},{10... | collective-permute-start | bytes 1179656 | tf_op jit(solution)/shard_map/ppermute | solution.py:199
  168.7 0.7 copy-start.8
  169.5 0.8 copy-start.9
  180.6 25.8 %all-to-all-start.3 = ((f32[8,64,512]{2,1,0:T(8,128)}), f32[8,64,512]{2,1,0:T(8,128)S(1)}, u32[]{:S(2)}, u32[]{:S(2)}) async-start(f32[8,64,512]{2,1,0:T(8,128)} %bitcast.25), calls=%async_computation.3 | async-start | bytes 2097152 | tf_op jit(solution)/shard_map/all_to_all | solution.py:205
  184.2 22.2 %collective-permute-start.15 = (f16[528,384]{1,0:T(8,128)(2,1)S(1)}, f16[528,384]{1,0:T(8,128)(2,1)S(1)}, u32[]{:S(2)}, u32[]{:S(2)}) collective-permute-start(f16[528,384]{1,0:T(8,128)(2,1)S(1)} %convert_element_type.23), channel_id=1, source_target_pairs={{0,32},{32,0},{1,33},{33,1},{2,34},{34,2},{3,35},{35,3},{4,36},{36... | collective-permute-start | bytes 1216520 | tf_op jit(solution)/shard_map/ppermute | solution.py:199
  206.4 4.6 %copy-start.5 = (f32[8,64,512]{2,1,0:T(8,128)}, f32[8,64,512]{2,1,0:T(8,128)S(1)}, u32[]{:S(2)}) copy-start(f32[8,64,512]{2,1,0:T(8,128)S(1)} %all-to-all-done.3.refs_0_) | copy-start | bytes 3145732
  246.6 5.5 %collective-permute-start.16 = (f32[88,128]{1,0:T(8,128)}, f32[88,128]{1,0:T(8,128)S(1)}, u32[]{:S(2)}, u32[]{:S(2)}) collective-permute-start(f32[88,128]{1,0:T(8,128)} %get-tuple-element.110.b0), channel_id=1, source_target_pairs={{0,64},{64,128},{128,192},{192,0},{1,65},{65,129},{129,193},{193,1... | collective-permute-start | bytes 135176 | tf_op jit(solution)/shard_map/band/ppermute | solution.py:199
  250.1 5.2 %collective-permute-start.17 = (f32[88,128]{1,0:T(8,128)}, f32[88,128]{1,0:T(8,128)S(1)}, u32[]{:S(2)}, u32[]{:S(2)}) collective-permute-start(f32[88,128]{1,0:T(8,128)} %get-tuple-element.110.b0), channel_id=1, source_target_pairs={{0,128},{64,192},{128,0},{192,64},{1,129},{65,193},{129,1},{193,65... | collective-permute-start | bytes 135176 | tf_op jit(solution)/shard_map/band/ppermute | solution.py:199
  250.1 5.2 %collective-permute-start.18 = (f32[88,128]{1,0:T(8,128)}, f32[88,128]{1,0:T(8,128)S(1)}, u32[]{:S(2)}, u32[]{:S(2)}) collective-permute-start(f32[88,128]{1,0:T(8,128)} %get-tuple-element.110.b0), channel_id=1, source_target_pairs={{0,192},{64,0},{128,64},{192,128},{1,193},{65,1},{129,65},{193,129... | collective-permute-start | bytes 135176 | tf_op jit(solution)/shard_map/band/ppermute | solution.py:199
  252.1 3.1 %copy-start.11 = (f32[88,128]{1,0:T(8,128)}, f32[88,128]{1,0:T(8,128)S(1)}, u32[]{:S(2)}) copy-start(f32[88,128]{1,0:T(8,128)S(1)} %collective-permute-done.16.b1) | copy-start | bytes 135172
  255.2 0.6 copy-start.12
  255.9 0.6 copy-start.13
Sparse Core Ops, SparseCore 0:
  66.1 38.6 all-gather.4
  106.7 33.9 all-gather.6

commit v5 on v4

--- a/solution.py
+++ b/solution.py
@@ -254,11 +254,11 @@
     half1 = halves(r1, l1)
     half1, r1, l1, v2, sent, kept = sync(half1, r1, l1, v2, sent, kept)
     far1 = along("x", 1, half1[0]), along("x", 3, half1[1])
-    r2, l2 = ring(v2)
     send0 = payload(sent, [v0, r0, l0, r1, l1])
     kept = lax.all_gather(kept, ("y", "core"))
 
-    send0, sent = sync(send0, sent)
+    far1, send0, v2, sent = sync(far1, send0, v2, sent)
+    r2, l2 = ring(v2)
     got0 = along("zh", 1, send0)
     send1 = payload(sent, [v1, r1, l1, *far1])
 

time: 268 us -> 266 us (level)
  local copies, waits for them, and re-layouts: 11 us -> 7.26 us
  transfers between devices with their start and end apart: 24 -> 24, of which waited for: 12 -> 14; matrix products, arithmetic and copies ran while one was open for 5% -> 5% of each run, Pallas kernels for 16% -> 16%
where the time goes in v5:
time: 266 us; the launch traced here: 265 us
  waiting for transfers between devices  63 us (24%)
  Pallas kernels  59.2 us (22%)
  starting transfers between devices  55.4 us (21%)
  blocking collectives  50.8 us (19%)
  other arithmetic  14.6 us (5%)
  between operations  14.3 us (5%)
  local copies, waits for them, and re-layouts  7.26 us (3%)
    all_to_all x2, blocking collectives, swap(): return lax.all_to_all(value, ('y', 'core'), 0, 0, tiled=True)  50.8 us
    ppermute x19, waiting for transfers between devices, along(): lax.ppermute(value, axis, shift(2 if axis in ('core', 'zh') else 4, by))  43.8 us
    ppermute x19, starting transfers between devices, along(): lax.ppermute(value, axis, shift(2 if axis in ('core', 'zh') else 4, by))  43.5 us
    pallas_call x6, Pallas kernels, tile(): pl.pallas_call(kernel, grid=(half // rows,), out_shape=jax.ShapeDtypeStru...  37.6 us
    all_to_all x3, waiting for transfers between devices, swap(): return lax.all_to_all(value, ('y', 'core'), 0, 0, tiled=True)  17.7 us
    pallas_call x5, Pallas kernels, call(): pl.pallas_call(kernel, out_shape=shapes, in_specs=spec or [VMEM] * len(ar...  15.3 us
    all_to_all x3, starting transfers between devices, swap(): return lax.all_to_all(value, ('y', 'core'), 0, 0, tiled=True)  11.7 us
    pallas_call x1, Pallas kernels, on_device(): pl.pallas_call(functools.partial(finish_kernel, [d.shape[2] for d in done...  6.38 us
  transfers between devices with their start and end apart: 24, of which 14 were waited for; matrix products, arithmetic and copies ran while one was open for 5% of the time, Pallas kernels for 16%

profile of v5, /device:TPU:32, one launch (start us, length us, event | category | flops | bytes accessed | tf_op | source)
XLA Modules:
  0.0 264.5 jit_solution(3807515034454100530)
XLA Ops:
  7.2 0.7 stack.65.at_ref
  7.9 2.3 shard_map.105
  10.2 3.0 %collective-permute-start.2 = (bf16[1024,128]{1,0:T(8,128)(2,1)}, bf16[1024,128]{1,0:T(8,128)(2,1)S(1)}, u32[]{:S(2)}, u32[]{:S(2)}) collective-permute-start(bf16[1024,128]{1,0:T(8,128)(2,1)} %get-tuple-element.63), channel_id=1, source_target_pairs={{0,16},{8,24},{16,0},{24,8},{1,17},{9,25},{17,1},{25,9},{2,18},{10... | collective-permute-start | bytes 786440 | tf_op jit(solution)/shard_map/ppermute | solution.py:199
  13.2 2.8 %shard_map.104 = bf16[8,128,512]{2,1,0:T(8,128)(2,1)} custom-call(bf16[128,11008]{1,0:T(8,128)(2,1)} %bitcast.46), custom_call_target="tpu_custom_call" | custom-call | flops 1 | bytes 1 | tf_op jit(solution)/shard_map/pallas_call | solution.py:85
  16.1 4.6 %all-to-all-start = ((bf16[8,128,512]{2,1,0:T(8,128)(2,1)}), bf16[8,128,512]{2,1,0:T(8,128)(2,1)S(1)}, u32[]{:S(2)}, u32[]{:S(2)}) async-start(bf16[8,128,512]{2,1,0:T(8,128)(2,1)} %shard_map.104), calls=%async_computation | async-start | bytes 2097152 | tf_op jit(solution)/shard_map/all_to_all | solution.py:205
  20.7 1.2 collective-permute-start.1
  21.9 0.9 collective-permute-start
  22.8 6.6 %collective-permute-done.1 = bf16[1024,128]{1,0:T(8,128)(2,1)S(1)} collective-permute-done((bf16[1024,128]{1,0:T(8,128)(2,1)S(1)}, bf16[1024,128]{1,0:T(8,128)(2,1)S(1)}, u32[]{:S(2)}, u32[]{:S(2)}) %collective-permute-start.1) | collective-permute-done | bytes 262176 | tf_op jit(solution)/shard_map/ppermute | solution.py:199
  29.4 2.1 collective-permute-done
  31.5 0.7 slice_bitcast_fusion.2
  32.2 0.8 pad_maximum_fusion.2
  33.0 3.6 %all-to-all-done = bf16[8,128,512]{2,1,0:T(8,128)(2,1)S(1)} async-done(((bf16[8,128,512]{2,1,0:T(8,128)(2,1)}), bf16[8,128,512]{2,1,0:T(8,128)(2,1)S(1)}, u32[]{:S(2)}, u32[]{:S(2)}) %all-to-all-start) | async-done | bytes 1048608 | tf_op jit(solution)/shard_map/all_to_all | solution.py:205
  36.6 0.6 collective-permute-start.3
  37.2 2.6 collective-permute-start.4
  39.9 3.1 %shard_map.106 = (bf16[8,128,512]{2,1,0:T(8,128)(2,1)}, bf16[8,128,384]{2,1,0:T(8,128)(2,1)}) custom-call(bf16[128,11008]{1,0:T(8,128)(2,1)} %bitcast.47), custom_call_target="tpu_custom_call" | custom-call | flops 1 | bytes 1 | tf_op jit(solution)/shard_map/pallas_call | solution.py:85
  43.0 3.6 %all-to-all-start.1 = ((bf16[8,128,512]{2,1,0:T(8,128)(2,1)}), bf16[8,128,512]{2,1,0:T(8,128)(2,1)S(1)}, u32[]{:S(2)}, u32[]{:S(2)}) async-start(bf16[8,128,512]{2,1,0:T(8,128)(2,1)} %get-tuple-element.65), calls=%async_computation.1 | async-start | bytes 2097152 | tf_op jit(solution)/shard_map/all_to_all | solution.py:205
  46.6 1.8 pad_maximum_fusion.3
  48.4 14.1 %all-to-all-done.1 = bf16[8,128,512]{2,1,0:T(8,128)(2,1)S(1)} async-done(((bf16[8,128,512]{2,1,0:T(8,128)(2,1)}), bf16[8,128,512]{2,1,0:T(8,128)(2,1)S(1)}, u32[]{:S(2)}, u32[]{:S(2)}) %all-to-all-start.1) | async-done | bytes 1048608 | tf_op jit(solution)/shard_map/all_to_all | solution.py:205
  62.6 1.5 slice.57
  64.1 1.9 pad_maximum_fusion
  66.1 3.2 %collective-permute-start.6 = (bf16[1536,512]{1,0:T(8,128)(2,1)}, bf16[1536,512]{1,0:T(8,128)(2,1)S(1)}, u32[]{:S(2)}, u32[]{:S(2)}) collective-permute-start(bf16[1536,512]{1,0:T(8,128)(2,1)} %get-tuple-element.76), channel_id=1, source_target_pairs={{0,24},{8,0},{16,8},{24,16},{1,25},{9,1},{17,9},{25,17},{2,26},{10... | collective-permute-start | bytes 4718600 | tf_op jit(solution)/shard_map/ppermute | solution.py:199
  69.4 21.6 %all_to_all.25 = bf16[8,128,384]{2,1,0:T(8,128)(2,1)} all-to-all(bf16[8,128,384]{2,1,0:T(8,128)(2,1)} %get-tuple-element.77), channel_id=1, replica_groups=mesh['rep'=4,'zh'=2,'x'=4,'y'=4,'core'=2] {'y','core'}, dimensions={0} | all-to-all | bytes 1572864 | tf_op jit(solution)/shard_map/all_to_all | solution.py:205
  91.0 12.4 %collective-permute-done.5.refs_3_.refs_1_ = bf16[1536,512]{1,0:T(8,128)(2,1)S(1)} collective-permute-done((bf16[1536,512]{1,0:T(8,128)(2,1)}, bf16[1536,512]{1,0:T(8,128)(2,1)S(1)}, u32[]{:S(2)}, u32[]{:S(2)}) %collective-permute-start.5) | collective-permute-done | bytes 1572896 | tf_op jit(solution)/shard_map/ppermute | solution.py:199
  103.4 1.5 all-gather.5.cloned.1.call-done
  104.8 0.8 slice.58
  105.7 0.8 slice.59
  106.6 3.2 %collective-permute-start.8 = (bf16[512,512]{1,0:T(8,128)(2,1)}, bf16[512,512]{1,0:T(8,128)(2,1)S(1)}, u32[]{:S(2)}, u32[]{:S(2)}) collective-permute-start(bf16[512,512]{1,0:T(8,128)(2,1)} %slice.59), channel_id=1, source_target_pairs={{0,24},{8,0},{16,8},{24,16},{1,25},{9,1},{17,9},{25,17},{2,26},{10... | collective-permute-start | bytes 1572872 | tf_op jit(solution)/shard_map/ppermute | solution.py:199
  109.8 6.6 %shard_map.107 = f32[528,512]{1,0:T(8,128)} custom-call(bf16[8,4,512,128]{3,2,1,0:T(8,128)(2,1)} %bitcast.37, bf16[1024,512]{1,0:T(8,128)(2,1)} %bitcast.50, bf16[1024,512]{1,0:T(8,128)(2,1)} %copy-done.5, bf16[1024,512]{1,0:T(8,128)(2,1)} %collective-permute-done.4.refs_2_, bf16[1536,512]{1,0:T(8,128)(2,1)} %copy-done, bf16[1536,512]{1,0:T(8,128)(2,1)} %copy-done.1), custom_call_target="tpu_custom_call" | custom-call | flops 1 | bytes 1 | tf_op jit(solution)/shard_map/pallas_call | solution.py:165
  116.5 2.2 convert_element_type.21
  118.7 3.4 %collective-permute-done.7.refs_3_ = bf16[512,512]{1,0:T(8,128)(2,1)S(1)} collective-permute-done((bf16[512,512]{1,0:T(8,128)(2,1)}, bf16[512,512]{1,0:T(8,128)(2,1)S(1)}, u32[]{:S(2)}, u32[]{:S(2)}) %collective-permute-start.7) | collective-permute-done | bytes 524320 | tf_op jit(solution)/shard_map/ppermute | solution.py:199
  122.2 3.2 %collective-permute-start.10 = (bf16[1024,384]{1,0:T(8,128)(2,1)S(1)}, bf16[1024,384]{1,0:T(8,128)(2,1)S(1)}, u32[]{:S(2)}, u32[]{:S(2)}) collective-permute-start(bf16[1024,384]{1,0:T(8,128)(2,1)S(1)} %bitcast.56), channel_id=1, source_target_pairs={{0,24},{8,0},{16,8},{24,16},{1,25},{9,1},{17,9},{25,17},{2,26},{10... | collective-permute-start | bytes 2359304 | tf_op jit(solution)/shard_map/ppermute | solution.py:199
  125.4 6.3 %collective-permute-start.14 = (f16[528,512]{1,0:T(8,128)(2,1)}, f16[528,512]{1,0:T(8,128)(2,1)}, u32[]{:S(2)}, u32[]{:S(2)}) collective-permute-start(f16[528,512]{1,0:T(8,128)(2,1)} %convert_element_type.21), channel_id=1, source_target_pairs={{0,32},{32,0},{1,33},{33,1},{2,34},{34,2},{3,35},{35,3},{4,36},{36... | collective-permute-start | bytes 1622024 | tf_op jit(solution)/shard_map/ppermute | solution.py:199
  131.7 6.8 %shard_map.108 = f32[528,512]{1,0:T(8,128)} custom-call(bf16[8,4,512,128]{3,2,1,0:T(8,128)(2,1)} %bitcast.38, bf16[1024,512]{1,0:T(8,128)(2,1)} %bitcast.44, bf16[1536,512]{1,0:T(8,128)(2,1)} %copy-done, bf16[1536,512]{1,0:T(8,128)(2,1)} %copy-done.1, bf16[512,512]{1,0:T(8,128)(2,1)} %copy-done.9, bf16[512,512]{1,0:T(8,128)(2,1)} %copy-done.10), custom_call_target="tpu_custom_call" | custom-call | flops 1 | bytes 1 | tf_op jit(solution)/shard_map/pallas_call | solution.py:165
  138.5 1.3 convert_element_type.22
  139.8 2.5 collective-permute-done.9.refs_1_
  142.4 6.5 %collective-permute-start.11 = (f16[528,512]{1,0:T(8,128)(2,1)S(1)}, f16[528,512]{1,0:T(8,128)(2,1)S(1)}, u32[]{:S(2)}, u32[]{:S(2)}) collective-permute-start(f16[528,512]{1,0:T(8,128)(2,1)S(1)} %convert_element_type.22), channel_id=1, source_target_pairs={{0,32},{32,0},{1,33},{33,1},{2,34},{34,2},{3,35},{35,3},{4,36},{36... | collective-permute-start | bytes 1622024 | tf_op jit(solution)/shard_map/ppermute | solution.py:199
  148.9 0.7 collective-permute-start.12
  149.6 2.5 collective-permute-start.13
  152.1 12.2 %collective-permute-done.14 = f16[528,512]{1,0:T(8,128)(2,1)} collective-permute-done((f16[528,512]{1,0:T(8,128)(2,1)}, f16[528,512]{1,0:T(8,128)(2,1)}, u32[]{:S(2)}, u32[]{:S(2)}) %collective-permute-start.14) | collective-permute-done | bytes 540704 | tf_op jit(solution)/shard_map/ppermute | solution.py:199
  164.3 0.7 multiply_exponential_fusion
  165.0 6.1 %shard_map.110 = f32[512,512]{1,0:T(8,128)} custom-call(bf16[8,4,512,128]{3,2,1,0:T(8,128)(2,1)} %bitcast.40, bf16[1024,512]{1,0:T(8,128)(2,1)} %bitcast.51, bf16[1024,512]{1,0:T(8,128)(2,1)} %copy-done.5, bf16[1024,512]{1,0:T(8,128)(2,1)} %collective-permute-done.4.refs_2_, bf16[1536,512]{1,0:T(8,128)(2,1)} %copy-done, bf16[1536,512]{1,0:T(8,128)(2,1)} %copy-done.1), custom_call_target="tpu_custom_call" | custom-call | flops 1 | bytes 1 | tf_op jit(solution)/shard_map/pallas_call | solution.py:165
  171.2 2.5 multiply_add_fusion
  173.7 0.7 copy-done.11
  174.4 0.7 copy-done.12
  175.2 6.2 %shard_map.109 = f32[528,384]{1,0:T(8,128)} custom-call(bf16[8,4,512,128]{3,2,1,0:T(8,128)(2,1)} %bitcast.39, bf16[1024,384]{1,0:T(8,128)(2,1)} %bitcast.53, bf16[1024,384]{1,0:T(8,128)(2,1)} %copy-done.6, bf16[1024,384]{1,0:T(8,128)(2,1)} %copy-done.7, bf16[512,384]{1,0:T(8,128)(2,1)} %copy-done.11, bf16[512,384]{1,0:T(8,128)(2,1)} %copy-done.12), custom_call_target="tpu_custom_call" | custom-call | flops 1 | bytes 1 | tf_op jit(solution)/shard_map/pallas_call | solution.py:165
  181.4 1.2 convert_element_type.23
  182.6 3.6 %all-to-all-start.3 = ((f32[8,64,512]{2,1,0:T(8,128)}), f32[8,64,512]{2,1,0:T(8,128)S(1)}, u32[]{:S(2)}, u32[]{:S(2)}) async-start(f32[8,64,512]{2,1,0:T(8,128)} %bitcast.25), calls=%async_computation.3 | async-start | bytes 2097152 | tf_op jit(solution)/shard_map/all_to_all | solution.py:205
  186.2 5.9 %collective-permute-start.15 = (f16[528,384]{1,0:T(8,128)(2,1)S(1)}, f16[528,384]{1,0:T(8,128)(2,1)S(1)}, u32[]{:S(2)}, u32[]{:S(2)}) collective-permute-start(f16[528,384]{1,0:T(8,128)(2,1)S(1)} %convert_element_type.23), channel_id=1, source_target_pairs={{0,32},{32,0},{1,33},{33,1},{2,34},{34,2},{3,35},{35,3},{4,36},{36... | collective-permute-start | bytes 1216520 | tf_op jit(solution)/shard_map/ppermute | solution.py:199
  192.1 6.1 %shard_map.111.refs_0_ = f32[512,512]{1,0:T(8,128)} custom-call(bf16[8,4,512,128]{3,2,1,0:T(8,128)(2,1)} %bitcast.41, bf16[1024,512]{1,0:T(8,128)(2,1)} %bitcast.45, bf16[1536,512]{1,0:T(8,128)(2,1)} %copy-done, bf16[1536,512]{1,0:T(8,128)(2,1)} %copy-done.1, bf16[512,512]{1,0:T(8,128)(2,1)} %copy-done.9, bf16[512,512]{1,0:T(8,128)(2,1)} %copy-done.10), custom_call_target="tpu_custom_call" | custom-call | flops 1 | bytes 1 | tf_op jit(solution)/shard_map/pallas_call | solution.py:165
  198.1 5.7 %shard_map.112.refs_2_ = f32[512,384]{1,0:T(8,128)} custom-call(bf16[8,4,512,128]{3,2,1,0:T(8,128)(2,1)} %bitcast.42, bf16[1024,384]{1,0:T(8,128)(2,1)} %bitcast.54, bf16[1024,384]{1,0:T(8,128)(2,1)} %copy-done.6, bf16[1024,384]{1,0:T(8,128)(2,1)} %copy-done.7, bf16[512,384]{1,0:T(8,128)(2,1)} %copy-done.11, bf16[512,384]{1,0:T(8,128)(2,1)} %copy-done.12), custom_call_target="tpu_custom_call" | custom-call | flops 1 | bytes 1 | tf_op jit(solution)/shard_map/pallas_call | solution.py:165
  203.9 1.1 convert_element_type.26.refs_1_
  205.0 0.7 collective-permute-done.15
  205.7 1.0 convert_element_type.27.refs_3_
  206.7 3.6 %shard_map.113 = f32[512,896]{1,0:T(8,128)} custom-call(f32[512,512]{1,0:T(8,128)} %shard_map.111.refs_0_, f32[528,512]{1,0:T(8,128)} %convert_element_type.26.refs_1_, f32[512,384]{1,0:T(8,128)} %shard_map.112.refs_2_, f32[528,384]{1,0:T(8,128)} %convert_element_type.27.refs_3_), custom_call_target="tpu_custom_call" | custom-call | flops 1 | bytes 1 | tf_op jit(solution)/shard_map/pallas_call | solution.py:85
  210.3 29.2 %all_to_all.26.refs_1_ = f32[8,64,896]{2,1,0:T(8,128)} all-to-all(f32[8,64,896]{2,1,0:T(8,128)} %bitcast.52), channel_id=1, replica_groups=mesh['rep'=4,'zh'=2,'x'=4,'y'=4,'core'=2] {'y','core'}, dimensions={0} | all-to-all | bytes 3670016 | tf_op jit(solution)/shard_map/all_to_all | solution.py:205
  239.5 6.4 %finish.1 = (f32[64,11008]{1,0:T(8,128)}, f32[88,128]{1,0:T(8,128)}) custom-call(f32[8,64]{1,0:T(8,128)} %constant.63.clone.basis_ref, f32[64,8]{1,0:T(8,128)} %constant.64.clone.back_ref, f32[1024,128]{1,0:T(8,128)} %constant.65.clone.wide_ref, f32[128,1024]{1,0:T(8,128)} %constant.66.clone.tall_ref, f32[64,11008]{1,0:T(8,128)} %bitcast.58, ...), custom_call_target="tpu_custom_call" | custom-call | tf_op jit(solution)/shard_map/finish/pallas_call | solution.py:290
  245.9 1.9 collective-permute-start.16
  247.8 0.7 collective-permute-start.17
  248.5 0.8 collective-permute-start.18
  249.3 1.2 collective-permute-done.16.b1
  250.5 2.6 collective-permute-done.17.b2
  253.2 0.5 copy-done.15
  253.7 0.6 copy-done.16
  254.3 3.4 %update.1 = f32[64,11008]{1,0:T(8,128)} custom-call(f32[64,8]{1,0:T(8,128)} %constant.64.clone.back_ref, f32[128,1024]{1,0:T(8,128)} %constant.66.clone.tall_ref, f32[88,128]{1,0:T(8,128)} %get-tuple-element.116.b0, f32[88,128]{1,0:T(8,128)} %copy-done.14, f32[88,128]{1,0:T(8,128)} %copy-done.15, f32[88,128]{1,0:T(8,128)} %copy-done.16), custom_call_target="tpu_custom_call" | custom-call | flops 1 | bytes 1 | tf_op jit(solution)/shard_map/update/pallas_call | solution.py:85
  (59 shorter events, 0.9 us)
Async XLA Ops:
  10.2 12.6 %collective-permute-start.2 = (bf16[1024,128]{1,0:T(8,128)(2,1)}, bf16[1024,128]{1,0:T(8,128)(2,1)S(1)}, u32[]{:S(2)}, u32[]{:S(2)}) collective-permute-start(bf16[1024,128]{1,0:T(8,128)(2,1)} %get-tuple-element.63), channel_id=1, source_target_pairs={{0,16},{8,24},{16,0},{24,8},{1,17},{9,25},{17,1},{25,9},{2,18},{10... | collective-permute-start | bytes 786440 | tf_op jit(solution)/shard_map/ppermute | solution.py:199
  16.1 4.6 %copy-start.18 = (bf16[1024,128]{1,0:T(8,128)(2,1)S(1)}, bf16[1024,128]{1,0:T(8,128)(2,1)}, u32[]{:S(2)}) copy-start(bf16[1024,128]{1,0:T(8,128)(2,1)} %get-tuple-element.62) | copy-start | bytes 786436
  16.1 5.8 %copy-start.17 = (bf16[1024,128]{1,0:T(8,128)(2,1)S(1)}, bf16[1024,128]{1,0:T(8,128)(2,1)}, u32[]{:S(2)}) copy-start(bf16[1024,128]{1,0:T(8,128)(2,1)} %get-tuple-element.61) | copy-start | bytes 786436
  16.1 6.7 %copy-start.13 = (bf16[1024,128]{1,0:T(8,128)(2,1)S(1)}, bf16[1024,128]{1,0:T(8,128)(2,1)}, u32[]{:S(2)}) copy-start(bf16[1024,128]{1,0:T(8,128)(2,1)} %get-tuple-element.60) | copy-start | bytes 786436
  16.1 20.6 %all-to-all-start = ((bf16[8,128,512]{2,1,0:T(8,128)(2,1)}), bf16[8,128,512]{2,1,0:T(8,128)(2,1)S(1)}, u32[]{:S(2)}, u32[]{:S(2)}) async-start(bf16[8,128,512]{2,1,0:T(8,128)(2,1)} %shard_map.104), calls=%async_computation | async-start | bytes 2097152 | tf_op jit(solution)/shard_map/all_to_all | solution.py:205
  20.7 8.7 %collective-permute-start.1 = (bf16[1024,128]{1,0:T(8,128)(2,1)S(1)}, bf16[1024,128]{1,0:T(8,128)(2,1)S(1)}, u32[]{:S(2)}, u32[]{:S(2)}) collective-permute-start(bf16[1024,128]{1,0:T(8,128)(2,1)S(1)} %copy-done.18), channel_id=1, source_target_pairs={{0,24},{8,0},{16,8},{24,16},{1,25},{9,1},{17,9},{25,17},{2,26},{10... | collective-permute-start | bytes 786440 | tf_op jit(solution)/shard_map/ppermute | solution.py:199
  21.9 9.6 %collective-permute-start = (bf16[1024,128]{1,0:T(8,128)(2,1)S(1)}, bf16[1024,128]{1,0:T(8,128)(2,1)S(1)}, u32[]{:S(2)}, u32[]{:S(2)}) collective-permute-start(bf16[1024,128]{1,0:T(8,128)(2,1)S(1)} %copy-done.17), channel_id=1, source_target_pairs={{0,8},{8,16},{16,24},{24,0},{1,9},{9,17},{17,25},{25,1},{2,10},{10... | collective-permute-start | bytes 786440 | tf_op jit(solution)/shard_map/ppermute | solution.py:199
  36.6 6.3 %copy-start.3 = (bf16[8,128,512]{2,1,0:T(8,128)(2,1)}, bf16[8,128,512]{2,1,0:T(8,128)(2,1)S(1)}, u32[]{:S(2)}) copy-start(bf16[8,128,512]{2,1,0:T(8,128)(2,1)S(1)} %all-to-all-done) | copy-start | bytes 3145732
  36.6 25.9 %collective-permute-start.3 = (bf16[1024,512]{1,0:T(8,128)(2,1)S(1)}, bf16[1024,512]{1,0:T(8,128)(2,1)S(1)}, u32[]{:S(2)}, u32[]{:S(2)}) collective-permute-start(bf16[1024,512]{1,0:T(8,128)(2,1)S(1)} %bitcast.48), channel_id=1, source_target_pairs={{0,8},{8,16},{16,24},{24,0},{1,9},{9,17},{17,25},{25,1},{2,10},{10... | collective-permute-start | bytes 3145736 | tf_op jit(solution)/shard_map/ppermute | solution.py:199
  37.2 25.3 %collective-permute-start.4 = (bf16[1024,512]{1,0:T(8,128)(2,1)S(1)}, bf16[1024,512]{1,0:T(8,128)(2,1)}, u32[]{:S(2)}, u32[]{:S(2)}) collective-permute-start(bf16[1024,512]{1,0:T(8,128)(2,1)S(1)} %bitcast.49), channel_id=1, source_target_pairs={{0,24},{8,0},{16,8},{24,16},{1,25},{9,1},{17,9},{25,17},{2,26},{10... | collective-permute-start | bytes 3145736 | tf_op jit(solution)/shard_map/ppermute | solution.py:199
  43.0 19.5 %all-to-all-start.1 = ((bf16[8,128,512]{2,1,0:T(8,128)(2,1)}), bf16[8,128,512]{2,1,0:T(8,128)(2,1)S(1)}, u32[]{:S(2)}, u32[]{:S(2)}) async-start(bf16[8,128,512]{2,1,0:T(8,128)(2,1)} %get-tuple-element.65), calls=%async_computation.1 | async-start | bytes 2097152 | tf_op jit(solution)/shard_map/all_to_all | solution.py:205
  46.6 58.3 %all-gather.5.cloned.1.call-start = ((), (), s32[]{:S(2)}) async-start(), calls=%async_computation.5 | async-start | bytes 4718592 | tf_op jit(solution)/shard_map/all_gather | solution.py:251
  62.4 3.5 %copy-start.2 = (bf16[8,128,512]{2,1,0:T(8,128)(2,1)}, bf16[8,128,512]{2,1,0:T(8,128)(2,1)S(1)}, u32[]{:S(2)}) copy-start(bf16[8,128,512]{2,1,0:T(8,128)(2,1)S(1)} %all-to-all-done.1) | copy-start | bytes 3145732
  62.6 3.4 %copy-start.5 = (bf16[1024,512]{1,0:T(8,128)(2,1)}, bf16[1024,512]{1,0:T(8,128)(2,1)S(1)}, u32[]{:S(2)}) copy-start(bf16[1024,512]{1,0:T(8,128)(2,1)S(1)} %collective-permute-done.3.refs_1_) | copy-start | bytes 3145732
  66.0 76.3 %all-gather.7.cloned.1.call-start = ((), (), s32[]{:S(2)}) async-start(), calls=%async_computation.6 | async-start | bytes 4718592 | tf_op jit(solution)/shard_map/all_gather | solution.py:258
  66.0 37.3 %collective-permute-start.5 = (bf16[1536,512]{1,0:T(8,128)(2,1)}, bf16[1536,512]{1,0:T(8,128)(2,1)S(1)}, u32[]{:S(2)}, u32[]{:S(2)}) collective-permute-start(bf16[1536,512]{1,0:T(8,128)(2,1)} %get-tuple-element.75), channel_id=1, source_target_pairs={{0,8},{8,16},{16,24},{24,0},{1,9},{9,17},{17,25},{25,1},{2,10},{10... | collective-permute-start | bytes 4718600 | tf_op jit(solution)/shard_map/ppermute | solution.py:199
  66.1 37.2 %collective-permute-start.6 = (bf16[1536,512]{1,0:T(8,128)(2,1)}, bf16[1536,512]{1,0:T(8,128)(2,1)S(1)}, u32[]{:S(2)}, u32[]{:S(2)}) collective-permute-start(bf16[1536,512]{1,0:T(8,128)(2,1)} %get-tuple-element.76), channel_id=1, source_target_pairs={{0,24},{8,0},{16,8},{24,16},{1,25},{9,1},{17,9},{25,17},{2,26},{10... | collective-permute-start | bytes 4718600 | tf_op jit(solution)/shard_map/ppermute | solution.py:199
  103.4 6.5 %copy-start = (bf16[1536,512]{1,0:T(8,128)(2,1)}, bf16[1536,512]{1,0:T(8,128)(2,1)S(1)}, u32[]{:S(2)}) copy-start(bf16[1536,512]{1,0:T(8,128)(2,1)S(1)} %collective-permute-done.5.refs_3_.refs_1_) | copy-start | bytes 4718596
  103.4 6.5 %copy-start.1 = (bf16[1536,512]{1,0:T(8,128)(2,1)}, bf16[1536,512]{1,0:T(8,128)(2,1)S(1)}, u32[]{:S(2)}) copy-start(bf16[1536,512]{1,0:T(8,128)(2,1)S(1)} %collective-permute-done.6.refs_4_.refs_2_) | copy-start | bytes 4718596
  106.5 15.6 %copy-start.4 = (bf16[8,128,384]{2,1,0:T(8,128)(2,1)S(1)}, bf16[8,128,384]{2,1,0:T(8,128)(2,1)}, u32[]{:S(2)}) copy-start(bf16[8,128,384]{2,1,0:T(8,128)(2,1)} %all_to_all.25) | copy-start | bytes 2359300
  106.5 15.6 %collective-permute-start.7 = (bf16[512,512]{1,0:T(8,128)(2,1)}, bf16[512,512]{1,0:T(8,128)(2,1)S(1)}, u32[]{:S(2)}, u32[]{:S(2)}) collective-permute-start(bf16[512,512]{1,0:T(8,128)(2,1)} %slice.58), channel_id=1, source_target_pairs={{0,8},{8,16},{16,24},{24,0},{1,9},{9,17},{17,25},{25,1},{2,10},{10... | collective-permute-start | bytes 1572872 | tf_op jit(solution)/shard_map/ppermute | solution.py:199
  106.6 15.5 %collective-permute-start.8 = (bf16[512,512]{1,0:T(8,128)(2,1)}, bf16[512,512]{1,0:T(8,128)(2,1)S(1)}, u32[]{:S(2)}, u32[]{:S(2)}) collective-permute-start(bf16[512,512]{1,0:T(8,128)(2,1)} %slice.59), channel_id=1, source_target_pairs={{0,24},{8,0},{16,8},{24,16},{1,25},{9,1},{17,9},{25,17},{2,26},{10... | collective-permute-start | bytes 1572872 | tf_op jit(solution)/shard_map/ppermute | solution.py:199
  122.1 9.6 %copy-start.9 = (bf16[512,512]{1,0:T(8,128)(2,1)}, bf16[512,512]{1,0:T(8,128)(2,1)S(1)}, u32[]{:S(2)}) copy-start(bf16[512,512]{1,0:T(8,128)(2,1)S(1)} %collective-permute-done.7.refs_3_) | copy-start | bytes 1572868
  122.1 9.6 %copy-start.10 = (bf16[512,512]{1,0:T(8,128)(2,1)}, bf16[512,512]{1,0:T(8,128)(2,1)S(1)}, u32[]{:S(2)}) copy-start(bf16[512,512]{1,0:T(8,128)(2,1)S(1)} %collective-permute-done.8.refs_4_) | copy-start | bytes 1572868
  122.1 20.2 %collective-permute-start.9 = (bf16[1024,384]{1,0:T(8,128)(2,1)S(1)}, bf16[1024,384]{1,0:T(8,128)(2,1)S(1)}, u32[]{:S(2)}, u32[]{:S(2)}) collective-permute-start(bf16[1024,384]{1,0:T(8,128)(2,1)S(1)} %bitcast.55), channel_id=1, source_target_pairs={{0,8},{8,16},{16,24},{24,0},{1,9},{9,17},{17,25},{25,1},{2,10},{10... | collective-permute-start | bytes 2359304 | tf_op jit(solution)/shard_map/ppermute | solution.py:199
  122.2 20.1 %collective-permute-start.10 = (bf16[1024,384]{1,0:T(8,128)(2,1)S(1)}, bf16[1024,384]{1,0:T(8,128)(2,1)S(1)}, u32[]{:S(2)}, u32[]{:S(2)}) collective-permute-start(bf16[1024,384]{1,0:T(8,128)(2,1)S(1)} %bitcast.56), channel_id=1, source_target_pairs={{0,24},{8,0},{16,8},{24,16},{1,25},{9,1},{17,9},{25,17},{2,26},{10... | collective-permute-start | bytes 2359304 | tf_op jit(solution)/shard_map/ppermute | solution.py:199
  125.4 38.9 %collective-permute-start.14 = (f16[528,512]{1,0:T(8,128)(2,1)}, f16[528,512]{1,0:T(8,128)(2,1)}, u32[]{:S(2)}, u32[]{:S(2)}) collective-permute-start(f16[528,512]{1,0:T(8,128)(2,1)} %convert_element_type.21), channel_id=1, source_target_pairs={{0,32},{32,0},{1,33},{33,1},{2,34},{34,2},{3,35},{35,3},{4,36},{36... | collective-permute-start | bytes 1622024 | tf_op jit(solution)/shard_map/ppermute | solution.py:199
  142.3 28.8 %copy-start.6 = (bf16[1024,384]{1,0:T(8,128)(2,1)}, bf16[1024,384]{1,0:T(8,128)(2,1)S(1)}, u32[]{:S(2)}) copy-start(bf16[1024,384]{1,0:T(8,128)(2,1)S(1)} %collective-permute-done.9.refs_1_) | copy-start | bytes 2359300
  142.3 28.8 %copy-start.7 = (bf16[1024,384]{1,0:T(8,128)(2,1)}, bf16[1024,384]{1,0:T(8,128)(2,1)S(1)}, u32[]{:S(2)}) copy-start(bf16[1024,384]{1,0:T(8,128)(2,1)S(1)} %collective-permute-done.10.refs_2_) | copy-start | bytes 2359300
  142.4 40.1 %collective-permute-start.11 = (f16[528,512]{1,0:T(8,128)(2,1)S(1)}, f16[528,512]{1,0:T(8,128)(2,1)S(1)}, u32[]{:S(2)}, u32[]{:S(2)}) collective-permute-start(f16[528,512]{1,0:T(8,128)(2,1)S(1)} %convert_element_type.22), channel_id=1, source_target_pairs={{0,32},{32,0},{1,33},{33,1},{2,34},{34,2},{3,35},{35,3},{4,36},{36... | collective-permute-start | bytes 1622024 | tf_op jit(solution)/shard_map/ppermute | solution.py:199
  148.9 24.8 %collective-permute-start.12 = (bf16[512,384]{1,0:T(8,128)(2,1)S(1)}, bf16[512,384]{1,0:T(8,128)(2,1)S(1)}, u32[]{:S(2)}, u32[]{:S(2)}) collective-permute-start(bf16[512,384]{1,0:T(8,128)(2,1)S(1)} %slice.60), channel_id=1, source_target_pairs={{0,8},{8,16},{16,24},{24,0},{1,9},{9,17},{17,25},{25,1},{2,10},{10... | collective-permute-start | bytes 1179656 | tf_op jit(solution)/shard_map/ppermute | solution.py:199
  149.6 24.1 %collective-permute-start.13 = (bf16[512,384]{1,0:T(8,128)(2,1)S(1)}, bf16[512,384]{1,0:T(8,128)(2,1)S(1)}, u32[]{:S(2)}, u32[]{:S(2)}) collective-permute-start(bf16[512,384]{1,0:T(8,128)(2,1)S(1)} %slice.61), channel_id=1, source_target_pairs={{0,24},{8,0},{16,8},{24,16},{1,25},{9,1},{17,9},{25,17},{2,26},{10... | collective-permute-start | bytes 1179656 | tf_op jit(solution)/shard_map/ppermute | solution.py:199
  173.7 0.7 copy-start.11
  174.4 0.7 copy-start.12
  182.6 23.1 %all-to-all-start.3 = ((f32[8,64,512]{2,1,0:T(8,128)}), f32[8,64,512]{2,1,0:T(8,128)S(1)}, u32[]{:S(2)}, u32[]{:S(2)}) async-start(f32[8,64,512]{2,1,0:T(8,128)} %bitcast.25), calls=%async_computation.3 | async-start | bytes 2097152 | tf_op jit(solution)/shard_map/all_to_all | solution.py:205
  186.2 19.5 %collective-permute-start.15 = (f16[528,384]{1,0:T(8,128)(2,1)S(1)}, f16[528,384]{1,0:T(8,128)(2,1)S(1)}, u32[]{:S(2)}, u32[]{:S(2)}) collective-permute-start(f16[528,384]{1,0:T(8,128)(2,1)S(1)} %convert_element_type.23), channel_id=1, source_target_pairs={{0,32},{32,0},{1,33},{33,1},{2,34},{34,2},{3,35},{35,3},{4,36},{36... | collective-permute-start | bytes 1216520 | tf_op jit(solution)/shard_map/ppermute | solution.py:199
  205.7 4.6 %copy-start.8 = (f32[8,64,512]{2,1,0:T(8,128)}, f32[8,64,512]{2,1,0:T(8,128)S(1)}, u32[]{:S(2)}) copy-start(f32[8,64,512]{2,1,0:T(8,128)S(1)} %all-to-all-done.3.refs_0_) | copy-start | bytes 3145732
  245.9 4.6 %collective-permute-start.16 = (f32[88,128]{1,0:T(8,128)}, f32[88,128]{1,0:T(8,128)S(1)}, u32[]{:S(2)}, u32[]{:S(2)}) collective-permute-start(f32[88,128]{1,0:T(8,128)} %get-tuple-element.116.b0), channel_id=1, source_target_pairs={{0,64},{64,128},{128,192},{192,0},{1,65},{65,129},{129,193},{193,1... | collective-permute-start | bytes 135176 | tf_op jit(solution)/shard_map/band/ppermute | solution.py:199
  247.8 5.3 %collective-permute-start.17 = (f32[88,128]{1,0:T(8,128)}, f32[88,128]{1,0:T(8,128)S(1)}, u32[]{:S(2)}, u32[]{:S(2)}) collective-permute-start(f32[88,128]{1,0:T(8,128)} %get-tuple-element.116.b0), channel_id=1, source_target_pairs={{0,128},{64,192},{128,0},{192,64},{1,129},{65,193},{129,1},{193,65... | collective-permute-start | bytes 135176 | tf_op jit(solution)/shard_map/band/ppermute | solution.py:199
  248.5 4.7 %collective-permute-start.18 = (f32[88,128]{1,0:T(8,128)}, f32[88,128]{1,0:T(8,128)S(1)}, u32[]{:S(2)}, u32[]{:S(2)}) collective-permute-start(f32[88,128]{1,0:T(8,128)} %get-tuple-element.116.b0), channel_id=1, source_target_pairs={{0,192},{64,0},{128,64},{192,128},{1,193},{65,1},{129,65},{193,129... | collective-permute-start | bytes 135176 | tf_op jit(solution)/shard_map/band/ppermute | solution.py:199
  250.5 2.7 %copy-start.14 = (f32[88,128]{1,0:T(8,128)}, f32[88,128]{1,0:T(8,128)S(1)}, u32[]{:S(2)}) copy-start(f32[88,128]{1,0:T(8,128)S(1)} %collective-permute-done.16.b1) | copy-start | bytes 135172
  253.1 0.6 copy-start.15
  253.7 0.6 copy-start.16
Sparse Core Ops, SparseCore 0:
  66.1 38.6 all-gather.4
  106.7 33.9 all-gather.6
